TPU v7x, 32 devices: a whole 2x2x4 slice. The times are simulated.
32 devices in a mesh: row: 4 (over y, x), col: 2 (over core), depth: 4 (over z).
Axes of the slice: x: 2, y: 2, z: 4, core: 2. Of those that a mesh axis runs over, the one named last changes fastest.
Arguments:
- blocks: bfloat16 [64, 16, 128, 128], P(('row', 'col'), 'depth'), may hold values from -2 to 2
- block_cols: int32 [64, 16], replicated, may hold values from 0 to 63, as said below
- product_cols: int32 [64, 24], P(('row', 'col')), may hold values from 0 to 63, as said below
Outputs:
- purified: bfloat16 [64, 24, 128, 128], P(('row', 'col'), 'depth')
Inputs may be any that keep to these rules, and one draw needn't show every extreme that they name: `block_cols`: the 16 entries of a block row i are distinct, each within 8 of i counted cyclically modulo 64. `product_cols`: the 24 entries of a block row i are distinct, each within 16 of i counted cyclically modulo 64.
All inputs are finite; a program needn't handle non-finite values.
Results may differ from a plain program's by a relative error of at most 0.015.
Values may be sent and summed in bfloat16 or wider, within the bound.
No kernel may reach another device: no remote copies, remote signals or barrier semaphores. Data moves between devices by JAX's collectives and lax.ppermute only.
A program may use at most 128 MiB of HBM per device.

v0:
```python
import math

import jax
import jax.numpy as jnp
from jax import lax
from jax.sharding import PartitionSpec as P


def shifted(value, axis, steps):
    count = lax.axis_size(axis)
    pairs = [(source, (source + steps) % count) for source in range(count)]
    return lax.ppermute(value, axis, pairs)


def pick_blocks(block_cols, inner_rows, local_rows, targets, fill_count):
    cols_of = block_cols[inner_rows]
    matches = cols_of[:, :, :, None] == targets[:, None, None, :]
    has_match = jnp.any(matches, axis=2)
    slot_ids = jnp.arange(fill_count, dtype=jnp.int32)[None, None, :, None]
    position = jnp.sum(jnp.where(matches, slot_ids, 0), axis=2)
    block_index = local_rows[:, :, None] * fill_count + position
    return (block_index, has_match)


def stacked_product(left_blocks, block_index, has_match, flat_blocks, slot_groups):
    row_count = left_blocks.shape[0]
    slot_total = left_blocks.shape[1]
    edge = left_blocks.shape[2]
    group_rows = math.gcd(row_count, 2)
    groups = row_count // group_rows
    left_group = left_blocks.reshape((groups, group_rows) + left_blocks.shape[1:])
    index_group = block_index.reshape((groups, group_rows) + block_index.shape[1:])
    match_group = has_match.reshape((groups, group_rows) + has_match.shape[1:])

    def one_group(group_items):
        left_part, index_part, match_part = group_items
        picked = flat_blocks[index_part]
        picked = jnp.where(match_part[:, :, :, None, None], picked, jnp.zeros((), jnp.bfloat16))
        target_count = picked.shape[2]
        left_split = left_part.reshape(
            group_rows, slot_groups, slot_total // slot_groups, edge, edge
        )
        picked_split = picked.reshape(
            group_rows, slot_groups, slot_total // slot_groups, target_count, edge, edge
        )
        partial_value = jnp.einsum(
            "rgsab,rgstbc->rgtac", left_split, picked_split, preferred_element_type=jnp.float32
        )
        return partial_value[:, 0]

    result = lax.map(one_group, (left_group, index_group, match_group))
    return result.reshape((row_count,) + result.shape[2:])


def local(blocks, block_cols, product_cols):
    row_count = blocks.shape[0]
    slot_count = blocks.shape[1]
    block_edge = blocks.shape[2]
    fill_count = block_cols.shape[1]
    order_total = row_count * lax.axis_size(("row", "col"))
    row_place = lax.axis_index(("row", "col"))
    depth_index = lax.axis_index("depth")
    depth_count = lax.axis_size("depth")
    pieces = []
    full_rows = lax.all_gather(blocks, "depth", axis=1, tiled=True)
    for offset in (2, 1, 0, -1, -2):
        pieces.append(full_rows if offset == 0 else shifted(full_rows, ("row", "col"), offset))
    extended = jnp.concatenate(pieces, axis=0)
    flat_blocks = extended.reshape(5 * row_count * fill_count, block_edge, block_edge)
    start_row = (row_place - 2) * row_count
    own_cols = lax.dynamic_slice_in_dim(block_cols, row_place * row_count, row_count, 0)
    target_share = product_cols.shape[1] // depth_count
    inner_rows = lax.dynamic_slice_in_dim(own_cols, depth_index * slot_count, slot_count, 1)
    local_rows = (inner_rows - start_row) % order_total
    block_index, has_match = pick_blocks(
        block_cols, inner_rows, local_rows, product_cols, fill_count
    )
    partial_value = stacked_product(blocks, block_index, has_match, flat_blocks, 1)
    square = lax.psum_scatter(
        partial_value.astype(jnp.bfloat16), "depth", scatter_dimension=1, tiled=True
    )
    inner_second = lax.dynamic_slice_in_dim(
        product_cols, depth_index * target_share, target_share, 1
    )
    local_second = (inner_second - start_row) % order_total
    index_second, match_second = pick_blocks(
        block_cols, inner_second, local_second, product_cols, fill_count
    )
    partial_second = stacked_product(square, index_second, match_second, flat_blocks, 1)
    cubed = lax.psum_scatter(
        partial_second.astype(jnp.bfloat16), "depth", scatter_dimension=1, tiled=True
    ).astype(jnp.float32)
    return (3.0 * square.astype(jnp.float32) - 2.0 * cubed).astype(jnp.bfloat16)


def solution(mesh):
    placed = (P(("row", "col"), "depth", None, None), P(), P(("row", "col"), None))
    return jax.shard_map(
        local,
        mesh=mesh,
        in_specs=placed,
        out_specs=P(("row", "col"), "depth", None, None),
        check_vma=False,
    )
```

profile of v0, /device:TPU:0, one launch (start us, length us, event | category | flops | bytes accessed | tf_op | source)
XLA Modules:
  0.0 1123.0 jit_solution(3224833015253034308)
XLA Ops:
  6.5 0.7 all-gather.2.cloned.1.call-update
  7.3 85.1 %all-gather.2.cloned.1.call-done = bf16[8,16,128,128]{3,2,1,0:T(8,128)(2,1)} async-done(((bf16[8,4,128,128]{3,2,1,0:T(8,128)(2,1)}), bf16[8,16,128,128]{3,2,1,0:T(8,128)(2,1)}) %all-gather.2.cloned.1.call-update) | async-done | bytes 4194320 | tf_op jit(solution)/shard_map/all_gather | solution.py:65
  92.4 1.5 collective-permute-start
  93.9 2.6 collective-permute-start.2
  96.5 0.6 collective-permute-start.3
  97.1 0.8 copy.33
  98.0 0.8 fusion.25
  98.9 0.6 gather_fusion.2
  99.5 0.8 fusion.21
  100.3 0.8 compare_reduce_fusion.1
  101.3 85.8 %collective-permute-done = bf16[8,16,128,128]{3,2,1,0:T(8,128)(2,1)} collective-permute-done((bf16[8,16,128,128]{3,2,1,0:T(8,128)(2,1)}, bf16[8,16,128,128]{3,2,1,0:T(8,128)(2,1)}, u32[]{:S(2)}, u32[]{:S(2)}) %collective-permute-start) | collective-permute-done | bytes 4194336 | tf_op jit(solution)/shard_map/ppermute | solution.py:12
  187.1 2.5 constant_dynamic-update-slice_fusion.4
  189.6 85.1 %collective-permute-done.1 = bf16[8,16,128,128]{3,2,1,0:T(8,128)(2,1)} collective-permute-done((bf16[8,16,128,128]{3,2,1,0:T(8,128)(2,1)}, bf16[8,16,128,128]{3,2,1,0:T(8,128)(2,1)}, u32[]{:S(2)}, u32[]{:S(2)}) %collective-permute-start.1) | collective-permute-done | bytes 4194336 | tf_op jit(solution)/shard_map/ppermute | solution.py:12
  274.7 3.0 constant_dynamic-update-slice_fusion.3
  277.8 0.6 constant_dynamic-update-slice_fusion.2
  278.3 3.0 constant_dynamic-update-slice_fusion.1
  281.4 84.4 %collective-permute-done.3 = bf16[8,16,128,128]{3,2,1,0:T(8,128)(2,1)} collective-permute-done((bf16[8,16,128,128]{3,2,1,0:T(8,128)(2,1)}, bf16[8,16,128,128]{3,2,1,0:T(8,128)(2,1)}, u32[]{:S(2)}, u32[]{:S(2)}) %collective-permute-start.3) | collective-permute-done | bytes 4194336 | tf_op jit(solution)/shard_map/ppermute | solution.py:12
  365.7 3.0 constant_dynamic-update-slice_fusion
  368.8 4.6 broadcast.70.clone
  373.4 4.2 copy-done
  377.6 118.4 %while.20 = (s32[]{:T(128)}, bf16[4,2,24,128,128]{3,4,2,1,0:T(8,128)(2,1)}, pred[4,2,4,24]{3,2,1,0:T(4,128)(4,1)S(1)}, s32[4,2,4,24]{3,2,1,0:T(4,128)S(1)}, bf16...) while((s32[]{:T(128)}, bf16[4,2,24,128,128]{3,4,2,1,0:T(8,128)(2,1)}, ...), condition=%wide.region_3.4_spmd, body=%wide.region_2.3_spmd.sunk | while | flops 808453696 | bytes 34875924 | solution.py:51
  377.7 14.9 %gather_fusion = bf16[192,128,128]{2,1,0:T(8,128)(2,1)} fusion(bf16[640,128,128]{2,1,0:T(8,128)(2,1)} %get-tuple-element.217, s32[1024]{0:T(1024)S(1)} %pad_clamp_fusion.6), kind=kCustom, calls=%fused_computation.clone.1 | custom fusion | bytes 12583680 | tf_op jit(solution)/shard_map/while/body/eval_jaxpr/gather | solution.py:37
  392.7 8.6 copy.61
  401.3 0.1 copy.62
  401.4 5.8 bitcast_dynamic-update-slice_fusion.4
  407.3 14.9 %gather_fusion = bf16[192,128,128]{2,1,0:T(8,128)(2,1)} fusion(bf16[640,128,128]{2,1,0:T(8,128)(2,1)} %get-tuple-element.217, s32[1024]{0:T(1024)S(1)} %pad_clamp_fusion.6), kind=kCustom, calls=%fused_computation.clone.1 | custom fusion | bytes 12583680 | tf_op jit(solution)/shard_map/while/body/eval_jaxpr/gather | solution.py:37
  422.3 8.6 copy.61
  430.9 0.1 copy.62
  431.0 5.9 bitcast_dynamic-update-slice_fusion.4
  437.0 14.9 %gather_fusion = bf16[192,128,128]{2,1,0:T(8,128)(2,1)} fusion(bf16[640,128,128]{2,1,0:T(8,128)(2,1)} %get-tuple-element.217, s32[1024]{0:T(1024)S(1)} %pad_clamp_fusion.6), kind=kCustom, calls=%fused_computation.clone.1 | custom fusion | bytes 12583680 | tf_op jit(solution)/shard_map/while/body/eval_jaxpr/gather | solution.py:37
  451.9 8.6 copy.61
  460.5 0.1 copy.62
  460.7 5.8 bitcast_dynamic-update-slice_fusion.4
  466.6 14.9 %gather_fusion = bf16[192,128,128]{2,1,0:T(8,128)(2,1)} fusion(bf16[640,128,128]{2,1,0:T(8,128)(2,1)} %get-tuple-element.217, s32[1024]{0:T(1024)S(1)} %pad_clamp_fusion.6), kind=kCustom, calls=%fused_computation.clone.1 | custom fusion | bytes 12583680 | tf_op jit(solution)/shard_map/while/body/eval_jaxpr/gather | solution.py:37
  481.5 8.6 copy.61
  490.1 0.1 copy.62
  490.2 5.8 bitcast_dynamic-update-slice_fusion.4
  496.0 8.6 copy.35
  504.7 0.2 all-reduce.7.cloned.1.call-start
  504.9 0.6 gather_fusion.3
  505.5 0.2 fusion.20
  505.9 0.6 dynamic-slice
  507.1 0.2 compare_reduce_fusion
  507.4 218.0 %all-reduce.5.cloned.1.call-done = bf16[8,24,128,128]{3,2,1,0:T(8,128)(2,1)} async-done(((bf16[8,24,128,128]{3,2,1,0:T(8,128)(2,1)}), bf16[8,24,128,128]{3,2,1,0:T(8,128)(2,1)}) %all-reduce.5.cloned.1.call-update) | async-done | bytes 6291472
  725.4 1.5 constant_dynamic-slice_fusion.3
  726.9 4.2 broadcast.70
  731.0 150.9 %while.21 = (s32[]{:T(128)}, bf16[4,2,24,128,128]{3,4,2,1,0:T(8,128)(2,1)}, pred[4,2,6,24]{3,2,1,0:T(8,128)(4,1)S(1)}, s32[4,2,6,24]{3,1,0,2:T(2,128)S(1)}, bf16...) while((s32[]{:T(128)}, bf16[4,2,24,128,128]{3,4,2,1,0:T(8,128)(2,1)}, ...), condition=%wide.region_8.9_spmd, body=%wide.region_7.8_spmd.sunk | while | flops 1212680064 | bytes 50746580 | solution.py:51
  731.2 17.3 %gather_fusion.1 = bf16[288,128,128]{2,1,0:T(8,128)(2,1)} fusion(bf16[640,128,128]{2,1,0:T(8,128)(2,1)} %get-tuple-element.238, s32[1024]{0:T(1024)S(1)} %pad_clamp_fusion.7), kind=kCustom, calls=%fused_computation.1.clone.1 | custom fusion | bytes 18875520 | tf_op jit(solution)/shard_map/while/body/eval_jaxpr/gather | solution.py:37
  748.4 12.7 %copy.64 = bf16[2,6,24,128,128]{3,4,1,2,0:T(8,128)(2,1)} copy(bf16[2,6,24,128,128]{4,3,2,1,0:T(8,128)(2,1)} %bitcast.87) | data formatting | bytes 18874368 | tf_op jit(solution)/shard_map/while/body/eval_jaxpr/gather | solution.py:37
  761.1 0.1 copy.65
  761.3 7.5 bitcast_dynamic-update-slice_fusion.5
  768.9 17.3 %gather_fusion.1 = bf16[288,128,128]{2,1,0:T(8,128)(2,1)} fusion(bf16[640,128,128]{2,1,0:T(8,128)(2,1)} %get-tuple-element.238, s32[1024]{0:T(1024)S(1)} %pad_clamp_fusion.7), kind=kCustom, calls=%fused_computation.1.clone.1 | custom fusion | bytes 18875520 | tf_op jit(solution)/shard_map/while/body/eval_jaxpr/gather | solution.py:37
  786.2 12.7 %copy.64 = bf16[2,6,24,128,128]{3,4,1,2,0:T(8,128)(2,1)} copy(bf16[2,6,24,128,128]{4,3,2,1,0:T(8,128)(2,1)} %bitcast.87) | data formatting | bytes 18874368 | tf_op jit(solution)/shard_map/while/body/eval_jaxpr/gather | solution.py:37
  799.0 7.5 bitcast_dynamic-update-slice_fusion.5
  806.6 17.3 %gather_fusion.1 = bf16[288,128,128]{2,1,0:T(8,128)(2,1)} fusion(bf16[640,128,128]{2,1,0:T(8,128)(2,1)} %get-tuple-element.238, s32[1024]{0:T(1024)S(1)} %pad_clamp_fusion.7), kind=kCustom, calls=%fused_computation.1.clone.1 | custom fusion | bytes 18875520 | tf_op jit(solution)/shard_map/while/body/eval_jaxpr/gather | solution.py:37
  823.9 12.7 %copy.64 = bf16[2,6,24,128,128]{3,4,1,2,0:T(8,128)(2,1)} copy(bf16[2,6,24,128,128]{4,3,2,1,0:T(8,128)(2,1)} %bitcast.87) | data formatting | bytes 18874368 | tf_op jit(solution)/shard_map/while/body/eval_jaxpr/gather | solution.py:37
  836.6 0.1 copy.65
  836.7 7.6 bitcast_dynamic-update-slice_fusion.5
  844.4 17.3 %gather_fusion.1 = bf16[288,128,128]{2,1,0:T(8,128)(2,1)} fusion(bf16[640,128,128]{2,1,0:T(8,128)(2,1)} %get-tuple-element.238, s32[1024]{0:T(1024)S(1)} %pad_clamp_fusion.7), kind=kCustom, calls=%fused_computation.1.clone.1 | custom fusion | bytes 18875520 | tf_op jit(solution)/shard_map/while/body/eval_jaxpr/gather | solution.py:37
  861.6 12.7 %copy.64 = bf16[2,6,24,128,128]{3,4,1,2,0:T(8,128)(2,1)} copy(bf16[2,6,24,128,128]{4,3,2,1,0:T(8,128)(2,1)} %bitcast.87) | data formatting | bytes 18874368 | tf_op jit(solution)/shard_map/while/body/eval_jaxpr/gather | solution.py:37
  874.5 7.5 bitcast_dynamic-update-slice_fusion.5
  882.0 8.6 copy.41
  890.6 221.9 %all-reduce.7.cloned.1.call-done = bf16[8,24,128,128]{3,2,1,0:T(8,128)(2,1)} async-done(((bf16[8,24,128,128]{3,2,1,0:T(8,128)(2,1)}), bf16[8,24,128,128]{3,2,1,0:T(8,128)(2,1)}) %all-reduce.7.cloned.1.call-update) | async-done | bytes 6291472
  1112.6 3.9 subtract_convert_fusion
  (60 shorter events, 1.6 us)
Async XLA Ops:
  6.5 85.9 %all-gather.2.cloned.1.call-start = ((), (), s32[]{:S(2)}) async-start(), calls=%async_computation | async-start | bytes 5242880 | tf_op jit(solution)/shard_map/all_gather | solution.py:65
  7.3 718.1 %all-reduce.5.cloned.1.call-start = ((), (), s32[]{:S(2)}) async-start(), calls=%async_computation.1 | async-start | bytes 12582912
  92.4 94.7 %collective-permute-start = (bf16[8,16,128,128]{3,2,1,0:T(8,128)(2,1)}, bf16[8,16,128,128]{3,2,1,0:T(8,128)(2,1)}, u32[]{:S(2)}, u32[]{:S(2)}) collective-permute-start(bf16[8,16,128,128]{3,2,1,0:T(8,128)(2,1)} %all-gather.2.cloned.1.call-done), channel_id=1, source_target_pairs={{0,8},{4,12},{8,16},{12,20},{16,24},{20,28},{24,0},{28,4},{1,9},{5... | collective-permute-start | bytes 12582920 | tf_op jit(solution)/shard_map/ppermute | solution.py:12
  93.9 180.8 %collective-permute-start.1 = (bf16[8,16,128,128]{3,2,1,0:T(8,128)(2,1)}, bf16[8,16,128,128]{3,2,1,0:T(8,128)(2,1)}, u32[]{:S(2)}, u32[]{:S(2)}) collective-permute-start(bf16[8,16,128,128]{3,2,1,0:T(8,128)(2,1)} %all-gather.2.cloned.1.call-done), channel_id=1, source_target_pairs={{0,4},{4,8},{8,12},{12,16},{16,20},{20,24},{24,28},{28,0},{1,5},{5... | collective-permute-start | bytes 12582920 | tf_op jit(solution)/shard_map/ppermute | solution.py:12
  93.9 184.4 %collective-permute-start.2 = (bf16[8,16,128,128]{3,2,1,0:T(8,128)(2,1)}, bf16[8,16,128,128]{3,2,1,0:T(8,128)(2,1)}, u32[]{:S(2)}, u32[]{:S(2)}) collective-permute-start(bf16[8,16,128,128]{3,2,1,0:T(8,128)(2,1)} %all-gather.2.cloned.1.call-done), channel_id=1, source_target_pairs={{0,28},{4,0},{8,4},{12,8},{16,12},{20,16},{24,20},{28,24},{1,29},{... | collective-permute-start | bytes 12582920 | tf_op jit(solution)/shard_map/ppermute | solution.py:12
  96.5 269.2 %collective-permute-start.3 = (bf16[8,16,128,128]{3,2,1,0:T(8,128)(2,1)}, bf16[8,16,128,128]{3,2,1,0:T(8,128)(2,1)}, u32[]{:S(2)}, u32[]{:S(2)}) collective-permute-start(bf16[8,16,128,128]{3,2,1,0:T(8,128)(2,1)} %all-gather.2.cloned.1.call-done), channel_id=1, source_target_pairs={{0,24},{4,28},{8,0},{12,4},{16,8},{20,12},{24,16},{28,20},{1,25},{... | collective-permute-start | bytes 12582920 | tf_op jit(solution)/shard_map/ppermute | solution.py:12
  101.3 176.5 %copy-start.1 = (bf16[8,16,128,128]{3,2,1,0:T(8,128)(2,1)S(1)}, bf16[8,16,128,128]{3,2,1,0:T(8,128)(2,1)}, u32[]{:S(2)}) copy-start(bf16[8,16,128,128]{3,2,1,0:T(8,128)(2,1)} %all-gather.2.cloned.1.call-done) | copy-start | bytes 12582916
  368.8 8.8 copy-start
  504.6 0.9 copy-start.2
  504.6 1.2 copy-start.3
  504.7 607.9 %all-reduce.7.cloned.1.call-start = ((), (), s32[]{:S(2)}) async-start(), calls=%async_computation.2 | async-start | bytes 12582912
Sparse Core Ops, SparseCore 0:
  8.9 83.4 all-gather.1
  504.8 220.5 all-reduce.4
  890.8 221.7 all-reduce.6
where the time goes:
time: 1130 us; the launch traced here: 1120 us
  waiting for transfers between devices  781 us (69%)
  local copies, waits for them, and re-layouts  263 us (23%)
  matrix products  53.4 us (5%)
  between operations  13.9 us (1%)
    unnamed x5, waiting for transfers between devices  441 us
    ppermute x4, waiting for transfers between devices, shifted(): return lax.ppermute(value, axis, pairs)  255 us
    gather x16, local copies, waits for them, and re-layouts, one_group(): picked = flat_blocks[index_part]  214 us
    all_gather x1, waiting for transfers between devices, local(): full_rows = lax.all_gather(blocks, 'depth', axis=1, tiled=True)  85.1 us
    dot_general x8, matrix products, one_group(): jnp.einsum('rgsab,rgstbc->rgtac', left_split, picked_split, preferred_ele...  53.4 us
  transfers between devices with their start and end apart: 7, of which 6 were waited for; matrix products, arithmetic and copies ran while one was open for 1% of the time, Pallas kernels for 0%

commit v1 on v0

v1 whole, which is shorter than its diff:
```python
import jax
import jax.numpy as jnp
from jax import lax
from jax.experimental import pallas as pl
from jax.experimental.pallas import tpu as pltpu
from jax.sharding import PartitionSpec as P

REACH = 8
WIDE = 2 * REACH
SPAN = 2 * REACH + 2


def permuted(value, axes, pairs):
    return lax.ppermute(value, axes, pairs)


def depth_pieces(own):
    count = lax.axis_size("depth")
    me = lax.axis_index("depth")
    if count != 4:
        pieces, owners = [own], [me]
        for step in range(1, count):
            pairs = [(i, (i + step) % count) for i in range(count)]
            pieces.append(permuted(own, "depth", pairs))
            owners.append((me - step) % count)
        return pieces, owners
    partner = permuted(own, "depth", [(0, 1), (1, 0), (2, 3), (3, 2)])
    across = permuted(own, "depth", [(1, 2), (2, 1)])
    across_outer = permuted(partner, "depth", [(1, 2), (2, 1)])
    outward = permuted(across, "depth", [(1, 0), (2, 3)])
    outward_outer = permuted(across_outer, "depth", [(1, 0), (2, 3)])
    at_end = jnp.logical_or(me == 0, me == 3)
    third = jnp.where(at_end, outward, across)
    fourth = jnp.where(at_end, outward_outer, across_outer)
    low = me < 2
    owners = [me, me ^ 1, jnp.where(low, 2, 1), jnp.where(low, 3, 0)]
    return [own, partner, third, fourth], owners


def row_groups(pieces):
    rows, cols = lax.axis_size("row"), lax.axis_size("col")
    axes = ("row", "col")
    if rows == 4 and cols == 2:
        place = lax.axis_index("row")
        core = lax.axis_index("col")
        even = place % 2 == 0
        swap_x = [(0, 1), (1, 0), (2, 3), (3, 2)]
        swap_y = [(0, 2), (2, 0), (1, 3), (3, 1)]
        swap_core = [(0, 1), (1, 0)]
        by_x = [permuted(p, "row", swap_x) for p in pieces]
        by_y = [permuted(p, "row", swap_y) for p in by_x]
        send_x = (core == 0) == even
        shared = [jnp.where(send_x, a, b) for a, b in zip(by_x, by_y)]
        other = [permuted(p, "col", swap_core) for p in pieces]
        shared = [permuted(p, "col", swap_core) for p in shared]
        beside = jnp.where(core == 0, 1, -1)
        over = jnp.where(even, 2, -2)
        return [pieces, other, by_x, by_y, shared], [0, beside, over, -over, -beside]
    count = rows * cols
    groups, offsets = [pieces], [0]
    for offset in (1, -1, 2, -2):
        pairs = [(i, (i - offset) % count) for i in range(count)]
        groups.append([permuted(p, axes, pairs) for p in pieces])
        offsets.append(offset)
    return groups, offsets


def purify_kernel(piece_count, piece_rows, piece_slots, own_rows, out_slots, *refs):
    place_ref, hole_ref, keep_ref, target_ref = refs[:4]
    piece_refs = refs[4 : 4 + piece_count]
    out_ref, panel, square, sem = refs[4 + piece_count :]
    window = own_rows + 2 * WIDE
    pairs = window // 2
    edge = out_ref.shape[-1]
    per_piece = piece_rows * piece_slots

    zero = jnp.zeros((edge, edge), jnp.bfloat16)

    for pair in range(pairs):
        base = pair * 2 * SPAN
        for half in range(2):
            for u in range(SPAN):
                row = 2 * pair - REACH + u
                inside = 0 <= row < window
                banded = (u < SPAN - 1) if half == 0 else (u > 0)
                if not (inside and banded):
                    panel[base + half * SPAN + u] = zero

    @pl.loop(0, window)
    def _(row):
        spot = hole_ref[row]

        @pl.when(spot >= 0)
        def _():
            panel[spot] = zero

    started = jnp.int32(0)
    for number, piece in enumerate(piece_refs):

        def start(row, done, number=number, piece=piece):
            for slot in range(piece_slots):
                spot = place_ref[number * per_piece + row * piece_slots + slot]

                @pl.when(spot >= 0)
                def _():
                    pltpu.make_async_copy(piece.at[row, slot], panel.at[spot], sem).start()

                done = done + jnp.where(spot >= 0, 1, 0)
            return done

        started = lax.fori_loop(0, piece_rows, start, started)

    @pl.loop(0, square.shape[0])
    def _(spot):
        square[spot] = zero

    @pl.loop(0, started)
    def _(_):
        pltpu.make_async_copy(piece_refs[0].at[0, 0], panel.at[0], sem).wait()

    cols = window + 2 * REACH
    first_pair = WIDE // 2

    @pl.loop(0, own_rows // 2)
    def _(pair_of_rows):
        base = (pair_of_rows + first_pair) * 2 * SPAN
        for delta in range(-REACH, REACH + 1):
            inner = range(max(delta, 0) - REACH // 2, min(delta, 0) + REACH // 2 + 1)
            left = jnp.concatenate(
                [
                    jnp.concatenate(
                        [
                            panel[base + e * 2 * SPAN + h * SPAN + a - 2 * e + REACH]
                            for e in inner
                            for h in range(2)
                        ],
                        axis=1,
                    )
                    for a in range(2)
                ],
                axis=0,
            )
            right = jnp.concatenate(
                [
                    panel[
                        pl.ds(
                            base + delta * 2 * SPAN + h * SPAN + 2 * (inner[0] - delta) + REACH,
                            2 * len(inner),
                        )
                    ].reshape(2 * len(inner) * edge, edge)
                    for h in range(2)
                ],
                axis=1,
            )
            both = jnp.dot(left, right, preferred_element_type=jnp.float32)
            for a in range(2):
                for h in range(2):
                    row = 2 * pair_of_rows + a
                    col = 2 * (pair_of_rows + first_pair + delta) + h
                    keep = keep_ref[row * window + col]
                    part = both[a * edge : (a + 1) * edge, h * edge : (h + 1) * edge]
                    part = jnp.where(keep > 0, part, 0.0)
                    square[row * cols + col + REACH] = part.astype(jnp.bfloat16)

    @pl.loop(0, own_rows)
    def _(row):
        for slot in range(out_slots):
            col = target_ref[row * out_slots + slot]
            pair = lax.shift_right_logical(col, 1)
            half = col - 2 * pair
            left = square[pl.ds(row * cols + 2 * pair, SPAN)]
            left = jnp.concatenate([left[u] for u in range(SPAN)], axis=1)
            right = panel[pl.ds((2 * pair + half) * SPAN, SPAN)].reshape(SPAN * edge, edge)
            cubed = jnp.dot(left, right, preferred_element_type=jnp.float32)
            own = square[row * cols + col + REACH].astype(jnp.float32)
            out_ref[row, slot] = (3.0 * own - 2.0 * cubed).astype(out_ref.dtype)


def local(blocks, block_cols, product_cols):
    rows, slots, edge = blocks.shape[0], blocks.shape[1], blocks.shape[2]
    order = block_cols.shape[0]
    targets = product_cols.shape[1]
    depth_count = lax.axis_size("depth")
    out_slots = targets // depth_count
    place = lax.axis_index(("row", "col"))
    depth = lax.axis_index("depth")
    window = rows + 2 * WIDE
    first = place * rows - WIDE

    pieces, owners = depth_pieces(blocks)
    groups, offsets = row_groups(pieces)

    row_ids = jnp.stack([(place + o) * rows + jnp.arange(rows) for o in offsets])
    slot_ids = jnp.stack([o * slots + jnp.arange(slots) for o in owners])
    wanted = block_cols[row_ids[:, None, :, None] % order, slot_ids[None, :, None, :]]

    def spot_of(row, col):
        pair = col // 2
        spot = (2 * pair + col % 2) * SPAN + row - 2 * pair + REACH
        return jnp.where(col < window, spot, -1).astype(jnp.int32)

    spots = spot_of(row_ids[:, None, :, None] - first, (wanted - first) % order).reshape(-1)
    all_rows = jnp.arange(window)
    filled = (block_cols[(all_rows + first) % order] - (all_rows + first)[:, None] + REACH) % order
    hole = (2 * REACH) * (2 * REACH + 1) // 2 - jnp.sum(filled, axis=1)
    hole_col = all_rows + hole - REACH
    holes = jnp.where(hole_col >= 0, spot_of(all_rows, hole_col), -1).astype(jnp.int32)
    target_cols = (product_cols - first) % order
    keep = jnp.any(target_cols[:, :, None] == jnp.arange(window), axis=1)
    mine = lax.dynamic_slice_in_dim(target_cols, depth * out_slots, out_slots, 1)

    flat = [p for group in groups for p in group]
    kernel_body = lambda *refs: purify_kernel(len(flat), rows, slots, rows, out_slots, *refs)
    smem = pl.BlockSpec(memory_space=pltpu.SMEM)
    hbm = pl.BlockSpec(memory_space=pl.ANY)
    return pl.pallas_call(
        kernel_body,
        out_shape=jax.ShapeDtypeStruct((rows, out_slots, edge, edge), jnp.bfloat16),
        in_specs=[smem] * 4 + [hbm] * len(flat),
        out_specs=pl.BlockSpec(memory_space=pltpu.VMEM),
        scratch_shapes=[
            pltpu.VMEM((window * SPAN, edge, edge), jnp.bfloat16),
            pltpu.VMEM((rows * (window + 2 * REACH), edge, edge), jnp.bfloat16),
            pltpu.SemaphoreType.DMA,
        ],
        compiler_params=pltpu.CompilerParams(vmem_limit_bytes=56 * 2**20),
        name="purify",
    )(
        spots,
        holes,
        keep.astype(jnp.int32).reshape(-1),
        mine.astype(jnp.int32).reshape(-1),
        *flat,
    )


def solution(mesh):
    placed = (P(("row", "col"), "depth", None, None), P(), P(("row", "col"), None))
    return jax.shard_map(
        local,
        mesh=mesh,
        in_specs=placed,
        out_specs=P(("row", "col"), "depth", None, None),
        check_vma=False,
    )
```

time: 1130 us -> 217 us (0.19)
  waiting for transfers between devices: 781 us -> 143 us
  local copies, waits for them, and re-layouts: 263 us -> 9.65 us
  matrix products: 53.4 us -> 0 us
  Pallas kernels: 0 us -> 31.9 us
  starting transfers between devices: 4.93 us -> 19.3 us
  between operations: 13.9 us -> 0.2 us
    unnamed x5 -> x0, waiting for transfers between devices: 441 us -> none
    gather x19 -> x2, local copies, waits for them, and re-layouts: 215 us -> 5.15 us  [the longest x1 4.57 us: local(): block_cols[row_ids[:, None, :, None] % order, slot_ids[None, :, None, :]]]
    ppermute x4 -> x21, waiting for transfers between devices: 255 us -> 143 us  [permuted(): return lax.ppermute(value, axes, pairs)]
    all_gather x1 -> x0, waiting for transfers between devices: 85.1 us -> none  [local(): full_rows = lax.all_gather(blocks, 'depth', axis=1, tiled=True)]
    dot_general x8 -> x0, matrix products: 53.4 us -> none  [one_group(): jnp.einsum('rgsab,rgstbc->rgtac', left_split, picked_split, preferred_ele...]
    pallas_call x0 -> x1, Pallas kernels: none -> 31.9 us  [local(): pl.pallas_call(kernel_body, out_shape=jax.ShapeDtypeStruct((rows, out_slo...]
    convert_element_type x2 -> x1, local copies, waits for them, and re-layouts: 17.2 us -> 0.66 us  [local(): keep.astype(jnp.int32).reshape(-1)]
    ppermute x4 -> x21, starting transfers between devices: 4.67 us -> 19.3 us  [permuted(): return lax.ppermute(value, axes, pairs)]
  transfers between devices with their start and end apart: 7 -> 21, of which waited for: 6 -> 8; matrix products, arithmetic and copies ran while one was open for 1% -> 9% of each run, Pallas kernels for 0% -> 0%
where the time goes in v1:
time: 217 us; the launch traced here: 216 us
  waiting for transfers between devices  143 us (66%)
  Pallas kernels  31.9 us (15%)
  starting transfers between devices  19.3 us (9%)
  other arithmetic  12.2 us (6%)
  local copies, waits for them, and re-layouts  9.65 us (4%)
    ppermute x21, waiting for transfers between devices, permuted(): return lax.ppermute(value, axes, pairs)  143 us
    pallas_call x1, Pallas kernels, local(): pl.pallas_call(kernel_body, out_shape=jax.ShapeDtypeStruct((rows, out_slo...  31.9 us
    ppermute x21, starting transfers between devices, permuted(): return lax.ppermute(value, axes, pairs)  19.3 us
    select_n x4, other arithmetic, row_groups(): shared = [jnp.where(send_x, a, b) for a, b in zip(by_x, by_y)]  6.85 us
    gather x1, local copies, waits for them, and re-layouts, local(): block_cols[row_ids[:, None, :, None] % order, slot_ids[None, :, None, :]]  4.57 us
  transfers between devices with their start and end apart: 21, of which 8 were waited for; matrix products, arithmetic and copies ran while one was open for 9% of the time, Pallas kernels for 0%

profile of v1, /device:TPU:0, one launch (start us, length us, event | category | flops | bytes accessed | tf_op | source)
XLA Modules:
  0.0 216.5 jit_solution(17662336196110340823)
XLA Ops:
  0.0 3.0 %collective-permute-start = (bf16[8,4,128,128]{3,2,1,0:T(8,128)(2,1)}, bf16[8,4,128,128]{3,2,1,0:T(8,128)(2,1)}, u32[]{:S(2)}, u32[]{:S(2)}) collective-permute-start(bf16[8,4,128,128]{3,2,1,0:T(8,128)(2,1)} %refs_4_.1), channel_id=1, source_target_pairs={{0,1},{1,0},{2,3},{3,2},{4,5},{5,4},{6,7},{7,6},{8,9},{9,8},{10,11... | collective-permute-start | bytes 3145736 | tf_op jit(solution)/shard_map/ppermute | solution.py:14
  3.0 0.7 collective-permute-start.1
  3.7 22.7 %collective-permute-done.refs_5_ = bf16[8,4,128,128]{3,2,1,0:T(8,128)(2,1)} collective-permute-done((bf16[8,4,128,128]{3,2,1,0:T(8,128)(2,1)}, bf16[8,4,128,128]{3,2,1,0:T(8,128)(2,1)}, u32[]{:S(2)}, u32[]{:S(2)}) %collective-permute-start) | collective-permute-done | bytes 1048608 | tf_op jit(solution)/shard_map/ppermute | solution.py:14
  26.5 1.6 collective-permute-start.3
  28.1 0.0 collective-permute-done.1
  28.1 1.3 collective-permute-start.2
  29.4 0.0 collective-permute-done.3
  29.4 1.3 collective-permute-start.4
  30.7 1.7 collective-permute-start.9
  32.5 0.4 collective-permute-start.10
  32.8 0.0 collective-permute-start.5
  32.8 22.4 %collective-permute-done.2 = bf16[8,4,128,128]{3,2,1,0:T(8,128)(2,1)} collective-permute-done((bf16[8,4,128,128]{3,2,1,0:T(8,128)(2,1)S(1)}, bf16[8,4,128,128]{3,2,1,0:T(8,128)(2,1)}, u32[]{:S(2)}, u32[]{:S(2)}) %collective-permute-start.2) | collective-permute-done | bytes 1048608 | tf_op jit(solution)/shard_map/ppermute | solution.py:14
  55.3 1.3 broadcast_select_fusion.5.refs_6_
  56.6 0.0 copy-start.9
  56.6 0.0 copy-start
  56.6 1.6 collective-permute-start.11
  58.2 19.4 %collective-permute-done.4 = bf16[8,4,128,128]{3,2,1,0:T(8,128)(2,1)} collective-permute-done((bf16[8,4,128,128]{3,2,1,0:T(8,128)(2,1)}, bf16[8,4,128,128]{3,2,1,0:T(8,128)(2,1)}, u32[]{:S(2)}, u32[]{:S(2)}) %collective-permute-start.4) | collective-permute-done | bytes 1048608 | tf_op jit(solution)/shard_map/ppermute | solution.py:14
  77.6 2.3 %broadcast_select_fusion.4.refs_7_ = bf16[8,4,128,128]{3,2,1,0:T(8,128)(2,1)} fusion(bf16[8,4,128,128]{3,2,1,0:T(8,128)(2,1)} %collective-permute-done.4, bf16[8,4,128,128]{3,2,1,0:T(8,128)(2,1)} %collective-permute-done.3, pred[]{:T(512)S(6)} %or.3), kind=kLoop, calls=%fused_computation.6 | loop fusion | flops 524288 | bytes 3145729 | tf_op jit(solution)/shard_map/jit(_where)/select_n | solution.py:34
  79.9 1.5 collective-permute-start.12
  81.4 1.6 collective-permute-start.13
  83.0 0.0 collective-permute-done.10.refs_13_
  83.0 0.5 collective-permute-start.14
  83.6 0.1 constant_dynamic-slice_fusion
  83.6 0.1 fusion
  83.8 18.4 %collective-permute-done.11.refs_14_ = bf16[8,4,128,128]{3,2,1,0:T(8,128)(2,1)} collective-permute-done((bf16[8,4,128,128]{3,2,1,0:T(8,128)(2,1)S(1)}, bf16[8,4,128,128]{3,2,1,0:T(8,128)(2,1)}, u32[]{:S(2)}, u32[]{:S(2)}) %collective-permute-start.11) | collective-permute-done | bytes 1048608 | tf_op jit(solution)/shard_map/ppermute | solution.py:14
  102.2 1.7 collective-permute-start.15
  103.9 19.0 %collective-permute-done.12.refs_15_ = bf16[8,4,128,128]{3,2,1,0:T(8,128)(2,1)} collective-permute-done((bf16[8,4,128,128]{3,2,1,0:T(8,128)(2,1)}, bf16[8,4,128,128]{3,2,1,0:T(8,128)(2,1)}, u32[]{:S(2)}, u32[]{:S(2)}) %collective-permute-start.12) | collective-permute-done | bytes 1048608 | tf_op jit(solution)/shard_map/ppermute | solution.py:14
  122.9 1.4 collective-permute-start.16
  124.3 0.6 reshape.222.refs_3_
  124.8 0.7 reshape.223.refs_2_
  125.5 0.1 copy.6
  125.6 0.1 collective-permute-start.6
  125.7 4.4 %collective-permute-done.14.refs_17_ = bf16[8,4,128,128]{3,2,1,0:T(8,128)(2,1)} collective-permute-done((bf16[8,4,128,128]{3,2,1,0:T(8,128)(2,1)S(1)}, bf16[8,4,128,128]{3,2,1,0:T(8,128)(2,1)}, u32[]{:S(2)}, u32[]{:S(2)}) %collective-permute-start.14) | collective-permute-done | bytes 1048608 | tf_op jit(solution)/shard_map/ppermute | solution.py:14
  130.2 0.0 collective-permute-start.7
  130.2 1.1 broadcast_select_fusion.3
  131.2 1.1 broadcast_select_fusion.2
  132.4 20.3 %collective-permute-done.15.refs_18_ = bf16[8,4,128,128]{3,2,1,0:T(8,128)(2,1)} collective-permute-done((bf16[8,4,128,128]{3,2,1,0:T(8,128)(2,1)}, bf16[8,4,128,128]{3,2,1,0:T(8,128)(2,1)}, u32[]{:S(2)}, u32[]{:S(2)}) %collective-permute-start.15) | collective-permute-done | bytes 1048608 | tf_op jit(solution)/shard_map/ppermute | solution.py:14
  152.6 0.0 collective-permute-start.17
  152.6 2.3 %broadcast_select_fusion.1 = bf16[8,4,128,128]{3,2,1,0:T(8,128)(2,1)} fusion(bf16[8,4,128,128]{3,2,1,0:T(8,128)(2,1)} %collective-permute-done.11.refs_14_, bf16[8,4,128,128]{3,2,1,0:T(8,128)(2,1)} %collective-permute-done.15.refs_18_, pred[]{:T(512)S(6)} %eq.50), kind=kLoop, calls=%fused_computation.3 | loop fusion | flops 524288 | bytes 3145729 | tf_op jit(solution)/shard_map/jit(_where)/select_n | solution.py:53
  154.9 16.4 %collective-permute-done.16.refs_19_ = bf16[8,4,128,128]{3,2,1,0:T(8,128)(2,1)} collective-permute-done((bf16[8,4,128,128]{3,2,1,0:T(8,128)(2,1)}, bf16[8,4,128,128]{3,2,1,0:T(8,128)(2,1)}, u32[]{:S(2)}, u32[]{:S(2)}) %collective-permute-start.16) | collective-permute-done | bytes 1048608 | tf_op jit(solution)/shard_map/ppermute | solution.py:14
  171.4 2.3 %broadcast_select_fusion = bf16[8,4,128,128]{3,2,1,0:T(8,128)(2,1)} fusion(bf16[8,4,128,128]{3,2,1,0:T(8,128)(2,1)} %collective-permute-done.12.refs_15_, bf16[8,4,128,128]{3,2,1,0:T(8,128)(2,1)} %collective-permute-done.16.refs_19_, pred[]{:T(512)S(6)} %eq.50), kind=kLoop, calls=%fused_computation.2 | loop fusion | flops 524288 | bytes 3145729 | tf_op jit(solution)/shard_map/jit(_where)/select_n | solution.py:53
  173.7 0.0 collective-permute-done.5.refs_8_
  173.7 0.5 collective-permute-start.18
  174.2 0.0 collective-permute-done.6.refs_9_
  174.2 0.1 collective-permute-start.19
  174.3 0.0 collective-permute-done.7.refs_10_
  174.3 0.4 collective-permute-start.20
  174.8 0.5 copy-done.4
  175.2 0.4 copy-done.5
  175.6 0.1 broadcast_or_fusion
  175.6 0.1 reshape.224
  175.7 4.6 %gather_fusion = s32[640]{0:T(1024)S(1)} fusion(s32[64,16]{0,1:T(8,128)S(1)} %copy-done, s32[640]{0:T(1024)S(1)} %reshape.224), kind=kCustom, calls=%fused_computation | custom fusion | bytes 10240 | tf_op jit(solution)/shard_map/gather | solution.py:195
  180.3 0.1 add.323
  180.4 0.1 add.324
  180.5 0.6 gather_fusion.1
  181.1 0.2 fusion.2
  181.3 0.6 compare_select_fusion.6.refs_1_
  181.9 0.6 fusion.11.refs_0_
  182.5 0.0 collective-permute-done.18.refs_21_
  182.6 0.0 collective-permute-done.8.refs_11_
  182.6 0.0 collective-permute-done.20.refs_23_
  182.6 0.9 copy-done.6
  183.5 1.0 copy-done.7
  184.5 31.9 %purify.1 = bf16[8,6,128,128]{3,2,1,0:T(8,128)(2,1)} custom-call(s32[640]{0:T(1024)} %fusion.11.refs_0_, s32[40]{0:T(128)} %compare_select_fusion.6.refs_1_, s32[320]{0:T(512)} %reshape.223.refs_2_, s32[48]{0:T(128)} %reshape.222.refs_3_, bf16[8,4,128,128]{3,2,1,0:T(8,128)(2,1)} %refs_4_.1, bf16[8,4,128,128]{3,2,1,0:T(8,128)(2,1)} %collective-permute-done.refs_5_, ...), custom_call_target="tpu_custom_call" | custom-call | tf_op jit(solution)/shard_map/purify/pallas_call | solution.py:216
  (33 shorter events, 0.1 us)
Async XLA Ops:
  0.0 26.5 %collective-permute-start = (bf16[8,4,128,128]{3,2,1,0:T(8,128)(2,1)}, bf16[8,4,128,128]{3,2,1,0:T(8,128)(2,1)}, u32[]{:S(2)}, u32[]{:S(2)}) collective-permute-start(bf16[8,4,128,128]{3,2,1,0:T(8,128)(2,1)} %refs_4_.1), channel_id=1, source_target_pairs={{0,1},{1,0},{2,3},{3,2},{4,5},{5,4},{6,7},{7,6},{8,9},{9,8},{10,11... | collective-permute-start | bytes 3145736 | tf_op jit(solution)/shard_map/ppermute | solution.py:14
  3.0 25.1 %collective-permute-start.1 = (bf16[8,4,128,128]{3,2,1,0:T(8,128)(2,1)}, bf16[8,4,128,128]{3,2,1,0:T(8,128)(2,1)S(1)}, u32[]{:S(2)}, u32[]{:S(2)}) collective-permute-start(bf16[8,4,128,128]{3,2,1,0:T(8,128)(2,1)} %refs_4_.1), channel_id=1, source_target_pairs={{1,2},{2,1},{5,6},{6,5},{9,10},{10,9},{13,14},{14,13},{17,18},{18,... | collective-permute-start | bytes 3145736 | tf_op jit(solution)/shard_map/ppermute | solution.py:14
  26.5 2.9 %collective-permute-start.3 = (bf16[8,4,128,128]{3,2,1,0:T(8,128)(2,1)}, bf16[8,4,128,128]{3,2,1,0:T(8,128)(2,1)}, u32[]{:S(2)}, u32[]{:S(2)}) collective-permute-start(bf16[8,4,128,128]{3,2,1,0:T(8,128)(2,1)} %collective-permute-done.refs_5_), channel_id=1, source_target_pairs={{1,2},{2,1},{5,6},{6,5},{9,10},{10,9},{13,14},{14,13},{17,18},{18,... | collective-permute-start | bytes 3145736 | tf_op jit(solution)/shard_map/ppermute | solution.py:14
  28.1 4.7 %copy-start.8 = (bf16[8,4,128,128]{3,2,1,0:T(8,128)(2,1)}, bf16[8,4,128,128]{3,2,1,0:T(8,128)(2,1)S(1)}, u32[]{:S(2)}) copy-start(bf16[8,4,128,128]{3,2,1,0:T(8,128)(2,1)S(1)} %collective-permute-done.1) | copy-start | bytes 3145732
  28.1 27.1 %collective-permute-start.2 = (bf16[8,4,128,128]{3,2,1,0:T(8,128)(2,1)S(1)}, bf16[8,4,128,128]{3,2,1,0:T(8,128)(2,1)}, u32[]{:S(2)}, u32[]{:S(2)}) collective-permute-start(bf16[8,4,128,128]{3,2,1,0:T(8,128)(2,1)S(1)} %collective-permute-done.1), channel_id=1, source_target_pairs={{1,0},{2,3},{5,4},{6,7},{9,8},{10,11},{13,12},{14,15},{17,16},{18,... | collective-permute-start | bytes 3145736 | tf_op jit(solution)/shard_map/ppermute | solution.py:14
  29.4 48.2 %collective-permute-start.4 = (bf16[8,4,128,128]{3,2,1,0:T(8,128)(2,1)}, bf16[8,4,128,128]{3,2,1,0:T(8,128)(2,1)}, u32[]{:S(2)}, u32[]{:S(2)}) collective-permute-start(bf16[8,4,128,128]{3,2,1,0:T(8,128)(2,1)} %collective-permute-done.3), channel_id=1, source_target_pairs={{1,0},{2,3},{5,4},{6,7},{9,8},{10,11},{13,12},{14,15},{17,16},{18,... | collective-permute-start | bytes 3145736 | tf_op jit(solution)/shard_map/ppermute | solution.py:14
  30.7 50.7 %collective-permute-start.9 = (bf16[8,4,128,128]{3,2,1,0:T(8,128)(2,1)}, bf16[8,4,128,128]{3,2,1,0:T(8,128)(2,1)S(1)}, u32[]{:S(2)}, u32[]{:S(2)}) collective-permute-start(bf16[8,4,128,128]{3,2,1,0:T(8,128)(2,1)} %refs_4_.1), channel_id=1, source_target_pairs={{0,8},{8,0},{16,24},{24,16},{1,9},{9,1},{17,25},{25,17},{2,10},{10... | collective-permute-start | bytes 3145736 | tf_op jit(solution)/shard_map/ppermute | solution.py:14
  32.5 50.5 %collective-permute-start.10 = (bf16[8,4,128,128]{3,2,1,0:T(8,128)(2,1)}, bf16[8,4,128,128]{3,2,1,0:T(8,128)(2,1)S(1)}, u32[]{:S(2)}, u32[]{:S(2)}) collective-permute-start(bf16[8,4,128,128]{3,2,1,0:T(8,128)(2,1)} %collective-permute-done.refs_5_), channel_id=1, source_target_pairs={{0,8},{8,0},{16,24},{24,16},{1,9},{9,1},{17,25},{25,17},{2,10},{10... | collective-permute-start | bytes 3145736 | tf_op jit(solution)/shard_map/ppermute | solution.py:14
  32.8 140.9 %collective-permute-start.5 = (bf16[8,4,128,128]{3,2,1,0:T(8,128)(2,1)}, bf16[8,4,128,128]{3,2,1,0:T(8,128)(2,1)}, u32[]{:S(2)}, u32[]{:S(2)}) collective-permute-start(bf16[8,4,128,128]{3,2,1,0:T(8,128)(2,1)} %refs_4_.1), channel_id=1, source_target_pairs={{0,4},{4,0},{1,5},{5,1},{2,6},{6,2},{3,7},{7,3},{8,12},{12,8},{9,1... | collective-permute-start | bytes 3145736 | tf_op jit(solution)/shard_map/ppermute | solution.py:14
  56.6 73.6 %copy-start.3 = (bf16[8,4,128,128]{3,2,1,0:T(8,128)(2,1)}, bf16[8,4,128,128]{3,2,1,0:T(8,128)(2,1)S(1)}, u32[]{:S(2)}) copy-start(bf16[8,4,128,128]{3,2,1,0:T(8,128)(2,1)S(1)} %broadcast_select_fusion.5.refs_6_) | copy-start | bytes 3145732
  56.6 26.9 %copy-start.9 = (s32[8,24]{1,0:T(8,128)S(1)}, s32[8,24]{1,0:T(8,128)}, u32[]{:S(2)}) copy-start(s32[8,24]{1,0:T(8,128)} %param.5) | copy-start | bytes 2308
  56.6 68.9 %copy-start = (s32[64,16]{0,1:T(8,128)S(1)}, s32[64,16]{0,1:T(8,128)}, u32[]{:S(2)}) copy-start(s32[64,16]{0,1:T(8,128)} %param.4) | copy-start | bytes 12292
  56.6 45.5 %collective-permute-start.11 = (bf16[8,4,128,128]{3,2,1,0:T(8,128)(2,1)S(1)}, bf16[8,4,128,128]{3,2,1,0:T(8,128)(2,1)}, u32[]{:S(2)}, u32[]{:S(2)}) collective-permute-start(bf16[8,4,128,128]{3,2,1,0:T(8,128)(2,1)S(1)} %broadcast_select_fusion.5.refs_6_), channel_id=1, source_target_pairs={{0,8},{8,0},{16,24},{24,16},{1,9},{9,1},{17,25},{25,17},{2,10},{10... | collective-permute-start | bytes 3145736 | tf_op jit(solution)/shard_map/ppermute | solution.py:14
  79.9 43.0 %collective-permute-start.12 = (bf16[8,4,128,128]{3,2,1,0:T(8,128)(2,1)}, bf16[8,4,128,128]{3,2,1,0:T(8,128)(2,1)}, u32[]{:S(2)}, u32[]{:S(2)}) collective-permute-start(bf16[8,4,128,128]{3,2,1,0:T(8,128)(2,1)} %broadcast_select_fusion.4.refs_7_), channel_id=1, source_target_pairs={{0,8},{8,0},{16,24},{24,16},{1,9},{9,1},{17,25},{25,17},{2,10},{10... | collective-permute-start | bytes 3145736 | tf_op jit(solution)/shard_map/ppermute | solution.py:14
  81.4 49.8 %copy-start.1 = (bf16[8,4,128,128]{3,2,1,0:T(8,128)(2,1)}, bf16[8,4,128,128]{3,2,1,0:T(8,128)(2,1)S(1)}, u32[]{:S(2)}) copy-start(bf16[8,4,128,128]{3,2,1,0:T(8,128)(2,1)S(1)} %collective-permute-done.9.refs_12_) | copy-start | bytes 3145732
  81.4 44.2 %collective-permute-start.13 = (bf16[8,4,128,128]{3,2,1,0:T(8,128)(2,1)S(1)}, bf16[8,4,128,128]{3,2,1,0:T(8,128)(2,1)}, u32[]{:S(2)}, u32[]{:S(2)}) collective-permute-start(bf16[8,4,128,128]{3,2,1,0:T(8,128)(2,1)S(1)} %collective-permute-done.9.refs_12_), channel_id=1, source_target_pairs={{0,16},{16,0},{8,24},{24,8},{1,17},{17,1},{9,25},{25,9},{2,18},{18... | collective-permute-start | bytes 3145736 | tf_op jit(solution)/shard_map/ppermute | solution.py:14
  83.0 48.2 %copy-start.2 = (bf16[8,4,128,128]{3,2,1,0:T(8,128)(2,1)}, bf16[8,4,128,128]{3,2,1,0:T(8,128)(2,1)S(1)}, u32[]{:S(2)}) copy-start(bf16[8,4,128,128]{3,2,1,0:T(8,128)(2,1)S(1)} %collective-permute-done.10.refs_13_) | copy-start | bytes 3145732
  83.0 47.1 %collective-permute-start.14 = (bf16[8,4,128,128]{3,2,1,0:T(8,128)(2,1)S(1)}, bf16[8,4,128,128]{3,2,1,0:T(8,128)(2,1)}, u32[]{:S(2)}, u32[]{:S(2)}) collective-permute-start(bf16[8,4,128,128]{3,2,1,0:T(8,128)(2,1)S(1)} %collective-permute-done.10.refs_13_), channel_id=1, source_target_pairs={{0,16},{16,0},{8,24},{24,8},{1,17},{17,1},{9,25},{25,9},{2,18},{18... | collective-permute-start | bytes 3145736 | tf_op jit(solution)/shard_map/ppermute | solution.py:14
  102.2 50.5 %collective-permute-start.15 = (bf16[8,4,128,128]{3,2,1,0:T(8,128)(2,1)}, bf16[8,4,128,128]{3,2,1,0:T(8,128)(2,1)}, u32[]{:S(2)}, u32[]{:S(2)}) collective-permute-start(bf16[8,4,128,128]{3,2,1,0:T(8,128)(2,1)} %collective-permute-done.11.refs_14_), channel_id=1, source_target_pairs={{0,16},{16,0},{8,24},{24,8},{1,17},{17,1},{9,25},{25,9},{2,18},{18... | collective-permute-start | bytes 3145736 | tf_op jit(solution)/shard_map/ppermute | solution.py:14
  122.9 48.5 %collective-permute-start.16 = (bf16[8,4,128,128]{3,2,1,0:T(8,128)(2,1)}, bf16[8,4,128,128]{3,2,1,0:T(8,128)(2,1)}, u32[]{:S(2)}, u32[]{:S(2)}) collective-permute-start(bf16[8,4,128,128]{3,2,1,0:T(8,128)(2,1)} %collective-permute-done.12.refs_15_), channel_id=1, source_target_pairs={{0,16},{16,0},{8,24},{24,8},{1,17},{17,1},{9,25},{25,9},{2,18},{18... | collective-permute-start | bytes 3145736 | tf_op jit(solution)/shard_map/ppermute | solution.py:14
  125.6 48.6 %collective-permute-start.6 = (bf16[8,4,128,128]{3,2,1,0:T(8,128)(2,1)}, bf16[8,4,128,128]{3,2,1,0:T(8,128)(2,1)S(1)}, u32[]{:S(2)}, u32[]{:S(2)}) collective-permute-start(bf16[8,4,128,128]{3,2,1,0:T(8,128)(2,1)} %collective-permute-done.refs_5_), channel_id=1, source_target_pairs={{0,4},{4,0},{1,5},{5,1},{2,6},{6,2},{3,7},{7,3},{8,12},{12,8},{9,1... | collective-permute-start | bytes 3145736 | tf_op jit(solution)/shard_map/ppermute | solution.py:14
  130.2 44.2 %collective-permute-start.7 = (bf16[8,4,128,128]{3,2,1,0:T(8,128)(2,1)S(1)}, bf16[8,4,128,128]{3,2,1,0:T(8,128)(2,1)S(1)}, u32[]{:S(2)}, u32[]{:S(2)}) collective-permute-start(bf16[8,4,128,128]{3,2,1,0:T(8,128)(2,1)S(1)} %broadcast_select_fusion.5.refs_6_), channel_id=1, source_target_pairs={{0,4},{4,0},{1,5},{5,1},{2,6},{6,2},{3,7},{7,3},{8,12},{12,8},{9,1... | collective-permute-start | bytes 3145736 | tf_op jit(solution)/shard_map/ppermute | solution.py:14
  152.6 29.9 %collective-permute-start.17 = (bf16[8,4,128,128]{3,2,1,0:T(8,128)(2,1)}, bf16[8,4,128,128]{3,2,1,0:T(8,128)(2,1)S(1)}, u32[]{:S(2)}, u32[]{:S(2)}) collective-permute-start(bf16[8,4,128,128]{3,2,1,0:T(8,128)(2,1)} %broadcast_select_fusion.3), channel_id=1, source_target_pairs={{0,4},{4,0},{1,5},{5,1},{2,6},{6,2},{3,7},{7,3},{8,12},{12,8},{9,1... | collective-permute-start | bytes 3145736 | tf_op jit(solution)/shard_map/ppermute | solution.py:14
  171.4 11.2 %collective-permute-start.8 = (bf16[8,4,128,128]{3,2,1,0:T(8,128)(2,1)}, bf16[8,4,128,128]{3,2,1,0:T(8,128)(2,1)}, u32[]{:S(2)}, u32[]{:S(2)}) collective-permute-start(bf16[8,4,128,128]{3,2,1,0:T(8,128)(2,1)} %broadcast_select_fusion.4.refs_7_), channel_id=1, source_target_pairs={{0,4},{4,0},{1,5},{5,1},{2,6},{6,2},{3,7},{7,3},{8,12},{12,8},{9,1... | collective-permute-start | bytes 3145736 | tf_op jit(solution)/shard_map/ppermute | solution.py:14
  173.7 8.8 %collective-permute-start.18 = (bf16[8,4,128,128]{3,2,1,0:T(8,128)(2,1)}, bf16[8,4,128,128]{3,2,1,0:T(8,128)(2,1)}, u32[]{:S(2)}, u32[]{:S(2)}) collective-permute-start(bf16[8,4,128,128]{3,2,1,0:T(8,128)(2,1)} %broadcast_select_fusion.2), channel_id=1, source_target_pairs={{0,4},{4,0},{1,5},{5,1},{2,6},{6,2},{3,7},{7,3},{8,12},{12,8},{9,1... | collective-permute-start | bytes 3145736 | tf_op jit(solution)/shard_map/ppermute | solution.py:14
  174.2 1.0 copy-start.4
  174.2 8.3 %collective-permute-start.19 = (bf16[8,4,128,128]{3,2,1,0:T(8,128)(2,1)}, bf16[8,4,128,128]{3,2,1,0:T(8,128)(2,1)}, u32[]{:S(2)}, u32[]{:S(2)}) collective-permute-start(bf16[8,4,128,128]{3,2,1,0:T(8,128)(2,1)} %broadcast_select_fusion.1), channel_id=1, source_target_pairs={{0,4},{4,0},{1,5},{5,1},{2,6},{6,2},{3,7},{7,3},{8,12},{12,8},{9,1... | collective-permute-start | bytes 3145736 | tf_op jit(solution)/shard_map/ppermute | solution.py:14
  174.3 1.2 copy-start.5
  174.3 8.3 %collective-permute-start.20 = (bf16[8,4,128,128]{3,2,1,0:T(8,128)(2,1)}, bf16[8,4,128,128]{3,2,1,0:T(8,128)(2,1)S(1)}, u32[]{:S(2)}, u32[]{:S(2)}) collective-permute-start(bf16[8,4,128,128]{3,2,1,0:T(8,128)(2,1)} %broadcast_select_fusion), channel_id=1, source_target_pairs={{0,4},{4,0},{1,5},{5,1},{2,6},{6,2},{3,7},{7,3},{8,12},{12,8},{9,1... | collective-permute-start | bytes 3145736 | tf_op jit(solution)/shard_map/ppermute | solution.py:14
  182.5 1.0 copy-start.6
  183.5 1.0 copy-start.7

commit v2 on v1

--- a/solution.py
+++ b/solution.py
@@ -14,55 +14,92 @@
     return lax.ppermute(value, axes, pairs)
 
 
-def depth_pieces(own):
-    count = lax.axis_size("depth")
+together = lax.optimization_barrier
+
+
+def line_window(own, extra):
     me = lax.axis_index("depth")
-    if count != 4:
-        pieces, owners = [own], [me]
-        for step in range(1, count):
-            pairs = [(i, (i + step) % count) for i in range(count)]
-            pieces.append(permuted(own, "depth", pairs))
-            owners.append((me - step) % count)
-        return pieces, owners
-    partner = permuted(own, "depth", [(0, 1), (1, 0), (2, 3), (3, 2)])
-    across = permuted(own, "depth", [(1, 2), (2, 1)])
-    across_outer = permuted(partner, "depth", [(1, 2), (2, 1)])
-    outward = permuted(across, "depth", [(1, 0), (2, 3)])
-    outward_outer = permuted(across_outer, "depth", [(1, 0), (2, 3)])
+    core = lax.axis_index("col")
+    even = lax.axis_index("row") % 2 == 0
     at_end = jnp.logical_or(me == 0, me == 3)
-    third = jnp.where(at_end, outward, across)
-    fourth = jnp.where(at_end, outward_outer, across_outer)
-    low = me < 2
-    owners = [me, me ^ 1, jnp.where(low, 2, 1), jnp.where(low, 3, 0)]
-    return [own, partner, third, fourth], owners
-
-
-def row_groups(pieces):
-    rows, cols = lax.axis_size("row"), lax.axis_size("col")
-    axes = ("row", "col")
-    if rows == 4 and cols == 2:
-        place = lax.axis_index("row")
-        core = lax.axis_index("col")
-        even = place % 2 == 0
-        swap_x = [(0, 1), (1, 0), (2, 3), (3, 2)]
-        swap_y = [(0, 2), (2, 0), (1, 3), (3, 1)]
-        swap_core = [(0, 1), (1, 0)]
-        by_x = [permuted(p, "row", swap_x) for p in pieces]
-        by_y = [permuted(p, "row", swap_y) for p in by_x]
-        send_x = (core == 0) == even
-        shared = [jnp.where(send_x, a, b) for a, b in zip(by_x, by_y)]
-        other = [permuted(p, "col", swap_core) for p in pieces]
-        shared = [permuted(p, "col", swap_core) for p in shared]
-        beside = jnp.where(core == 0, 1, -1)
-        over = jnp.where(even, 2, -2)
-        return [pieces, other, by_x, by_y, shared], [0, beside, over, -over, -beside]
-    count = rows * cols
-    groups, offsets = [pieces], [0]
+    ends = [(0, 1), (1, 0), (2, 3), (3, 2)]
+    middle = [(1, 2), (2, 1)]
+    outward = [(1, 0), (2, 3)]
+
+    def along_x(value):
+        return permuted(value, "row", [(0, 1), (1, 0), (2, 3), (3, 2)])
+
+    def along_y(value):
+        return permuted(value, "row", [(0, 2), (2, 0), (1, 3), (3, 1)])
+
+    def over_core(value):
+        return permuted(value, "col", [(0, 1), (1, 0)])
+
+    send_x = (core == 0) == even
+
+    def shared(by_x, by_y):
+        return over_core(jnp.where(send_x, by_x, by_y))
+
+    x0 = along_x(own)
+    p1 = permuted(own, "depth", ends)
+    across = permuted(own, "depth", middle)
+    x0, p1, across = together((x0, p1, across))
+
+    x1 = along_x(p1)
+    y0 = along_y(x0)
+    across_outer = permuted(p1, "depth", middle)
+    out = permuted(across, "depth", outward)
+    extra, x1, y0, across_outer, out = together((extra, x1, y0, across_outer, out))
+
+    p2 = jnp.where(at_end, out, across)
+    x2 = along_x(p2)
+    y1 = along_y(x1)
+    out_outer = permuted(across_outer, "depth", outward)
+    c0 = over_core(own)
+    s0 = shared(x0, y0)
+    x2, y1, out_outer, c0, s0 = together((x2, y1, out_outer, c0, s0))
+
+    p3 = jnp.where(at_end, out_outer, across_outer)
+    x3 = along_x(p3)
+    y2 = along_y(x2)
+    c1 = over_core(p1)
+    c2 = over_core(p2)
+    s1 = shared(x1, y1)
+    x3, y2, c1, c2, s1 = together((x3, y2, c1, c2, s1))
+
+    y3 = along_y(x3)
+    c3 = over_core(p3)
+    s2 = shared(x2, y2)
+    y3, c3, s2 = together((y3, c3, s2))
+    s3 = shared(x3, y3)
+
+    groups = [
+        [own, p1, p2, p3],
+        [c0, c1, c2, c3],
+        [x0, x1, x2, x3],
+        [y0, y1, y2, y3],
+        [s0, s1, s2, s3],
+    ]
+    return groups, extra
+
+
+def ring_window(own, extra):
+    depths = lax.axis_size("depth")
+    pieces = [own]
+    for step in range(1, depths):
+        pairs = [(i, (i + step) % depths) for i in range(depths)]
+        pieces.append(permuted(own, "depth", pairs))
+    count = lax.axis_size(("row", "col"))
+    groups = [pieces]
     for offset in (1, -1, 2, -2):
         pairs = [(i, (i - offset) % count) for i in range(count)]
-        groups.append([permuted(p, axes, pairs) for p in pieces])
-        offsets.append(offset)
-    return groups, offsets
+        groups.append([permuted(p, ("row", "col"), pairs) for p in pieces])
+    return groups, extra
+
+
+def window_plan():
+    sizes = (lax.axis_size("row"), lax.axis_size("col"), lax.axis_size("depth"))
+    return line_window if sizes == (4, 2, 4) else ring_window
 
 
 def purify_kernel(piece_count, piece_rows, piece_slots, own_rows, out_slots, *refs):
@@ -176,6 +213,17 @@
             out_ref[row, slot] = (3.0 * own - 2.0 * cubed).astype(out_ref.dtype)
 
 
+def window_places(place, depth):
+    if window_plan() is line_window:
+        low = depth < 2
+        owners = [depth, depth ^ 1, jnp.where(low, 2, 1), jnp.where(low, 3, 0)]
+        beside = jnp.where(lax.axis_index("col") == 0, 1, -1)
+        over = jnp.where(lax.axis_index("row") % 2 == 0, 2, -2)
+        return owners, [0, beside, over, -over, -beside]
+    depths = lax.axis_size("depth")
+    return [(depth - step) % depths for step in range(depths)], [0, 1, -1, 2, -2]
+
+
 def local(blocks, block_cols, product_cols):
     rows, slots, edge = blocks.shape[0], blocks.shape[1], blocks.shape[2]
     order = block_cols.shape[0]
@@ -187,9 +235,7 @@
     window = rows + 2 * WIDE
     first = place * rows - WIDE
 
-    pieces, owners = depth_pieces(blocks)
-    groups, offsets = row_groups(pieces)
-
+    owners, offsets = window_places(place, depth)
     row_ids = jnp.stack([(place + o) * rows + jnp.arange(rows) for o in offsets])
     slot_ids = jnp.stack([o * slots + jnp.arange(slots) for o in owners])
     wanted = block_cols[row_ids[:, None, :, None] % order, slot_ids[None, :, None, :]]
@@ -207,8 +253,11 @@
     holes = jnp.where(hole_col >= 0, spot_of(all_rows, hole_col), -1).astype(jnp.int32)
     target_cols = (product_cols - first) % order
     keep = jnp.any(target_cols[:, :, None] == jnp.arange(window), axis=1)
+    keep = keep.astype(jnp.int32).reshape(-1)
     mine = lax.dynamic_slice_in_dim(target_cols, depth * out_slots, out_slots, 1)
-
+    mine = mine.astype(jnp.int32).reshape(-1)
+
+    groups, tables = window_plan()(blocks, (spots, holes, keep, mine))
     flat = [p for group in groups for p in group]
     kernel_body = lambda *refs: purify_kernel(len(flat), rows, slots, rows, out_slots, *refs)
     smem = pl.BlockSpec(memory_space=pltpu.SMEM)
@@ -225,13 +274,7 @@
         ],
         compiler_params=pltpu.CompilerParams(vmem_limit_bytes=56 * 2**20),
         name="purify",
-    )(
-        spots,
-        holes,
-        keep.astype(jnp.int32).reshape(-1),
-        mine.astype(jnp.int32).reshape(-1),
-        *flat,
-    )
+    )(*tables, *flat)
 
 
 def solution(mesh):

time: 217 us -> 182 us (0.84)
  waiting for transfers between devices: 143 us -> 110 us
  other arithmetic: 12.2 us -> 4.24 us
  starting transfers between devices: 19.3 us -> 22.9 us
  local copies, waits for them, and re-layouts: 9.65 us -> 12.1 us
    ppermute x21, waiting for transfers between devices: 143 us -> 110 us  [permuted(): return lax.ppermute(value, axes, pairs)]
    select_n x6, other arithmetic: 10.5 us -> 1.93 us  [the longest x1 1.34 us: line_window(): p2 = jnp.where(at_end, out, across)]
    ppermute x21, starting transfers between devices: 19.3 us -> 22.9 us  [permuted(): return lax.ppermute(value, axes, pairs)]
    unnamed x21 -> x37, local copies, waits for them, and re-layouts: 2.86 us -> 5.28 us
  transfers between devices with their start and end apart: 21 -> 21, of which waited for: 8 -> 10; matrix products, arithmetic and copies ran while one was open for 9% -> 6% of each run, Pallas kernels for 0% -> 0%
where the time goes in v2:
time: 182 us; the launch traced here: 181 us
  waiting for transfers between devices  110 us (60%)
  Pallas kernels  31.9 us (18%)
  starting transfers between devices  22.9 us (13%)
  local copies, waits for them, and re-layouts  12.1 us (7%)
  other arithmetic  4.24 us (2%)
    ppermute x21, waiting for transfers between devices, permuted(): return lax.ppermute(value, axes, pairs)  110 us
    pallas_call x1, Pallas kernels, local(): pl.pallas_call(kernel_body, out_shape=jax.ShapeDtypeStruct((rows, out_slo...  31.9 us
    ppermute x21, starting transfers between devices, permuted(): return lax.ppermute(value, axes, pairs)  22.9 us
    unnamed x37, local copies, waits for them, and re-layouts  5.28 us
    gather x1, local copies, waits for them, and re-layouts, local(): block_cols[row_ids[:, None, :, None] % order, slot_ids[None, :, None, :]]  4.57 us
  transfers between devices with their start and end apart: 21, of which 10 were waited for; matrix products, arithmetic and copies ran while one was open for 6% of the time, Pallas kernels for 0%

profile of v2, /device:TPU:0, one launch (start us, length us, event | category | flops | bytes accessed | tf_op | source)
XLA Modules:
  0.0 181.5 jit_solution(18225959763867191582)
XLA Ops:
  0.0 1.8 collective-permute-start.2
  1.8 4.9 %collective-permute-start.1 = (bf16[8,4,128,128]{3,2,1,0:T(8,128)(2,1)}, bf16[8,4,128,128]{3,2,1,0:T(8,128)(2,1)}, u32[]{:S(2)}, u32[]{:S(2)}) collective-permute-start(bf16[8,4,128,128]{3,2,1,0:T(8,128)(2,1)} %refs_4_.1), channel_id=1, source_target_pairs={{0,1},{1,0},{2,3},{3,2},{4,5},{5,4},{6,7},{7,6},{8,9},{9,8},{10,11... | collective-permute-start | bytes 3145736 | tf_op jit(solution)/shard_map/ppermute | solution.py:14
  6.7 1.5 collective-permute-start
  8.2 0.0 collective-permute-start.10
  8.2 0.7 add_select_fusion.1
  8.9 0.1 constant_dynamic-slice_fusion
  9.0 0.6 reshape.222.refs_3_
  9.6 0.1 fusion
  9.7 0.7 reshape.223.refs_2_
  10.4 0.8 copy.6
  11.3 0.0 collective-permute-done.2
  11.3 18.6 %collective-permute-done.1.refs_5_ = bf16[8,4,128,128]{3,2,1,0:T(8,128)(2,1)} collective-permute-done((bf16[8,4,128,128]{3,2,1,0:T(8,128)(2,1)}, bf16[8,4,128,128]{3,2,1,0:T(8,128)(2,1)}, u32[]{:S(2)}, u32[]{:S(2)}) %collective-permute-start.1) | collective-permute-done | bytes 1048608 | tf_op jit(solution)/shard_map/ppermute | solution.py:14
  29.9 1.4 collective-permute-done.refs_12_
  31.3 1.6 collective-permute-start.5
  32.9 1.5 collective-permute-start.3
  34.4 1.3 collective-permute-start.6
  35.7 1.6 collective-permute-start.4
  37.3 0.1 broadcast_or_fusion
  37.3 0.1 reshape.224
  37.5 4.6 %gather_fusion = s32[640]{0:T(1024)S(1)} fusion(s32[64,16]{0,1:T(8,128)S(1)} %copy-done, s32[640]{0:T(1024)S(1)} %reshape.224), kind=kCustom, calls=%fused_computation | custom fusion | bytes 10240 | tf_op jit(solution)/shard_map/gather | solution.py:241
  42.0 0.1 add.324
  42.1 0.1 add.325
  42.3 0.6 gather_fusion.1
  42.9 0.2 fusion.2
  43.0 0.5 compare_select_fusion.6.refs_1_
  43.6 0.6 fusion.11.refs_0_
  44.2 15.6 %collective-permute-done.6 = bf16[8,4,128,128]{3,2,1,0:T(8,128)(2,1)} collective-permute-done((bf16[8,4,128,128]{3,2,1,0:T(8,128)(2,1)}, bf16[8,4,128,128]{3,2,1,0:T(8,128)(2,1)}, u32[]{:S(2)}, u32[]{:S(2)}) %collective-permute-start.6) | collective-permute-done | bytes 1048608 | tf_op jit(solution)/shard_map/ppermute | solution.py:14
  59.8 0.0 collective-permute-done.3.refs_13_
  59.9 0.1 broadcast_select_fusion.3
  60.0 0.9 copy-done.3
  60.9 0.0 collective-permute-start.11
  60.9 1.3 broadcast_select_fusion.5.refs_6_
  62.2 0.6 collective-permute-start.7
  62.8 1.3 collective-permute-start.9
  64.1 1.6 collective-permute-start.8
  65.7 0.0 collective-permute-done.10.refs_8_
  65.7 0.0 collective-permute-start.14
  65.7 0.0 collective-permute-done.11.refs_20_
  65.7 0.5 collective-permute-start.15
  66.2 21.6 %collective-permute-done.7.refs_14_ = bf16[8,4,128,128]{3,2,1,0:T(8,128)(2,1)S(1)} collective-permute-done((bf16[8,4,128,128]{3,2,1,0:T(8,128)(2,1)S(1)}, bf16[8,4,128,128]{3,2,1,0:T(8,128)(2,1)S(1)}, u32[]{:S(2)}, u32[]{:S(2)}) %collective-permute-start.7) | collective-permute-done | bytes 1048608 | tf_op jit(solution)/shard_map/ppermute | solution.py:14
  87.9 2.4 %collective-permute-done.9 = bf16[8,4,128,128]{3,2,1,0:T(8,128)(2,1)S(1)} collective-permute-done((bf16[8,4,128,128]{3,2,1,0:T(8,128)(2,1)}, bf16[8,4,128,128]{3,2,1,0:T(8,128)(2,1)S(1)}, u32[]{:S(2)}, u32[]{:S(2)}) %collective-permute-start.9) | collective-permute-done | bytes 1048608 | tf_op jit(solution)/shard_map/ppermute | solution.py:14
  90.3 0.1 broadcast_select_fusion.4.refs_7_
  90.4 0.9 copy-done.6
  91.3 0.1 broadcast_select_fusion.2
  91.5 0.1 collective-permute-start.16
  91.5 1.6 collective-permute-start.12
  93.1 1.5 collective-permute-start.13
  94.6 0.0 collective-permute-done.14.refs_9_
  94.6 0.1 collective-permute-start.18
  94.7 0.0 collective-permute-done.15.refs_10_
  94.7 22.4 %collective-permute-done.12.refs_15_ = bf16[8,4,128,128]{3,2,1,0:T(8,128)(2,1)S(1)} collective-permute-done((bf16[8,4,128,128]{3,2,1,0:T(8,128)(2,1)S(1)}, bf16[8,4,128,128]{3,2,1,0:T(8,128)(2,1)S(1)}, u32[]{:S(2)}, u32[]{:S(2)}) %collective-permute-start.12) | collective-permute-done | bytes 1048608 | tf_op jit(solution)/shard_map/ppermute | solution.py:14
  117.1 1.2 collective-permute-done.13.refs_18_
  118.3 0.1 broadcast_select_fusion.1
  118.5 0.9 copy-done.9
  119.3 0.0 collective-permute-start.19
  119.3 1.5 collective-permute-start.17
  120.8 0.0 collective-permute-done.18.refs_11_
  120.8 1.1 collective-permute-done.19.refs_22_
  122.0 22.9 %collective-permute-done.17.refs_19_ = bf16[8,4,128,128]{3,2,1,0:T(8,128)(2,1)S(1)} collective-permute-done((bf16[8,4,128,128]{3,2,1,0:T(8,128)(2,1)S(1)}, bf16[8,4,128,128]{3,2,1,0:T(8,128)(2,1)S(1)}, u32[]{:S(2)}, u32[]{:S(2)}) %collective-permute-start.17) | collective-permute-done | bytes 1048608 | tf_op jit(solution)/shard_map/ppermute | solution.py:14
  144.9 0.1 broadcast_select_fusion
  145.0 0.8 copy-done.10
  145.9 2.7 %collective-permute-done.20.refs_23_ = bf16[8,4,128,128]{3,2,1,0:T(8,128)(2,1)S(1)} collective-permute-done((bf16[8,4,128,128]{3,2,1,0:T(8,128)(2,1)S(1)}, bf16[8,4,128,128]{3,2,1,0:T(8,128)(2,1)S(1)}, u32[]{:S(2)}, u32[]{:S(2)}) %collective-permute-start.20) | collective-permute-done | bytes 1048608 | tf_op jit(solution)/shard_map/ppermute | solution.py:14
  148.5 1.0 copy-done.17
  149.5 31.9 %purify.1 = bf16[8,6,128,128]{3,2,1,0:T(8,128)(2,1)} custom-call(s32[640]{0:T(1024)} %fusion.11.refs_0_, s32[40]{0:T(128)} %compare_select_fusion.6.refs_1_, s32[320]{0:T(512)} %reshape.223.refs_2_, s32[48]{0:T(128)} %reshape.222.refs_3_, bf16[8,4,128,128]{3,2,1,0:T(8,128)(2,1)} %refs_4_.1, bf16[8,4,128,128]{3,2,1,0:T(8,128)(2,1)} %collective-permute-done.1.refs_5_, ...), custom_call_target="tpu_custom_call" | custom-call | tf_op jit(solution)/shard_map/purify/pallas_call | solution.py:265
  (48 shorter events, 0.2 us)
Async XLA Ops:
  0.0 37.5 %copy-start = (s32[64,16]{0,1:T(8,128)S(1)}, s32[64,16]{0,1:T(8,128)}, u32[]{:S(2)}) copy-start(s32[64,16]{0,1:T(8,128)} %param.4) | copy-start | bytes 12292
  0.0 11.3 %collective-permute-start.2 = (bf16[8,4,128,128]{3,2,1,0:T(8,128)(2,1)}, bf16[8,4,128,128]{3,2,1,0:T(8,128)(2,1)}, u32[]{:S(2)}, u32[]{:S(2)}) collective-permute-start(bf16[8,4,128,128]{3,2,1,0:T(8,128)(2,1)} %refs_4_.1), channel_id=1, source_target_pairs={{1,2},{2,1},{5,6},{6,5},{9,10},{10,9},{13,14},{14,13},{17,18},{18,... | collective-permute-start | bytes 3145736 | tf_op jit(solution)/shard_map/ppermute | solution.py:14
  1.8 28.1 %collective-permute-start.1 = (bf16[8,4,128,128]{3,2,1,0:T(8,128)(2,1)}, bf16[8,4,128,128]{3,2,1,0:T(8,128)(2,1)}, u32[]{:S(2)}, u32[]{:S(2)}) collective-permute-start(bf16[8,4,128,128]{3,2,1,0:T(8,128)(2,1)} %refs_4_.1), channel_id=1, source_target_pairs={{0,1},{1,0},{2,3},{3,2},{4,5},{5,4},{6,7},{7,6},{8,9},{9,8},{10,11... | collective-permute-start | bytes 3145736 | tf_op jit(solution)/shard_map/ppermute | solution.py:14
  6.7 24.5 %collective-permute-start = (bf16[8,4,128,128]{3,2,1,0:T(8,128)(2,1)}, bf16[8,4,128,128]{3,2,1,0:T(8,128)(2,1)S(1)}, u32[]{:S(2)}, u32[]{:S(2)}) collective-permute-start(bf16[8,4,128,128]{3,2,1,0:T(8,128)(2,1)} %refs_4_.1), channel_id=1, source_target_pairs={{0,8},{8,0},{16,24},{24,16},{1,9},{9,1},{17,25},{25,17},{2,10},{10... | collective-permute-start | bytes 3145736 | tf_op jit(solution)/shard_map/ppermute | solution.py:14
  8.2 57.5 %collective-permute-start.10 = (bf16[8,4,128,128]{3,2,1,0:T(8,128)(2,1)}, bf16[8,4,128,128]{3,2,1,0:T(8,128)(2,1)}, u32[]{:S(2)}, u32[]{:S(2)}) collective-permute-start(bf16[8,4,128,128]{3,2,1,0:T(8,128)(2,1)} %refs_4_.1), channel_id=1, source_target_pairs={{0,4},{4,0},{1,5},{5,1},{2,6},{6,2},{3,7},{7,3},{8,12},{12,8},{9,1... | collective-permute-start | bytes 3145736 | tf_op jit(solution)/shard_map/ppermute | solution.py:14
  31.3 28.6 %copy-start.1 = (bf16[8,4,128,128]{3,2,1,0:T(8,128)(2,1)}, bf16[8,4,128,128]{3,2,1,0:T(8,128)(2,1)S(1)}, u32[]{:S(2)}) copy-start(bf16[8,4,128,128]{3,2,1,0:T(8,128)(2,1)S(1)} %collective-permute-done.refs_12_) | copy-start | bytes 3145732
  31.3 28.6 %collective-permute-start.5 = (bf16[8,4,128,128]{3,2,1,0:T(8,128)(2,1)}, bf16[8,4,128,128]{3,2,1,0:T(8,128)(2,1)}, u32[]{:S(2)}, u32[]{:S(2)}) collective-permute-start(bf16[8,4,128,128]{3,2,1,0:T(8,128)(2,1)} %collective-permute-done.1.refs_5_), channel_id=1, source_target_pairs={{1,2},{2,1},{5,6},{6,5},{9,10},{10,9},{13,14},{14,13},{17,18},{18,... | collective-permute-start | bytes 3145736 | tf_op jit(solution)/shard_map/ppermute | solution.py:14
  32.9 26.9 %collective-permute-start.3 = (bf16[8,4,128,128]{3,2,1,0:T(8,128)(2,1)}, bf16[8,4,128,128]{3,2,1,0:T(8,128)(2,1)S(1)}, u32[]{:S(2)}, u32[]{:S(2)}) collective-permute-start(bf16[8,4,128,128]{3,2,1,0:T(8,128)(2,1)} %collective-permute-done.1.refs_5_), channel_id=1, source_target_pairs={{0,8},{8,0},{16,24},{24,16},{1,9},{9,1},{17,25},{25,17},{2,10},{10... | collective-permute-start | bytes 3145736 | tf_op jit(solution)/shard_map/ppermute | solution.py:14
  34.4 25.4 %collective-permute-start.6 = (bf16[8,4,128,128]{3,2,1,0:T(8,128)(2,1)}, bf16[8,4,128,128]{3,2,1,0:T(8,128)(2,1)}, u32[]{:S(2)}, u32[]{:S(2)}) collective-permute-start(bf16[8,4,128,128]{3,2,1,0:T(8,128)(2,1)} %collective-permute-done.2), channel_id=1, source_target_pairs={{1,0},{2,3},{5,4},{6,7},{9,8},{10,11},{13,12},{14,15},{17,16},{18,... | collective-permute-start | bytes 3145736 | tf_op jit(solution)/shard_map/ppermute | solution.py:14
  35.7 24.2 %collective-permute-start.4 = (bf16[8,4,128,128]{3,2,1,0:T(8,128)(2,1)S(1)}, bf16[8,4,128,128]{3,2,1,0:T(8,128)(2,1)S(1)}, u32[]{:S(2)}, u32[]{:S(2)}) collective-permute-start(bf16[8,4,128,128]{3,2,1,0:T(8,128)(2,1)S(1)} %collective-permute-done.refs_12_), channel_id=1, source_target_pairs={{0,16},{16,0},{8,24},{24,8},{1,17},{17,1},{9,25},{25,9},{2,18},{18... | collective-permute-start | bytes 3145736 | tf_op jit(solution)/shard_map/ppermute | solution.py:14
  59.8 1.0 copy-start.3
  59.9 30.5 %copy-start.2 = (bf16[8,4,128,128]{3,2,1,0:T(8,128)(2,1)}, bf16[8,4,128,128]{3,2,1,0:T(8,128)(2,1)S(1)}, u32[]{:S(2)}) copy-start(bf16[8,4,128,128]{3,2,1,0:T(8,128)(2,1)S(1)} %collective-permute-done.3.refs_13_) | copy-start | bytes 3145732
  60.9 4.8 %collective-permute-start.11 = (bf16[8,4,128,128]{3,2,1,0:T(8,128)(2,1)S(1)}, bf16[8,4,128,128]{3,2,1,0:T(8,128)(2,1)S(1)}, u32[]{:S(2)}, u32[]{:S(2)}) collective-permute-start(bf16[8,4,128,128]{3,2,1,0:T(8,128)(2,1)S(1)} %broadcast_select_fusion.3), channel_id=1, source_target_pairs={{0,4},{4,0},{1,5},{5,1},{2,6},{6,2},{3,7},{7,3},{8,12},{12,8},{9,1... | collective-permute-start | bytes 3145736 | tf_op jit(solution)/shard_map/ppermute | solution.py:14
  62.2 28.2 %copy-start.4 = (bf16[8,4,128,128]{3,2,1,0:T(8,128)(2,1)}, bf16[8,4,128,128]{3,2,1,0:T(8,128)(2,1)S(1)}, u32[]{:S(2)}) copy-start(bf16[8,4,128,128]{3,2,1,0:T(8,128)(2,1)S(1)} %broadcast_select_fusion.5.refs_6_) | copy-start | bytes 3145732
  62.2 25.6 %collective-permute-start.7 = (bf16[8,4,128,128]{3,2,1,0:T(8,128)(2,1)S(1)}, bf16[8,4,128,128]{3,2,1,0:T(8,128)(2,1)S(1)}, u32[]{:S(2)}, u32[]{:S(2)}) collective-permute-start(bf16[8,4,128,128]{3,2,1,0:T(8,128)(2,1)S(1)} %broadcast_select_fusion.5.refs_6_), channel_id=1, source_target_pairs={{0,8},{8,0},{16,24},{24,16},{1,9},{9,1},{17,25},{25,17},{2,10},{10... | collective-permute-start | bytes 3145736 | tf_op jit(solution)/shard_map/ppermute | solution.py:14
  62.8 27.4 %collective-permute-start.9 = (bf16[8,4,128,128]{3,2,1,0:T(8,128)(2,1)}, bf16[8,4,128,128]{3,2,1,0:T(8,128)(2,1)S(1)}, u32[]{:S(2)}, u32[]{:S(2)}) collective-permute-start(bf16[8,4,128,128]{3,2,1,0:T(8,128)(2,1)} %collective-permute-done.5), channel_id=1, source_target_pairs={{1,0},{2,3},{5,4},{6,7},{9,8},{10,11},{13,12},{14,15},{17,16},{18,... | collective-permute-start | bytes 3145736 | tf_op jit(solution)/shard_map/ppermute | solution.py:14
  64.1 26.1 %collective-permute-start.8 = (bf16[8,4,128,128]{3,2,1,0:T(8,128)(2,1)S(1)}, bf16[8,4,128,128]{3,2,1,0:T(8,128)(2,1)S(1)}, u32[]{:S(2)}, u32[]{:S(2)}) collective-permute-start(bf16[8,4,128,128]{3,2,1,0:T(8,128)(2,1)S(1)} %collective-permute-done.3.refs_13_), channel_id=1, source_target_pairs={{0,16},{16,0},{8,24},{24,8},{1,17},{17,1},{9,25},{25,9},{2,18},{18... | collective-permute-start | bytes 3145736 | tf_op jit(solution)/shard_map/ppermute | solution.py:14
  65.7 28.9 %collective-permute-start.14 = (bf16[8,4,128,128]{3,2,1,0:T(8,128)(2,1)}, bf16[8,4,128,128]{3,2,1,0:T(8,128)(2,1)S(1)}, u32[]{:S(2)}, u32[]{:S(2)}) collective-permute-start(bf16[8,4,128,128]{3,2,1,0:T(8,128)(2,1)} %collective-permute-done.1.refs_5_), channel_id=1, source_target_pairs={{0,4},{4,0},{1,5},{5,1},{2,6},{6,2},{3,7},{7,3},{8,12},{12,8},{9,1... | collective-permute-start | bytes 3145736 | tf_op jit(solution)/shard_map/ppermute | solution.py:14
  65.7 24.5 %copy-start.11 = (bf16[8,4,128,128]{3,2,1,0:T(8,128)(2,1)}, bf16[8,4,128,128]{3,2,1,0:T(8,128)(2,1)S(1)}, u32[]{:S(2)}) copy-start(bf16[8,4,128,128]{3,2,1,0:T(8,128)(2,1)S(1)} %collective-permute-done.11.refs_20_) | copy-start | bytes 3145732
  65.7 29.0 %collective-permute-start.15 = (bf16[8,4,128,128]{3,2,1,0:T(8,128)(2,1)S(1)}, bf16[8,4,128,128]{3,2,1,0:T(8,128)(2,1)S(1)}, u32[]{:S(2)}, u32[]{:S(2)}) collective-permute-start(bf16[8,4,128,128]{3,2,1,0:T(8,128)(2,1)S(1)} %broadcast_select_fusion.5.refs_6_), channel_id=1, source_target_pairs={{0,4},{4,0},{1,5},{5,1},{2,6},{6,2},{3,7},{7,3},{8,12},{12,8},{9,1... | collective-permute-start | bytes 3145736 | tf_op jit(solution)/shard_map/ppermute | solution.py:14
  87.9 30.5 %copy-start.5 = (bf16[8,4,128,128]{3,2,1,0:T(8,128)(2,1)}, bf16[8,4,128,128]{3,2,1,0:T(8,128)(2,1)S(1)}, u32[]{:S(2)}) copy-start(bf16[8,4,128,128]{3,2,1,0:T(8,128)(2,1)S(1)} %collective-permute-done.7.refs_14_) | copy-start | bytes 3145732
  90.3 1.1 copy-start.6
  91.3 3.3 %copy-start.7 = (bf16[8,4,128,128]{3,2,1,0:T(8,128)(2,1)}, bf16[8,4,128,128]{3,2,1,0:T(8,128)(2,1)S(1)}, u32[]{:S(2)}) copy-start(bf16[8,4,128,128]{3,2,1,0:T(8,128)(2,1)S(1)} %broadcast_select_fusion.4.refs_7_) | copy-start | bytes 3145732
  91.5 3.3 %collective-permute-start.16 = (bf16[8,4,128,128]{3,2,1,0:T(8,128)(2,1)S(1)}, bf16[8,4,128,128]{3,2,1,0:T(8,128)(2,1)S(1)}, u32[]{:S(2)}, u32[]{:S(2)}) collective-permute-start(bf16[8,4,128,128]{3,2,1,0:T(8,128)(2,1)S(1)} %broadcast_select_fusion.2), channel_id=1, source_target_pairs={{0,4},{4,0},{1,5},{5,1},{2,6},{6,2},{3,7},{7,3},{8,12},{12,8},{9,1... | collective-permute-start | bytes 3145736 | tf_op jit(solution)/shard_map/ppermute | solution.py:14
  91.5 25.6 %collective-permute-start.12 = (bf16[8,4,128,128]{3,2,1,0:T(8,128)(2,1)S(1)}, bf16[8,4,128,128]{3,2,1,0:T(8,128)(2,1)S(1)}, u32[]{:S(2)}, u32[]{:S(2)}) collective-permute-start(bf16[8,4,128,128]{3,2,1,0:T(8,128)(2,1)S(1)} %broadcast_select_fusion.4.refs_7_), channel_id=1, source_target_pairs={{0,8},{8,0},{16,24},{24,16},{1,9},{9,1},{17,25},{25,17},{2,10},{10... | collective-permute-start | bytes 3145736 | tf_op jit(solution)/shard_map/ppermute | solution.py:14
  93.1 25.2 %collective-permute-start.13 = (bf16[8,4,128,128]{3,2,1,0:T(8,128)(2,1)S(1)}, bf16[8,4,128,128]{3,2,1,0:T(8,128)(2,1)S(1)}, u32[]{:S(2)}, u32[]{:S(2)}) collective-permute-start(bf16[8,4,128,128]{3,2,1,0:T(8,128)(2,1)S(1)} %collective-permute-done.7.refs_14_), channel_id=1, source_target_pairs={{0,16},{16,0},{8,24},{24,8},{1,17},{17,1},{9,25},{25,9},{2,18},{18... | collective-permute-start | bytes 3145736 | tf_op jit(solution)/shard_map/ppermute | solution.py:14
  94.6 23.8 %copy-start.12 = (bf16[8,4,128,128]{3,2,1,0:T(8,128)(2,1)}, bf16[8,4,128,128]{3,2,1,0:T(8,128)(2,1)S(1)}, u32[]{:S(2)}) copy-start(bf16[8,4,128,128]{3,2,1,0:T(8,128)(2,1)S(1)} %collective-permute-done.14.refs_9_) | copy-start | bytes 3145732
  94.6 26.2 %collective-permute-start.18 = (bf16[8,4,128,128]{3,2,1,0:T(8,128)(2,1)S(1)}, bf16[8,4,128,128]{3,2,1,0:T(8,128)(2,1)S(1)}, u32[]{:S(2)}, u32[]{:S(2)}) collective-permute-start(bf16[8,4,128,128]{3,2,1,0:T(8,128)(2,1)S(1)} %broadcast_select_fusion.4.refs_7_), channel_id=1, source_target_pairs={{0,4},{4,0},{1,5},{5,1},{2,6},{6,2},{3,7},{7,3},{8,12},{12,8},{9,1... | collective-permute-start | bytes 3145736 | tf_op jit(solution)/shard_map/ppermute | solution.py:14
  94.7 51.2 %copy-start.13 = (bf16[8,4,128,128]{3,2,1,0:T(8,128)(2,1)}, bf16[8,4,128,128]{3,2,1,0:T(8,128)(2,1)S(1)}, u32[]{:S(2)}) copy-start(bf16[8,4,128,128]{3,2,1,0:T(8,128)(2,1)S(1)} %collective-permute-done.15.refs_10_) | copy-start | bytes 3145732
  94.7 53.8 %copy-start.14 = (bf16[8,4,128,128]{3,2,1,0:T(8,128)(2,1)}, bf16[8,4,128,128]{3,2,1,0:T(8,128)(2,1)S(1)}, u32[]{:S(2)}) copy-start(bf16[8,4,128,128]{3,2,1,0:T(8,128)(2,1)S(1)} %collective-permute-done.16.refs_21_) | copy-start | bytes 3145732
  117.1 27.8 %copy-start.8 = (bf16[8,4,128,128]{3,2,1,0:T(8,128)(2,1)}, bf16[8,4,128,128]{3,2,1,0:T(8,128)(2,1)S(1)}, u32[]{:S(2)}) copy-start(bf16[8,4,128,128]{3,2,1,0:T(8,128)(2,1)S(1)} %collective-permute-done.12.refs_15_) | copy-start | bytes 3145732
  118.3 1.0 copy-start.9
  119.3 2.7 %collective-permute-start.19 = (bf16[8,4,128,128]{3,2,1,0:T(8,128)(2,1)S(1)}, bf16[8,4,128,128]{3,2,1,0:T(8,128)(2,1)S(1)}, u32[]{:S(2)}, u32[]{:S(2)}) collective-permute-start(bf16[8,4,128,128]{3,2,1,0:T(8,128)(2,1)S(1)} %broadcast_select_fusion.1), channel_id=1, source_target_pairs={{0,4},{4,0},{1,5},{5,1},{2,6},{6,2},{3,7},{7,3},{8,12},{12,8},{9,1... | collective-permute-start | bytes 3145736 | tf_op jit(solution)/shard_map/ppermute | solution.py:14
  119.3 25.6 %collective-permute-start.17 = (bf16[8,4,128,128]{3,2,1,0:T(8,128)(2,1)S(1)}, bf16[8,4,128,128]{3,2,1,0:T(8,128)(2,1)S(1)}, u32[]{:S(2)}, u32[]{:S(2)}) collective-permute-start(bf16[8,4,128,128]{3,2,1,0:T(8,128)(2,1)S(1)} %collective-permute-done.12.refs_15_), channel_id=1, source_target_pairs={{0,16},{16,0},{8,24},{24,8},{1,17},{17,1},{9,25},{25,9},{2,18},{18... | collective-permute-start | bytes 3145736 | tf_op jit(solution)/shard_map/ppermute | solution.py:14
  120.8 24.2 %copy-start.15 = (bf16[8,4,128,128]{3,2,1,0:T(8,128)(2,1)}, bf16[8,4,128,128]{3,2,1,0:T(8,128)(2,1)S(1)}, u32[]{:S(2)}) copy-start(bf16[8,4,128,128]{3,2,1,0:T(8,128)(2,1)S(1)} %collective-permute-done.18.refs_11_) | copy-start | bytes 3145732
  122.0 23.0 %copy-start.16 = (bf16[8,4,128,128]{3,2,1,0:T(8,128)(2,1)}, bf16[8,4,128,128]{3,2,1,0:T(8,128)(2,1)S(1)}, u32[]{:S(2)}) copy-start(bf16[8,4,128,128]{3,2,1,0:T(8,128)(2,1)S(1)} %collective-permute-done.19.refs_22_) | copy-start | bytes 3145732
  144.9 1.0 copy-start.10
  145.9 2.7 %collective-permute-start.20 = (bf16[8,4,128,128]{3,2,1,0:T(8,128)(2,1)S(1)}, bf16[8,4,128,128]{3,2,1,0:T(8,128)(2,1)S(1)}, u32[]{:S(2)}, u32[]{:S(2)}) collective-permute-start(bf16[8,4,128,128]{3,2,1,0:T(8,128)(2,1)S(1)} %broadcast_select_fusion), channel_id=1, source_target_pairs={{0,4},{4,0},{1,5},{5,1},{2,6},{6,2},{3,7},{7,3},{8,12},{12,8},{9,1... | collective-permute-start | bytes 3145736 | tf_op jit(solution)/shard_map/ppermute | solution.py:14
  148.5 1.0 copy-start.17

commit v3 on v2

--- a/solution.py
+++ b/solution.py
@@ -18,13 +18,10 @@
 
 
 def line_window(own, extra):
-    me = lax.axis_index("depth")
-    core = lax.axis_index("col")
-    even = lax.axis_index("row") % 2 == 0
-    at_end = jnp.logical_or(me == 0, me == 3)
-    ends = [(0, 1), (1, 0), (2, 3), (3, 2)]
-    middle = [(1, 2), (2, 1)]
-    outward = [(1, 0), (2, 3)]
+    send_x = (lax.axis_index("col") == 0) == (lax.axis_index("row") % 2 == 0)
+
+    def along_z(value):
+        return permuted(value, "depth", [(0, 1), (1, 2), (2, 3), (3, 0)])
 
     def along_x(value):
         return permuted(value, "row", [(0, 1), (1, 0), (2, 3), (3, 2)])
@@ -35,44 +32,19 @@
     def over_core(value):
         return permuted(value, "col", [(0, 1), (1, 0)])
 
-    send_x = (core == 0) == even
-
     def shared(by_x, by_y):
         return over_core(jnp.where(send_x, by_x, by_y))
 
-    x0 = along_x(own)
-    p1 = permuted(own, "depth", ends)
-    across = permuted(own, "depth", middle)
-    x0, p1, across = together((x0, p1, across))
-
-    x1 = along_x(p1)
-    y0 = along_y(x0)
-    across_outer = permuted(p1, "depth", middle)
-    out = permuted(across, "depth", outward)
-    extra, x1, y0, across_outer, out = together((extra, x1, y0, across_outer, out))
-
-    p2 = jnp.where(at_end, out, across)
-    x2 = along_x(p2)
-    y1 = along_y(x1)
-    out_outer = permuted(across_outer, "depth", outward)
-    c0 = over_core(own)
-    s0 = shared(x0, y0)
-    x2, y1, out_outer, c0, s0 = together((x2, y1, out_outer, c0, s0))
-
-    p3 = jnp.where(at_end, out_outer, across_outer)
-    x3 = along_x(p3)
-    y2 = along_y(x2)
-    c1 = over_core(p1)
-    c2 = over_core(p2)
-    s1 = shared(x1, y1)
-    x3, y2, c1, c2, s1 = together((x3, y2, c1, c2, s1))
-
-    y3 = along_y(x3)
-    c3 = over_core(p3)
-    s2 = shared(x2, y2)
-    y3, c3, s2 = together((y3, c3, s2))
+    x0, p1, c0 = together((along_x(own), along_z(own), over_core(own)))
+    extra, x1, y0, p2 = together((extra, along_x(p1), along_y(x0), along_z(p1)))
+    x2, y1, p3, c1, s0 = together(
+        (along_x(p2), along_y(x1), along_z(p2), over_core(p1), shared(x0, y0))
+    )
+    x3, y2, c2, c3, s1 = together(
+        (along_x(p3), along_y(x2), over_core(p2), over_core(p3), shared(x1, y1))
+    )
+    y3, s2 = together((along_y(x3), shared(x2, y2)))
     s3 = shared(x3, y3)
-
     groups = [
         [own, p1, p2, p3],
         [c0, c1, c2, c3],
@@ -214,14 +186,13 @@
 
 
 def window_places(place, depth):
-    if window_plan() is line_window:
-        low = depth < 2
-        owners = [depth, depth ^ 1, jnp.where(low, 2, 1), jnp.where(low, 3, 0)]
-        beside = jnp.where(lax.axis_index("col") == 0, 1, -1)
-        over = jnp.where(lax.axis_index("row") % 2 == 0, 2, -2)
-        return owners, [0, beside, over, -over, -beside]
     depths = lax.axis_size("depth")
-    return [(depth - step) % depths for step in range(depths)], [0, 1, -1, 2, -2]
+    owners = [(depth - step) % depths for step in range(depths)]
+    if window_plan() is not line_window:
+        return owners, [0, 1, -1, 2, -2]
+    beside = jnp.where(lax.axis_index("col") == 0, 1, -1)
+    over = jnp.where(lax.axis_index("row") % 2 == 0, 2, -2)
+    return owners, [0, beside, over, -over, -beside]
 
 
 def local(blocks, block_cols, product_cols):
@@ -272,7 +243,7 @@
             pltpu.VMEM((rows * (window + 2 * REACH), edge, edge), jnp.bfloat16),
             pltpu.SemaphoreType.DMA,
         ],
-        compiler_params=pltpu.CompilerParams(vmem_limit_bytes=56 * 2**20),
+        compiler_params=pltpu.CompilerParams(vmem_limit_bytes=42 * 2**20),
         name="purify",
     )(*tables, *flat)
 

time: 182 us -> 190 us (1.044)
  Pallas kernels: 31.9 us -> 46.1 us
  starting transfers between devices: 22.9 us -> 17.4 us
  waiting for transfers between devices: 110 us -> 114 us
  other arithmetic: 4.24 us -> 1.65 us
  local copies, waits for them, and re-layouts: 12.1 us -> 10.2 us
    pallas_call x1, Pallas kernels: 31.9 us -> 46.1 us  [local(): pl.pallas_call(kernel_body, out_shape=jax.ShapeDtypeStruct((rows, out_slo...]
    ppermute x21 -> x19, starting transfers between devices: 22.9 us -> 17.4 us  [permuted(): return lax.ppermute(value, axes, pairs)]
    ppermute x21 -> x19, waiting for transfers between devices: 110 us -> 114 us  [permuted(): return lax.ppermute(value, axes, pairs)]
    unnamed x37 -> x25, local copies, waits for them, and re-layouts: 5.28 us -> 4.51 us
  transfers between devices with their start and end apart: 21 -> 19, of which waited for: 10 -> 11; matrix products, arithmetic and copies ran while one was open for 6% -> 4% of each run, Pallas kernels for 0% -> 0%
where the time goes in v3:
time: 190 us
  waiting for transfers between devices  114 us (60%)
  Pallas kernels  46.1 us (24%)
  starting transfers between devices  17.4 us (9%)
  local copies, waits for them, and re-layouts  10.2 us (5%)
    ppermute x19, waiting for transfers between devices, permuted(): return lax.ppermute(value, axes, pairs)  114 us
    pallas_call x1, Pallas kernels, local(): pl.pallas_call(kernel_body, out_shape=jax.ShapeDtypeStruct((rows, out_slo...  46.1 us
    ppermute x19, starting transfers between devices, permuted(): return lax.ppermute(value, axes, pairs)  17.4 us
    gather x1, local copies, waits for them, and re-layouts, local(): block_cols[row_ids[:, None, :, None] % order, slot_ids[None, :, None, :]]  4.57 us
    unnamed x25, local copies, waits for them, and re-layouts  4.51 us
  transfers between devices with their start and end apart: 19, of which 11 were waited for; matrix products, arithmetic and copies ran while one was open for 4% of the time, Pallas kernels for 0%

profile of v3, /device:TPU:0, one launch (start us, length us, event | category | flops | bytes accessed | tf_op | source)
XLA Modules:
  0.0 190.1 jit_solution(14549832667615965578)
XLA Ops:
  0.0 3.0 %collective-permute-start.1 = (bf16[8,4,128,128]{3,2,1,0:T(8,128)(2,1)}, bf16[8,4,128,128]{3,2,1,0:T(8,128)(2,1)S(1)}, u32[]{:S(2)}, u32[]{:S(2)}) collective-permute-start(bf16[8,4,128,128]{3,2,1,0:T(8,128)(2,1)} %refs_4_.1), channel_id=1, source_target_pairs={{0,1},{1,2},{2,3},{3,0},{4,5},{5,6},{6,7},{7,4},{8,9},{9,10},{10,1... | collective-permute-start | bytes 3145736 | tf_op jit(solution)/shard_map/ppermute | solution.py:14
  3.0 1.5 collective-permute-start
  4.5 0.0 collective-permute-start.2
  4.5 0.7 add_select_fusion.1
  5.2 0.1 constant_dynamic-slice_fusion
  5.3 0.1 reshape.222.refs_3_
  5.4 0.1 fusion
  5.5 0.1 reshape.223.refs_2_
  5.6 0.8 copy.6
  6.5 21.9 %collective-permute-done.1.refs_5_ = bf16[8,4,128,128]{3,2,1,0:T(8,128)(2,1)S(1)} collective-permute-done((bf16[8,4,128,128]{3,2,1,0:T(8,128)(2,1)}, bf16[8,4,128,128]{3,2,1,0:T(8,128)(2,1)S(1)}, u32[]{:S(2)}, u32[]{:S(2)}) %collective-permute-start.1) | collective-permute-done | bytes 1048608 | tf_op jit(solution)/shard_map/ppermute | solution.py:14
  28.4 0.0 collective-permute-done.refs_12_
  28.4 0.0 collective-permute-done.2.refs_8_
  28.4 1.0 copy-done.1
  29.4 1.0 collective-permute-start.5
  30.4 1.5 collective-permute-start.3
  31.9 1.5 collective-permute-start.4
  33.4 0.1 broadcast_or_fusion
  33.5 0.1 reshape.224
  33.6 0.0 copy-done.3
  33.6 4.6 %gather_fusion = s32[640]{0:T(1024)S(1)} fusion(s32[64,16]{0,1:T(8,128)S(1)} %copy-done.3, s32[640]{0:T(1024)S(1)} %reshape.224), kind=kCustom, calls=%fused_computation | custom fusion | bytes 10240 | tf_op jit(solution)/shard_map/gather | solution.py:212
  38.2 0.1 add.343
  38.3 0.1 add.344
  38.4 0.6 gather_fusion.1
  39.0 0.2 fusion.2
  39.2 0.1 collective-permute-start.9
  39.3 15.8 %collective-permute-done.4.refs_16_ = bf16[8,4,128,128]{3,2,1,0:T(8,128)(2,1)} collective-permute-done((bf16[8,4,128,128]{3,2,1,0:T(8,128)(2,1)S(1)}, bf16[8,4,128,128]{3,2,1,0:T(8,128)(2,1)}, u32[]{:S(2)}, u32[]{:S(2)}) %collective-permute-start.4) | collective-permute-done | bytes 1048608 | tf_op jit(solution)/shard_map/ppermute | solution.py:14
  55.2 0.5 collective-permute-done.5.refs_6_
  55.6 0.0 collective-permute-done.3.refs_13_
  55.6 0.1 broadcast_select_fusion.3
  55.8 0.1 collective-permute-start.10
  55.8 1.3 collective-permute-start.7
  57.2 1.3 collective-permute-start.8
  58.5 1.8 collective-permute-start.6
  60.3 0.0 collective-permute-done.9.refs_9_
  60.3 0.0 collective-permute-start.13
  60.3 0.0 collective-permute-done.10.refs_20_
  60.3 0.0 copy-start.8
  60.3 21.1 %collective-permute-done.7.refs_17_ = bf16[8,4,128,128]{3,2,1,0:T(8,128)(2,1)S(1)} collective-permute-done((bf16[8,4,128,128]{3,2,1,0:T(8,128)(2,1)S(1)}, bf16[8,4,128,128]{3,2,1,0:T(8,128)(2,1)S(1)}, u32[]{:S(2)}, u32[]{:S(2)}) %collective-permute-start.7) | collective-permute-done | bytes 1048608 | tf_op jit(solution)/shard_map/ppermute | solution.py:14
  81.4 3.0 %collective-permute-done.8.refs_7_ = bf16[8,4,128,128]{3,2,1,0:T(8,128)(2,1)S(1)} collective-permute-done((bf16[8,4,128,128]{3,2,1,0:T(8,128)(2,1)}, bf16[8,4,128,128]{3,2,1,0:T(8,128)(2,1)S(1)}, u32[]{:S(2)}, u32[]{:S(2)}) %collective-permute-start.8) | collective-permute-done | bytes 1048608 | tf_op jit(solution)/shard_map/ppermute | solution.py:14
  84.4 0.0 collective-permute-done.6.refs_14_
  84.4 0.1 broadcast_select_fusion.2
  84.6 0.1 collective-permute-start.15
  84.6 0.5 collective-permute-start.14
  85.1 2.7 %collective-permute-start.11 = (bf16[8,4,128,128]{3,2,1,0:T(8,128)(2,1)S(1)}, bf16[8,4,128,128]{3,2,1,0:T(8,128)(2,1)S(1)}, u32[]{:S(2)}, u32[]{:S(2)}) collective-permute-start(bf16[8,4,128,128]{3,2,1,0:T(8,128)(2,1)S(1)} %collective-permute-done.8.refs_7_), channel_id=1, source_target_pairs={{0,8},{8,0},{16,24},{24,16},{1,9},{9,1},{17,25},{25,17},{2,10},{10... | collective-permute-start | bytes 3145736 | tf_op jit(solution)/shard_map/ppermute | solution.py:14
  87.9 0.5 collective-permute-start.12
  88.4 0.0 collective-permute-done.13.refs_10_
  88.4 0.0 collective-permute-done.15.refs_21_
  88.4 0.4 collective-permute-done.14.refs_11_
  88.8 22.5 %collective-permute-done.11.refs_15_ = bf16[8,4,128,128]{3,2,1,0:T(8,128)(2,1)S(1)} collective-permute-done((bf16[8,4,128,128]{3,2,1,0:T(8,128)(2,1)S(1)}, bf16[8,4,128,128]{3,2,1,0:T(8,128)(2,1)S(1)}, u32[]{:S(2)}, u32[]{:S(2)}) %collective-permute-start.11) | collective-permute-done | bytes 1048608 | tf_op jit(solution)/shard_map/ppermute | solution.py:14
  111.3 1.5 collective-permute-done.12.refs_18_
  112.7 0.1 broadcast_select_fusion.1
  112.8 0.9 copy-done.6
  113.7 0.0 collective-permute-start.17
  113.7 0.5 collective-permute-start.16
  114.2 2.2 %collective-permute-done.17.refs_22_ = bf16[8,4,128,128]{3,2,1,0:T(8,128)(2,1)S(1)} collective-permute-done((bf16[8,4,128,128]{3,2,1,0:T(8,128)(2,1)S(1)}, bf16[8,4,128,128]{3,2,1,0:T(8,128)(2,1)S(1)}, u32[]{:S(2)}, u32[]{:S(2)}) %collective-permute-start.17) | collective-permute-done | bytes 1048608 | tf_op jit(solution)/shard_map/ppermute | solution.py:14
  116.4 22.9 %collective-permute-done.16.refs_19_ = bf16[8,4,128,128]{3,2,1,0:T(8,128)(2,1)S(1)} collective-permute-done((bf16[8,4,128,128]{3,2,1,0:T(8,128)(2,1)S(1)}, bf16[8,4,128,128]{3,2,1,0:T(8,128)(2,1)S(1)}, u32[]{:S(2)}, u32[]{:S(2)}) %collective-permute-start.16) | collective-permute-done | bytes 1048608 | tf_op jit(solution)/shard_map/ppermute | solution.py:14
  139.3 0.1 broadcast_select_fusion
  139.4 0.0 copy-done.10
  139.4 0.9 copy-done.7
  140.3 0.0 collective-permute-start.18
  140.3 2.7 %collective-permute-done.18.refs_23_ = bf16[8,4,128,128]{3,2,1,0:T(8,128)(2,1)S(1)} collective-permute-done((bf16[8,4,128,128]{3,2,1,0:T(8,128)(2,1)S(1)}, bf16[8,4,128,128]{3,2,1,0:T(8,128)(2,1)S(1)}, u32[]{:S(2)}, u32[]{:S(2)}) %collective-permute-start.18) | collective-permute-done | bytes 1048608 | tf_op jit(solution)/shard_map/ppermute | solution.py:14
  142.9 1.0 copy-done.11
  143.9 0.0 copy-done.2
  143.9 46.1 %purify.1 = bf16[8,6,128,128]{3,2,1,0:T(8,128)(2,1)} custom-call(s32[640]{0:T(1024)S(1)} %fusion.11.refs_0_, s32[40]{0:T(128)S(1)} %compare_select_fusion.6.refs_1_, s32[320]{0:T(512)S(1)} %reshape.223.refs_2_, s32[48]{0:T(128)S(1)} %reshape.222.refs_3_, bf16[8,4,128,128]{3,2,1,0:T(8,128)(2,1)S(1)} %copy-done, ...), custom_call_target="tpu_custom_call" | custom-call | tf_op jit(solution)/shard_map/purify/pallas_call | solution.py:236
  (30 shorter events, 0.2 us)
Async XLA Ops:
  0.0 33.6 %copy-start.3 = (s32[64,16]{0,1:T(8,128)S(1)}, s32[64,16]{0,1:T(8,128)}, u32[]{:S(2)}) copy-start(s32[64,16]{0,1:T(8,128)} %param.4) | copy-start | bytes 12292
  0.0 28.4 %collective-permute-start.1 = (bf16[8,4,128,128]{3,2,1,0:T(8,128)(2,1)}, bf16[8,4,128,128]{3,2,1,0:T(8,128)(2,1)S(1)}, u32[]{:S(2)}, u32[]{:S(2)}) collective-permute-start(bf16[8,4,128,128]{3,2,1,0:T(8,128)(2,1)} %refs_4_.1), channel_id=1, source_target_pairs={{0,1},{1,2},{2,3},{3,0},{4,5},{5,6},{6,7},{7,4},{8,9},{9,10},{10,1... | collective-permute-start | bytes 3145736 | tf_op jit(solution)/shard_map/ppermute | solution.py:14
  3.0 25.4 %collective-permute-start = (bf16[8,4,128,128]{3,2,1,0:T(8,128)(2,1)}, bf16[8,4,128,128]{3,2,1,0:T(8,128)(2,1)S(1)}, u32[]{:S(2)}, u32[]{:S(2)}) collective-permute-start(bf16[8,4,128,128]{3,2,1,0:T(8,128)(2,1)} %refs_4_.1), channel_id=1, source_target_pairs={{0,8},{8,0},{16,24},{24,16},{1,9},{9,1},{17,25},{25,17},{2,10},{10... | collective-permute-start | bytes 3145736 | tf_op jit(solution)/shard_map/ppermute | solution.py:14
  4.5 23.9 %collective-permute-start.2 = (bf16[8,4,128,128]{3,2,1,0:T(8,128)(2,1)}, bf16[8,4,128,128]{3,2,1,0:T(8,128)(2,1)S(1)}, u32[]{:S(2)}, u32[]{:S(2)}) collective-permute-start(bf16[8,4,128,128]{3,2,1,0:T(8,128)(2,1)} %refs_4_.1), channel_id=1, source_target_pairs={{0,4},{4,0},{1,5},{5,1},{2,6},{6,2},{3,7},{7,3},{8,12},{12,8},{9,1... | collective-permute-start | bytes 3145736 | tf_op jit(solution)/shard_map/ppermute | solution.py:14
  28.4 1.0 copy-start.1
  29.4 26.2 %collective-permute-start.5 = (bf16[8,4,128,128]{3,2,1,0:T(8,128)(2,1)S(1)}, bf16[8,4,128,128]{3,2,1,0:T(8,128)(2,1)}, u32[]{:S(2)}, u32[]{:S(2)}) collective-permute-start(bf16[8,4,128,128]{3,2,1,0:T(8,128)(2,1)S(1)} %collective-permute-done.1.refs_5_), channel_id=1, source_target_pairs={{0,1},{1,2},{2,3},{3,0},{4,5},{5,6},{6,7},{7,4},{8,9},{9,10},{10,1... | collective-permute-start | bytes 3145736 | tf_op jit(solution)/shard_map/ppermute | solution.py:14
  30.4 25.2 %collective-permute-start.3 = (bf16[8,4,128,128]{3,2,1,0:T(8,128)(2,1)S(1)}, bf16[8,4,128,128]{3,2,1,0:T(8,128)(2,1)S(1)}, u32[]{:S(2)}, u32[]{:S(2)}) collective-permute-start(bf16[8,4,128,128]{3,2,1,0:T(8,128)(2,1)S(1)} %collective-permute-done.1.refs_5_), channel_id=1, source_target_pairs={{0,8},{8,0},{16,24},{24,16},{1,9},{9,1},{17,25},{25,17},{2,10},{10... | collective-permute-start | bytes 3145736 | tf_op jit(solution)/shard_map/ppermute | solution.py:14
  31.9 23.3 %collective-permute-start.4 = (bf16[8,4,128,128]{3,2,1,0:T(8,128)(2,1)S(1)}, bf16[8,4,128,128]{3,2,1,0:T(8,128)(2,1)}, u32[]{:S(2)}, u32[]{:S(2)}) collective-permute-start(bf16[8,4,128,128]{3,2,1,0:T(8,128)(2,1)S(1)} %collective-permute-done.refs_12_), channel_id=1, source_target_pairs={{0,16},{16,0},{8,24},{24,8},{1,17},{17,1},{9,25},{25,9},{2,18},{18... | collective-permute-start | bytes 3145736 | tf_op jit(solution)/shard_map/ppermute | solution.py:14
  39.2 21.0 %collective-permute-start.9 = (bf16[8,4,128,128]{3,2,1,0:T(8,128)(2,1)S(1)}, bf16[8,4,128,128]{3,2,1,0:T(8,128)(2,1)S(1)}, u32[]{:S(2)}, u32[]{:S(2)}) collective-permute-start(bf16[8,4,128,128]{3,2,1,0:T(8,128)(2,1)S(1)} %collective-permute-done.1.refs_5_), channel_id=1, source_target_pairs={{0,4},{4,0},{1,5},{5,1},{2,6},{6,2},{3,7},{7,3},{8,12},{12,8},{9,1... | collective-permute-start | bytes 3145736 | tf_op jit(solution)/shard_map/ppermute | solution.py:14
  55.8 4.5 %collective-permute-start.10 = (bf16[8,4,128,128]{3,2,1,0:T(8,128)(2,1)S(1)}, bf16[8,4,128,128]{3,2,1,0:T(8,128)(2,1)S(1)}, u32[]{:S(2)}, u32[]{:S(2)}) collective-permute-start(bf16[8,4,128,128]{3,2,1,0:T(8,128)(2,1)S(1)} %broadcast_select_fusion.3), channel_id=1, source_target_pairs={{0,4},{4,0},{1,5},{5,1},{2,6},{6,2},{3,7},{7,3},{8,12},{12,8},{9,1... | collective-permute-start | bytes 3145736 | tf_op jit(solution)/shard_map/ppermute | solution.py:14
  55.8 25.6 %collective-permute-start.7 = (bf16[8,4,128,128]{3,2,1,0:T(8,128)(2,1)S(1)}, bf16[8,4,128,128]{3,2,1,0:T(8,128)(2,1)S(1)}, u32[]{:S(2)}, u32[]{:S(2)}) collective-permute-start(bf16[8,4,128,128]{3,2,1,0:T(8,128)(2,1)S(1)} %collective-permute-done.3.refs_13_), channel_id=1, source_target_pairs={{0,16},{16,0},{8,24},{24,8},{1,17},{17,1},{9,25},{25,9},{2,18},{18... | collective-permute-start | bytes 3145736 | tf_op jit(solution)/shard_map/ppermute | solution.py:14
  57.2 27.2 %collective-permute-start.8 = (bf16[8,4,128,128]{3,2,1,0:T(8,128)(2,1)}, bf16[8,4,128,128]{3,2,1,0:T(8,128)(2,1)S(1)}, u32[]{:S(2)}, u32[]{:S(2)}) collective-permute-start(bf16[8,4,128,128]{3,2,1,0:T(8,128)(2,1)} %collective-permute-done.5.refs_6_), channel_id=1, source_target_pairs={{0,1},{1,2},{2,3},{3,0},{4,5},{5,6},{6,7},{7,4},{8,9},{9,10},{10,1... | collective-permute-start | bytes 3145736 | tf_op jit(solution)/shard_map/ppermute | solution.py:14
  58.5 25.9 %collective-permute-start.6 = (bf16[8,4,128,128]{3,2,1,0:T(8,128)(2,1)}, bf16[8,4,128,128]{3,2,1,0:T(8,128)(2,1)S(1)}, u32[]{:S(2)}, u32[]{:S(2)}) collective-permute-start(bf16[8,4,128,128]{3,2,1,0:T(8,128)(2,1)} %collective-permute-done.5.refs_6_), channel_id=1, source_target_pairs={{0,8},{8,0},{16,24},{24,16},{1,9},{9,1},{17,25},{25,17},{2,10},{10... | collective-permute-start | bytes 3145736 | tf_op jit(solution)/shard_map/ppermute | solution.py:14
  60.3 28.1 %collective-permute-start.13 = (bf16[8,4,128,128]{3,2,1,0:T(8,128)(2,1)}, bf16[8,4,128,128]{3,2,1,0:T(8,128)(2,1)S(1)}, u32[]{:S(2)}, u32[]{:S(2)}) collective-permute-start(bf16[8,4,128,128]{3,2,1,0:T(8,128)(2,1)} %collective-permute-done.5.refs_6_), channel_id=1, source_target_pairs={{0,4},{4,0},{1,5},{5,1},{2,6},{6,2},{3,7},{7,3},{8,12},{12,8},{9,1... | collective-permute-start | bytes 3145736 | tf_op jit(solution)/shard_map/ppermute | solution.py:14
  60.3 24.3 %copy-start.8 = (bf16[8,4,128,128]{3,2,1,0:T(8,128)(2,1)}, bf16[8,4,128,128]{3,2,1,0:T(8,128)(2,1)S(1)}, u32[]{:S(2)}) copy-start(bf16[8,4,128,128]{3,2,1,0:T(8,128)(2,1)S(1)} %collective-permute-done.10.refs_20_) | copy-start | bytes 3145732
  81.4 3.1 %copy-start.4 = (bf16[8,4,128,128]{3,2,1,0:T(8,128)(2,1)}, bf16[8,4,128,128]{3,2,1,0:T(8,128)(2,1)S(1)}, u32[]{:S(2)}) copy-start(bf16[8,4,128,128]{3,2,1,0:T(8,128)(2,1)S(1)} %collective-permute-done.7.refs_17_) | copy-start | bytes 3145732
  84.6 3.8 %collective-permute-start.15 = (bf16[8,4,128,128]{3,2,1,0:T(8,128)(2,1)S(1)}, bf16[8,4,128,128]{3,2,1,0:T(8,128)(2,1)S(1)}, u32[]{:S(2)}, u32[]{:S(2)}) collective-permute-start(bf16[8,4,128,128]{3,2,1,0:T(8,128)(2,1)S(1)} %broadcast_select_fusion.2), channel_id=1, source_target_pairs={{0,4},{4,0},{1,5},{5,1},{2,6},{6,2},{3,7},{7,3},{8,12},{12,8},{9,1... | collective-permute-start | bytes 3145736 | tf_op jit(solution)/shard_map/ppermute | solution.py:14
  84.6 4.1 %collective-permute-start.14 = (bf16[8,4,128,128]{3,2,1,0:T(8,128)(2,1)S(1)}, bf16[8,4,128,128]{3,2,1,0:T(8,128)(2,1)S(1)}, u32[]{:S(2)}, u32[]{:S(2)}) collective-permute-start(bf16[8,4,128,128]{3,2,1,0:T(8,128)(2,1)S(1)} %collective-permute-done.8.refs_7_), channel_id=1, source_target_pairs={{0,4},{4,0},{1,5},{5,1},{2,6},{6,2},{3,7},{7,3},{8,12},{12,8},{9,1... | collective-permute-start | bytes 3145736 | tf_op jit(solution)/shard_map/ppermute | solution.py:14
  85.1 26.1 %collective-permute-start.11 = (bf16[8,4,128,128]{3,2,1,0:T(8,128)(2,1)S(1)}, bf16[8,4,128,128]{3,2,1,0:T(8,128)(2,1)S(1)}, u32[]{:S(2)}, u32[]{:S(2)}) collective-permute-start(bf16[8,4,128,128]{3,2,1,0:T(8,128)(2,1)S(1)} %collective-permute-done.8.refs_7_), channel_id=1, source_target_pairs={{0,8},{8,0},{16,24},{24,16},{1,9},{9,1},{17,25},{25,17},{2,10},{10... | collective-permute-start | bytes 3145736 | tf_op jit(solution)/shard_map/ppermute | solution.py:14
  87.9 24.9 %collective-permute-start.12 = (bf16[8,4,128,128]{3,2,1,0:T(8,128)(2,1)S(1)}, bf16[8,4,128,128]{3,2,1,0:T(8,128)(2,1)S(1)}, u32[]{:S(2)}, u32[]{:S(2)}) collective-permute-start(bf16[8,4,128,128]{3,2,1,0:T(8,128)(2,1)S(1)} %collective-permute-done.6.refs_14_), channel_id=1, source_target_pairs={{0,16},{16,0},{8,24},{24,8},{1,17},{17,1},{9,25},{25,9},{2,18},{18... | collective-permute-start | bytes 3145736 | tf_op jit(solution)/shard_map/ppermute | solution.py:14
  88.4 24.5 %copy-start.9 = (bf16[8,4,128,128]{3,2,1,0:T(8,128)(2,1)}, bf16[8,4,128,128]{3,2,1,0:T(8,128)(2,1)S(1)}, u32[]{:S(2)}) copy-start(bf16[8,4,128,128]{3,2,1,0:T(8,128)(2,1)S(1)} %collective-permute-done.15.refs_21_) | copy-start | bytes 3145732
  111.3 28.1 %copy-start.5 = (bf16[8,4,128,128]{3,2,1,0:T(8,128)(2,1)}, bf16[8,4,128,128]{3,2,1,0:T(8,128)(2,1)S(1)}, u32[]{:S(2)}) copy-start(bf16[8,4,128,128]{3,2,1,0:T(8,128)(2,1)S(1)} %collective-permute-done.11.refs_15_) | copy-start | bytes 3145732
  112.7 1.0 copy-start.6
  113.7 30.2 %copy-start = (bf16[8,4,128,128]{3,2,1,0:T(8,128)(2,1)S(1)}, bf16[8,4,128,128]{3,2,1,0:T(8,128)(2,1)}, u32[]{:S(2)}) copy-start(bf16[8,4,128,128]{3,2,1,0:T(8,128)(2,1)} %refs_4_.1) | copy-start | bytes 3145732
  113.7 30.2 %copy-start.2 = (bf16[8,4,128,128]{3,2,1,0:T(8,128)(2,1)S(1)}, bf16[8,4,128,128]{3,2,1,0:T(8,128)(2,1)}, u32[]{:S(2)}) copy-start(bf16[8,4,128,128]{3,2,1,0:T(8,128)(2,1)} %copy-done.1) | copy-start | bytes 3145732
  113.7 2.7 %collective-permute-start.17 = (bf16[8,4,128,128]{3,2,1,0:T(8,128)(2,1)S(1)}, bf16[8,4,128,128]{3,2,1,0:T(8,128)(2,1)S(1)}, u32[]{:S(2)}, u32[]{:S(2)}) collective-permute-start(bf16[8,4,128,128]{3,2,1,0:T(8,128)(2,1)S(1)} %broadcast_select_fusion.1), channel_id=1, source_target_pairs={{0,4},{4,0},{1,5},{5,1},{2,6},{6,2},{3,7},{7,3},{8,12},{12,8},{9,1... | collective-permute-start | bytes 3145736 | tf_op jit(solution)/shard_map/ppermute | solution.py:14
  113.7 25.6 %collective-permute-start.16 = (bf16[8,4,128,128]{3,2,1,0:T(8,128)(2,1)S(1)}, bf16[8,4,128,128]{3,2,1,0:T(8,128)(2,1)S(1)}, u32[]{:S(2)}, u32[]{:S(2)}) collective-permute-start(bf16[8,4,128,128]{3,2,1,0:T(8,128)(2,1)S(1)} %collective-permute-done.11.refs_15_), channel_id=1, source_target_pairs={{0,16},{16,0},{8,24},{24,8},{1,17},{17,1},{9,25},{25,9},{2,18},{18... | collective-permute-start | bytes 3145736 | tf_op jit(solution)/shard_map/ppermute | solution.py:14
  116.4 23.0 %copy-start.10 = (bf16[8,4,128,128]{3,2,1,0:T(8,128)(2,1)}, bf16[8,4,128,128]{3,2,1,0:T(8,128)(2,1)S(1)}, u32[]{:S(2)}) copy-start(bf16[8,4,128,128]{3,2,1,0:T(8,128)(2,1)S(1)} %collective-permute-done.17.refs_22_) | copy-start | bytes 3145732
  139.3 1.0 copy-start.7
  140.3 2.7 %collective-permute-start.18 = (bf16[8,4,128,128]{3,2,1,0:T(8,128)(2,1)S(1)}, bf16[8,4,128,128]{3,2,1,0:T(8,128)(2,1)S(1)}, u32[]{:S(2)}, u32[]{:S(2)}) collective-permute-start(bf16[8,4,128,128]{3,2,1,0:T(8,128)(2,1)S(1)} %broadcast_select_fusion), channel_id=1, source_target_pairs={{0,4},{4,0},{1,5},{5,1},{2,6},{6,2},{3,7},{7,3},{8,12},{12,8},{9,1... | collective-permute-start | bytes 3145736 | tf_op jit(solution)/shard_map/ppermute | solution.py:14
  142.9 1.0 copy-start.11

commit v4 on v3

--- a/solution.py
+++ b/solution.py
@@ -35,23 +35,33 @@
     def shared(by_x, by_y):
         return over_core(jnp.where(send_x, by_x, by_y))
 
-    x0, p1, c0 = together((along_x(own), along_z(own), over_core(own)))
-    extra, x1, y0, p2 = together((extra, along_x(p1), along_y(x0), along_z(p1)))
-    x2, y1, p3, c1, s0 = together(
-        (along_x(p2), along_y(x1), along_z(p2), over_core(p1), shared(x0, y0))
-    )
-    x3, y2, c2, c3, s1 = together(
-        (along_x(p3), along_y(x2), over_core(p2), over_core(p3), shared(x1, y1))
-    )
-    y3, s2 = together((along_y(x3), shared(x2, y2)))
-    s3 = shared(x3, y3)
-    groups = [
-        [own, p1, p2, p3],
-        [c0, c1, c2, c3],
-        [x0, x1, x2, x3],
-        [y0, y1, y2, y3],
-        [s0, s1, s2, s3],
-    ]
+    def round_one(own):
+        return together((own, along_x(own), along_z(own), over_core(own)))
+
+    def round_two(own, x0, p1, c0):
+        return own, c0, *together((x0, p1, along_x(p1), along_y(x0), along_z(p1)))
+
+    def round_three(own, c0, x0, p1, x1, y0, p2):
+        sent = along_x(p2), along_y(x1), along_z(p2), over_core(p1), shared(x0, y0)
+        return own, c0, x0, p1, y0, *together((x1, p2, *sent))
+
+    def round_four(own, c0, x0, p1, y0, x1, p2, x2, y1, p3, c1, s0):
+        sent = along_x(p3), along_y(x2), over_core(p2), over_core(p3), shared(x1, y1)
+        return own, c0, x0, p1, y0, x1, p2, y1, p3, c1, s0, *together((x2, *sent))
+
+    def round_five(own, c0, x0, p1, y0, x1, p2, y1, p3, c1, s0, x2, x3, y2, c2, c3, s1):
+        x3, y3, s2 = together((x3, along_y(x3), shared(x2, y2)))
+        s3 = shared(x3, y3)
+        pieces = own, p1, p2, p3
+        return pieces, (c0, c1, c2, c3), (x0, x1, x2, x3), (y0, y1, y2, y3), (s0, s1, s2, s3)
+
+    half = own.shape[0] // 2
+    streams = [(own[:half],), (own[half:],)]
+    for one_round in (round_one, round_two, round_three, round_four, round_five):
+        streams = [one_round(*stream) for stream in streams]
+        if one_round is round_one:
+            extra, streams[1] = together((extra, streams[1]))
+    groups = [[(a, b) for a, b in zip(*both)] for both in zip(*streams)]
     return groups, extra
 
 
@@ -62,10 +72,10 @@
         pairs = [(i, (i + step) % depths) for i in range(depths)]
         pieces.append(permuted(own, "depth", pairs))
     count = lax.axis_size(("row", "col"))
-    groups = [pieces]
+    groups = [[(p,) for p in pieces]]
     for offset in (1, -1, 2, -2):
         pairs = [(i, (i - offset) % count) for i in range(count)]
-        groups.append([permuted(p, ("row", "col"), pairs) for p in pieces])
+        groups.append([(permuted(p, ("row", "col"), pairs),) for p in pieces])
     return groups, extra
 
 
@@ -229,8 +239,10 @@
     mine = mine.astype(jnp.int32).reshape(-1)
 
     groups, tables = window_plan()(blocks, (spots, holes, keep, mine))
-    flat = [p for group in groups for p in group]
-    kernel_body = lambda *refs: purify_kernel(len(flat), rows, slots, rows, out_slots, *refs)
+    flat = [part for group in groups for piece in group for part in piece]
+    kernel_body = lambda *refs: purify_kernel(
+        len(flat), flat[0].shape[0], slots, rows, out_slots, *refs
+    )
     smem = pl.BlockSpec(memory_space=pltpu.SMEM)
     hbm = pl.BlockSpec(memory_space=pl.ANY)
     return pl.pallas_call(
@@ -243,7 +255,7 @@
             pltpu.VMEM((rows * (window + 2 * REACH), edge, edge), jnp.bfloat16),
             pltpu.SemaphoreType.DMA,
         ],
-        compiler_params=pltpu.CompilerParams(vmem_limit_bytes=42 * 2**20),
+        compiler_params=pltpu.CompilerParams(vmem_limit_bytes=56 * 2**20),
         name="purify",
     )(*tables, *flat)
 

time: 190 us -> 161 us (0.85)
  waiting for transfers between devices: 114 us -> 83.9 us
  starting transfers between devices: 17.4 us -> 31.9 us
  Pallas kernels: 46.1 us -> 31.8 us
    ppermute x19 -> x38, waiting for transfers between devices: 114 us -> 83.9 us  [permuted(): return lax.ppermute(value, axes, pairs)]
    ppermute x19 -> x38, starting transfers between devices: 17.4 us -> 31.9 us  [permuted(): return lax.ppermute(value, axes, pairs)]
    pallas_call x1, Pallas kernels: 46.1 us -> 31.8 us  [local(): pl.pallas_call(kernel_body, out_shape=jax.ShapeDtypeStruct((rows, out_slo...]
    unnamed x25 -> x77, local copies, waits for them, and re-layouts: 4.51 us -> 1.83 us
  transfers between devices with their start and end apart: 19 -> 38, of which waited for: 11 -> 12; matrix products, arithmetic and copies ran while one was open for 4% -> 6% of each run, Pallas kernels for 0% -> 0%
where the time goes in v4:
time: 161 us; the launch traced here: 160 us
  waiting for transfers between devices  83.9 us (52%)
  starting transfers between devices  31.9 us (20%)
  Pallas kernels  31.8 us (20%)
  local copies, waits for them, and re-layouts  9.99 us (6%)
  other arithmetic  2.16 us (1%)
    ppermute x38, waiting for transfers between devices, permuted(): return lax.ppermute(value, axes, pairs)  83.9 us
    ppermute x38, starting transfers between devices, permuted(): return lax.ppermute(value, axes, pairs)  31.9 us
    pallas_call x1, Pallas kernels, local(): pl.pallas_call(kernel_body, out_shape=jax.ShapeDtypeStruct((rows, out_slo...  31.8 us
    gather x1, local copies, waits for them, and re-layouts, local(): block_cols[row_ids[:, None, :, None] % order, slot_ids[None, :, None, :]]  4.57 us
  transfers between devices with their start and end apart: 38, of which 12 were waited for; matrix products, arithmetic and copies ran while one was open for 6% of the time, Pallas kernels for 0%

profile of v4, /device:TPU:0, one launch (start us, length us, event | category | flops | bytes accessed | tf_op | source)
XLA Modules:
  0.0 160.4 jit_solution(3147363689817257942)
XLA Ops:
  0.0 1.3 fusion.24
  1.4 0.5 collective-permute-start.5
  1.9 2.6 %collective-permute-start.4 = (bf16[4,4,128,128]{3,2,1,0:T(8,128)(2,1)S(1)}, bf16[4,4,128,128]{3,2,1,0:T(8,128)(2,1)}, u32[]{:S(2)}, u32[]{:S(2)}) collective-permute-start(bf16[4,4,128,128]{3,2,1,0:T(8,128)(2,1)S(1)} %get-tuple-element.71.refs_4_), channel_id=1, source_target_pairs={{0,1},{1,2},{2,3},{3,0},{4,5},{5,6},{6,7},{7,4},{8,9},{9,10},{10,1... | collective-permute-start | bytes 1572872 | tf_op jit(solution)/shard_map/ppermute | solution.py:14
  4.5 1.5 collective-permute-start.3
  6.0 1.6 collective-permute-start.1
  7.7 0.1 fusion
  7.8 0.1 copy.6
  7.9 0.6 gather_fusion.1
  8.5 0.2 fusion.2
  8.8 0.1 broadcast_or_fusion
  8.9 0.6 collective-permute-start
  9.5 10.0 %collective-permute-done.4.refs_6_ = bf16[4,4,128,128]{3,2,1,0:T(8,128)(2,1)} collective-permute-done((bf16[4,4,128,128]{3,2,1,0:T(8,128)(2,1)S(1)}, bf16[4,4,128,128]{3,2,1,0:T(8,128)(2,1)}, u32[]{:S(2)}, u32[]{:S(2)}) %collective-permute-start.4) | collective-permute-done | bytes 524320 | tf_op jit(solution)/shard_map/ppermute | solution.py:14
  19.4 1.7 %collective-permute-start.7 = (bf16[4,4,128,128]{3,2,1,0:T(8,128)(2,1)S(1)}, bf16[4,4,128,128]{3,2,1,0:T(8,128)(2,1)S(1)}, u32[]{:S(2)}, u32[]{:S(2)}) collective-permute-start(bf16[4,4,128,128]{3,2,1,0:T(8,128)(2,1)S(1)} %collective-permute-done.3.refs_20_), channel_id=1, source_target_pairs={{0,16},{16,0},{8,24},{24,8},{1,17},{17,1},{9,25},{25,9},{2,18},{18... | collective-permute-start | bytes 1572872 | tf_op jit(solution)/shard_map/ppermute | solution.py:14
  21.2 0.6 compare_select_fusion.6.refs_1_
  21.7 1.2 collective-permute-start.8
  23.0 1.6 collective-permute-start.6
  24.5 0.1 constant_dynamic-slice_fusion
  24.6 0.7 reshape.222.refs_3_
  25.3 0.6 reshape.223.refs_2_
  25.9 0.1 reshape.224
  26.0 4.6 %gather_fusion = s32[640]{0:T(1024)S(1)} fusion(s32[64,16]{0,1:T(8,128)S(1)} %copy-done, s32[640]{0:T(1024)S(1)} %reshape.224), kind=kCustom, calls=%fused_computation | custom fusion | bytes 10240 | tf_op jit(solution)/shard_map/gather | solution.py:222
  30.6 0.1 add.343
  30.7 0.1 add.344
  30.8 0.6 fusion.11.refs_0_
  31.4 0.9 collective-permute-start.10
  32.3 1.3 collective-permute-start.11
  33.6 1.5 collective-permute-start.9
  35.1 6.8 %collective-permute-done.8.refs_8_ = bf16[4,4,128,128]{3,2,1,0:T(8,128)(2,1)} collective-permute-done((bf16[4,4,128,128]{3,2,1,0:T(8,128)(2,1)}, bf16[4,4,128,128]{3,2,1,0:T(8,128)(2,1)}, u32[]{:S(2)}, u32[]{:S(2)}) %collective-permute-start.8) | collective-permute-done | bytes 524320 | tf_op jit(solution)/shard_map/ppermute | solution.py:14
  42.0 0.1 collective-permute-start.16
  42.0 0.5 collective-permute-start.15
  42.5 1.6 %collective-permute-done.10.refs_29_ = bf16[4,4,128,128]{3,2,1,0:T(8,128)(2,1)S(1)} collective-permute-done((bf16[4,4,128,128]{3,2,1,0:T(8,128)(2,1)S(1)}, bf16[4,4,128,128]{3,2,1,0:T(8,128)(2,1)S(1)}, u32[]{:S(2)}, u32[]{:S(2)}) %collective-permute-start.10) | collective-permute-done | bytes 524320 | tf_op jit(solution)/shard_map/ppermute | solution.py:14
  44.2 1.4 collective-permute-start.13
  45.6 7.3 %collective-permute-done.11.refs_9_ = bf16[4,4,128,128]{3,2,1,0:T(8,128)(2,1)} collective-permute-done((bf16[4,4,128,128]{3,2,1,0:T(8,128)(2,1)}, bf16[4,4,128,128]{3,2,1,0:T(8,128)(2,1)}, u32[]{:S(2)}, u32[]{:S(2)}) %collective-permute-start.11) | collective-permute-done | bytes 524320 | tf_op jit(solution)/shard_map/ppermute | solution.py:14
  52.9 1.6 collective-permute-start.12
  54.5 0.1 collective-permute-start.21
  54.6 0.5 collective-permute-start.20
  55.1 1.3 collective-permute-done.13.refs_30_
  56.5 1.7 %collective-permute-start.18 = (bf16[4,4,128,128]{3,2,1,0:T(8,128)(2,1)S(1)}, bf16[4,4,128,128]{3,2,1,0:T(8,128)(2,1)S(1)}, u32[]{:S(2)}, u32[]{:S(2)}) collective-permute-start(bf16[4,4,128,128]{3,2,1,0:T(8,128)(2,1)S(1)} %collective-permute-done.9.refs_23_), channel_id=1, source_target_pairs={{0,16},{16,0},{8,24},{24,8},{1,17},{17,1},{9,25},{25,9},{2,18},{18... | collective-permute-start | bytes 1572872 | tf_op jit(solution)/shard_map/ppermute | solution.py:14
  58.1 10.5 %collective-permute-done.14.refs_10_ = bf16[4,4,128,128]{3,2,1,0:T(8,128)(2,1)S(1)} collective-permute-done((bf16[4,4,128,128]{3,2,1,0:T(8,128)(2,1)}, bf16[4,4,128,128]{3,2,1,0:T(8,128)(2,1)S(1)}, u32[]{:S(2)}, u32[]{:S(2)}) %collective-permute-start.14) | collective-permute-done | bytes 524320 | tf_op jit(solution)/shard_map/ppermute | solution.py:14
  68.6 1.4 collective-permute-start.17
  70.0 0.1 broadcast_select_fusion.5
  70.1 0.1 collective-permute-start.26
  70.2 0.5 collective-permute-start.24
  70.7 1.5 collective-permute-start.23
  72.2 11.2 %collective-permute-done.19.refs_11_ = bf16[4,4,128,128]{3,2,1,0:T(8,128)(2,1)S(1)} collective-permute-done((bf16[4,4,128,128]{3,2,1,0:T(8,128)(2,1)}, bf16[4,4,128,128]{3,2,1,0:T(8,128)(2,1)S(1)}, u32[]{:S(2)}, u32[]{:S(2)}) %collective-permute-start.19) | collective-permute-done | bytes 524320 | tf_op jit(solution)/shard_map/ppermute | solution.py:14
  83.4 1.3 collective-permute-start.22
  84.7 0.1 broadcast_select_fusion.4
  84.8 0.2 collective-permute-start.31
  85.1 0.3 collective-permute-start.29
  85.4 1.5 collective-permute-start.28
  87.0 0.8 copy-done.29
  87.8 10.0 %collective-permute-done.22.refs_26_ = bf16[4,4,128,128]{3,2,1,0:T(8,128)(2,1)S(1)} collective-permute-done((bf16[4,4,128,128]{3,2,1,0:T(8,128)(2,1)S(1)}, bf16[4,4,128,128]{3,2,1,0:T(8,128)(2,1)S(1)}, u32[]{:S(2)}, u32[]{:S(2)}) %collective-permute-start.22) | collective-permute-done | bytes 524320 | tf_op jit(solution)/shard_map/ppermute | solution.py:14
  97.8 1.2 collective-permute-start.27
  99.1 0.1 collective-permute-start.33
  99.2 1.6 collective-permute-start.32
  100.8 10.5 %collective-permute-done.27.refs_27_ = bf16[4,4,128,128]{3,2,1,0:T(8,128)(2,1)S(1)} collective-permute-done((bf16[4,4,128,128]{3,2,1,0:T(8,128)(2,1)S(1)}, bf16[4,4,128,128]{3,2,1,0:T(8,128)(2,1)S(1)}, u32[]{:S(2)}, u32[]{:S(2)}) %collective-permute-start.27) | collective-permute-done | bytes 524320 | tf_op jit(solution)/shard_map/ppermute | solution.py:14
  111.4 0.1 collective-permute-start.35
  111.4 1.3 collective-permute-start.34
  112.7 0.8 collective-permute-done.32.refs_34_
  113.7 12.1 %collective-permute-done.34.refs_35_ = bf16[4,4,128,128]{3,2,1,0:T(8,128)(2,1)S(1)} collective-permute-done((bf16[4,4,128,128]{3,2,1,0:T(8,128)(2,1)S(1)}, bf16[4,4,128,128]{3,2,1,0:T(8,128)(2,1)S(1)}, u32[]{:S(2)}, u32[]{:S(2)}) %collective-permute-start.34) | collective-permute-done | bytes 524320 | tf_op jit(solution)/shard_map/ppermute | solution.py:14
  125.9 0.1 collective-permute-start.37
  126.0 1.9 %collective-permute-done.37.refs_43_ = bf16[4,4,128,128]{3,2,1,0:T(8,128)(2,1)S(1)} collective-permute-done((bf16[4,4,128,128]{3,2,1,0:T(8,128)(2,1)S(1)}, bf16[4,4,128,128]{3,2,1,0:T(8,128)(2,1)S(1)}, u32[]{:S(2)}, u32[]{:S(2)}) %collective-permute-start.37) | collective-permute-done | bytes 524320 | tf_op jit(solution)/shard_map/ppermute | solution.py:14
  127.9 0.8 copy-done.36
  128.7 31.8 %purify.1 = bf16[8,6,128,128]{3,2,1,0:T(8,128)(2,1)} custom-call(s32[640]{0:T(1024)} %fusion.11.refs_0_, s32[40]{0:T(128)} %compare_select_fusion.6.refs_1_, s32[320]{0:T(512)} %reshape.223.refs_2_, s32[48]{0:T(128)} %reshape.222.refs_3_, bf16[4,4,128,128]{3,2,1,0:T(8,128)(2,1)} %copy-done.17, bf16[4,4,128,128]{3,2,1,0:T(8,128)(2,1)} %copy-done.18, ...), custom_call_target="tpu_custom_call" | custom-call | tf_op jit(solution)/shard_map/purify/pallas_call | solution.py:248
  (125 shorter events, 0.8 us)
Async XLA Ops:
  1.3 18.1 %copy-start.17 = (bf16[4,4,128,128]{3,2,1,0:T(8,128)(2,1)}, bf16[4,4,128,128]{3,2,1,0:T(8,128)(2,1)S(1)}, u32[]{:S(2)}) copy-start(bf16[4,4,128,128]{3,2,1,0:T(8,128)(2,1)S(1)} %get-tuple-element.71.refs_4_) | copy-start | bytes 1572868
  1.3 29.3 %copy-start.18 = (bf16[4,4,128,128]{3,2,1,0:T(8,128)(2,1)}, bf16[4,4,128,128]{3,2,1,0:T(8,128)(2,1)S(1)}, u32[]{:S(2)}) copy-start(bf16[4,4,128,128]{3,2,1,0:T(8,128)(2,1)S(1)} %get-tuple-element.72.refs_5_) | copy-start | bytes 1572868
  1.4 7.5 %collective-permute-start.5 = (bf16[4,4,128,128]{3,2,1,0:T(8,128)(2,1)S(1)}, bf16[4,4,128,128]{3,2,1,0:T(8,128)(2,1)S(1)}, u32[]{:S(2)}, u32[]{:S(2)}) collective-permute-start(bf16[4,4,128,128]{3,2,1,0:T(8,128)(2,1)S(1)} %get-tuple-element.71.refs_4_), channel_id=1, source_target_pairs={{0,4},{4,0},{1,5},{5,1},{2,6},{6,2},{3,7},{7,3},{8,12},{12,8},{9,1... | collective-permute-start | bytes 1572872 | tf_op jit(solution)/shard_map/ppermute | solution.py:14
  1.9 17.5 %collective-permute-start.4 = (bf16[4,4,128,128]{3,2,1,0:T(8,128)(2,1)S(1)}, bf16[4,4,128,128]{3,2,1,0:T(8,128)(2,1)}, u32[]{:S(2)}, u32[]{:S(2)}) collective-permute-start(bf16[4,4,128,128]{3,2,1,0:T(8,128)(2,1)S(1)} %get-tuple-element.71.refs_4_), channel_id=1, source_target_pairs={{0,1},{1,2},{2,3},{3,0},{4,5},{5,6},{6,7},{7,4},{8,9},{9,10},{10,1... | collective-permute-start | bytes 1572872 | tf_op jit(solution)/shard_map/ppermute | solution.py:14
  4.5 14.9 %collective-permute-start.3 = (bf16[4,4,128,128]{3,2,1,0:T(8,128)(2,1)S(1)}, bf16[4,4,128,128]{3,2,1,0:T(8,128)(2,1)S(1)}, u32[]{:S(2)}, u32[]{:S(2)}) collective-permute-start(bf16[4,4,128,128]{3,2,1,0:T(8,128)(2,1)S(1)} %get-tuple-element.71.refs_4_), channel_id=1, source_target_pairs={{0,8},{8,0},{16,24},{24,16},{1,9},{9,1},{17,25},{25,17},{2,10},{10... | collective-permute-start | bytes 1572872 | tf_op jit(solution)/shard_map/ppermute | solution.py:14
  6.0 17.0 %collective-permute-start.2 = (bf16[4,4,128,128]{3,2,1,0:T(8,128)(2,1)S(1)}, bf16[4,4,128,128]{3,2,1,0:T(8,128)(2,1)S(1)}, u32[]{:S(2)}, u32[]{:S(2)}) collective-permute-start(bf16[4,4,128,128]{3,2,1,0:T(8,128)(2,1)S(1)} %get-tuple-element.72.refs_5_), channel_id=1, source_target_pairs={{0,4},{4,0},{1,5},{5,1},{2,6},{6,2},{3,7},{7,3},{8,12},{12,8},{9,1... | collective-permute-start | bytes 1572872 | tf_op jit(solution)/shard_map/ppermute | solution.py:14
  6.0 25.4 %collective-permute-start.1 = (bf16[4,4,128,128]{3,2,1,0:T(8,128)(2,1)S(1)}, bf16[4,4,128,128]{3,2,1,0:T(8,128)(2,1)}, u32[]{:S(2)}, u32[]{:S(2)}) collective-permute-start(bf16[4,4,128,128]{3,2,1,0:T(8,128)(2,1)S(1)} %get-tuple-element.72.refs_5_), channel_id=1, source_target_pairs={{0,1},{1,2},{2,3},{3,0},{4,5},{5,6},{6,7},{7,4},{8,9},{9,10},{10,1... | collective-permute-start | bytes 1572872 | tf_op jit(solution)/shard_map/ppermute | solution.py:14
  8.9 22.6 %collective-permute-start = (bf16[4,4,128,128]{3,2,1,0:T(8,128)(2,1)S(1)}, bf16[4,4,128,128]{3,2,1,0:T(8,128)(2,1)S(1)}, u32[]{:S(2)}, u32[]{:S(2)}) collective-permute-start(bf16[4,4,128,128]{3,2,1,0:T(8,128)(2,1)S(1)} %get-tuple-element.72.refs_5_), channel_id=1, source_target_pairs={{0,8},{8,0},{16,24},{24,16},{1,9},{9,1},{17,25},{25,17},{2,10},{10... | collective-permute-start | bytes 1572872 | tf_op jit(solution)/shard_map/ppermute | solution.py:14
  19.4 22.5 %copy-start.1 = (bf16[4,4,128,128]{3,2,1,0:T(8,128)(2,1)}, bf16[4,4,128,128]{3,2,1,0:T(8,128)(2,1)S(1)}, u32[]{:S(2)}) copy-start(bf16[4,4,128,128]{3,2,1,0:T(8,128)(2,1)S(1)} %collective-permute-done.3.refs_20_) | copy-start | bytes 1572868
  19.4 14.2 %collective-permute-start.7 = (bf16[4,4,128,128]{3,2,1,0:T(8,128)(2,1)S(1)}, bf16[4,4,128,128]{3,2,1,0:T(8,128)(2,1)S(1)}, u32[]{:S(2)}, u32[]{:S(2)}) collective-permute-start(bf16[4,4,128,128]{3,2,1,0:T(8,128)(2,1)S(1)} %collective-permute-done.3.refs_20_), channel_id=1, source_target_pairs={{0,16},{16,0},{8,24},{24,8},{1,17},{17,1},{9,25},{25,9},{2,18},{18... | collective-permute-start | bytes 1572872 | tf_op jit(solution)/shard_map/ppermute | solution.py:14
  21.7 20.1 %collective-permute-start.8 = (bf16[4,4,128,128]{3,2,1,0:T(8,128)(2,1)}, bf16[4,4,128,128]{3,2,1,0:T(8,128)(2,1)}, u32[]{:S(2)}, u32[]{:S(2)}) collective-permute-start(bf16[4,4,128,128]{3,2,1,0:T(8,128)(2,1)} %collective-permute-done.4.refs_6_), channel_id=1, source_target_pairs={{0,1},{1,2},{2,3},{3,0},{4,5},{5,6},{6,7},{7,4},{8,9},{9,10},{10,1... | collective-permute-start | bytes 1572872 | tf_op jit(solution)/shard_map/ppermute | solution.py:14
  23.0 18.9 %collective-permute-start.6 = (bf16[4,4,128,128]{3,2,1,0:T(8,128)(2,1)}, bf16[4,4,128,128]{3,2,1,0:T(8,128)(2,1)S(1)}, u32[]{:S(2)}, u32[]{:S(2)}) collective-permute-start(bf16[4,4,128,128]{3,2,1,0:T(8,128)(2,1)} %collective-permute-done.4.refs_6_), channel_id=1, source_target_pairs={{0,8},{8,0},{16,24},{24,16},{1,9},{9,1},{17,25},{25,17},{2,10},{10... | collective-permute-start | bytes 1572872 | tf_op jit(solution)/shard_map/ppermute | solution.py:14
  31.4 23.1 %copy-start.2 = (bf16[4,4,128,128]{3,2,1,0:T(8,128)(2,1)}, bf16[4,4,128,128]{3,2,1,0:T(8,128)(2,1)S(1)}, u32[]{:S(2)}) copy-start(bf16[4,4,128,128]{3,2,1,0:T(8,128)(2,1)S(1)} %collective-permute-done.refs_21_) | copy-start | bytes 1572868
  31.4 12.8 %collective-permute-start.10 = (bf16[4,4,128,128]{3,2,1,0:T(8,128)(2,1)S(1)}, bf16[4,4,128,128]{3,2,1,0:T(8,128)(2,1)S(1)}, u32[]{:S(2)}, u32[]{:S(2)}) collective-permute-start(bf16[4,4,128,128]{3,2,1,0:T(8,128)(2,1)S(1)} %collective-permute-done.refs_21_), channel_id=1, source_target_pairs={{0,16},{16,0},{8,24},{24,8},{1,17},{17,1},{9,25},{25,9},{2,18},{18... | collective-permute-start | bytes 1572872 | tf_op jit(solution)/shard_map/ppermute | solution.py:14
  32.3 20.6 %collective-permute-start.11 = (bf16[4,4,128,128]{3,2,1,0:T(8,128)(2,1)}, bf16[4,4,128,128]{3,2,1,0:T(8,128)(2,1)}, u32[]{:S(2)}, u32[]{:S(2)}) collective-permute-start(bf16[4,4,128,128]{3,2,1,0:T(8,128)(2,1)} %collective-permute-done.1.refs_7_), channel_id=1, source_target_pairs={{0,1},{1,2},{2,3},{3,0},{4,5},{5,6},{6,7},{7,4},{8,9},{9,10},{10,1... | collective-permute-start | bytes 1572872 | tf_op jit(solution)/shard_map/ppermute | solution.py:14
  33.6 20.9 %copy-start.3 = (bf16[4,4,128,128]{3,2,1,0:T(8,128)(2,1)}, bf16[4,4,128,128]{3,2,1,0:T(8,128)(2,1)S(1)}, u32[]{:S(2)}) copy-start(bf16[4,4,128,128]{3,2,1,0:T(8,128)(2,1)S(1)} %collective-permute-done.7.refs_28_) | copy-start | bytes 1572868
  33.6 19.3 %collective-permute-start.9 = (bf16[4,4,128,128]{3,2,1,0:T(8,128)(2,1)}, bf16[4,4,128,128]{3,2,1,0:T(8,128)(2,1)S(1)}, u32[]{:S(2)}, u32[]{:S(2)}) collective-permute-start(bf16[4,4,128,128]{3,2,1,0:T(8,128)(2,1)} %collective-permute-done.1.refs_7_), channel_id=1, source_target_pairs={{0,8},{8,0},{16,24},{24,16},{1,9},{9,1},{17,25},{25,17},{2,10},{10... | collective-permute-start | bytes 1572872 | tf_op jit(solution)/shard_map/ppermute | solution.py:14
  41.9 28.1 %copy-start.4 = (bf16[4,4,128,128]{3,2,1,0:T(8,128)(2,1)}, bf16[4,4,128,128]{3,2,1,0:T(8,128)(2,1)S(1)}, u32[]{:S(2)}) copy-start(bf16[4,4,128,128]{3,2,1,0:T(8,128)(2,1)S(1)} %collective-permute-done.6.refs_22_) | copy-start | bytes 1572868
  42.0 12.6 %collective-permute-start.16 = (bf16[4,4,128,128]{3,2,1,0:T(8,128)(2,1)S(1)}, bf16[4,4,128,128]{3,2,1,0:T(8,128)(2,1)S(1)}, u32[]{:S(2)}, u32[]{:S(2)}) collective-permute-start(bf16[4,4,128,128]{3,2,1,0:T(8,128)(2,1)S(1)} %broadcast_select_fusion.7), channel_id=1, source_target_pairs={{0,4},{4,0},{1,5},{5,1},{2,6},{6,2},{3,7},{7,3},{8,12},{12,8},{9,1... | collective-permute-start | bytes 1572872 | tf_op jit(solution)/shard_map/ppermute | solution.py:14
  42.0 12.6 %collective-permute-start.15 = (bf16[4,4,128,128]{3,2,1,0:T(8,128)(2,1)}, bf16[4,4,128,128]{3,2,1,0:T(8,128)(2,1)S(1)}, u32[]{:S(2)}, u32[]{:S(2)}) collective-permute-start(bf16[4,4,128,128]{3,2,1,0:T(8,128)(2,1)} %collective-permute-done.4.refs_6_), channel_id=1, source_target_pairs={{0,4},{4,0},{1,5},{5,1},{2,6},{6,2},{3,7},{7,3},{8,12},{12,8},{9,1... | collective-permute-start | bytes 1572872 | tf_op jit(solution)/shard_map/ppermute | solution.py:14
  44.2 25.9 %copy-start.5 = (bf16[4,4,128,128]{3,2,1,0:T(8,128)(2,1)}, bf16[4,4,128,128]{3,2,1,0:T(8,128)(2,1)S(1)}, u32[]{:S(2)}) copy-start(bf16[4,4,128,128]{3,2,1,0:T(8,128)(2,1)S(1)} %collective-permute-done.10.refs_29_) | copy-start | bytes 1572868
  44.2 12.3 %collective-permute-start.13 = (bf16[4,4,128,128]{3,2,1,0:T(8,128)(2,1)S(1)}, bf16[4,4,128,128]{3,2,1,0:T(8,128)(2,1)S(1)}, u32[]{:S(2)}, u32[]{:S(2)}) collective-permute-start(bf16[4,4,128,128]{3,2,1,0:T(8,128)(2,1)S(1)} %collective-permute-done.6.refs_22_), channel_id=1, source_target_pairs={{0,16},{16,0},{8,24},{24,8},{1,17},{17,1},{9,25},{25,9},{2,18},{18... | collective-permute-start | bytes 1572872 | tf_op jit(solution)/shard_map/ppermute | solution.py:14
  52.9 15.7 %collective-permute-start.14 = (bf16[4,4,128,128]{3,2,1,0:T(8,128)(2,1)}, bf16[4,4,128,128]{3,2,1,0:T(8,128)(2,1)S(1)}, u32[]{:S(2)}, u32[]{:S(2)}) collective-permute-start(bf16[4,4,128,128]{3,2,1,0:T(8,128)(2,1)} %collective-permute-done.8.refs_8_), channel_id=1, source_target_pairs={{0,1},{1,2},{2,3},{3,0},{4,5},{5,6},{6,7},{7,4},{8,9},{9,10},{10,1... | collective-permute-start | bytes 1572872 | tf_op jit(solution)/shard_map/ppermute | solution.py:14
  52.9 31.8 %copy-start.6 = (bf16[4,4,128,128]{3,2,1,0:T(8,128)(2,1)}, bf16[4,4,128,128]{3,2,1,0:T(8,128)(2,1)S(1)}, u32[]{:S(2)}) copy-start(bf16[4,4,128,128]{3,2,1,0:T(8,128)(2,1)S(1)} %collective-permute-done.9.refs_23_) | copy-start | bytes 1572868
  52.9 15.7 %collective-permute-start.12 = (bf16[4,4,128,128]{3,2,1,0:T(8,128)(2,1)}, bf16[4,4,128,128]{3,2,1,0:T(8,128)(2,1)S(1)}, u32[]{:S(2)}, u32[]{:S(2)}) collective-permute-start(bf16[4,4,128,128]{3,2,1,0:T(8,128)(2,1)} %collective-permute-done.8.refs_8_), channel_id=1, source_target_pairs={{0,8},{8,0},{16,24},{24,16},{1,9},{9,1},{17,25},{25,17},{2,10},{10... | collective-permute-start | bytes 1572872 | tf_op jit(solution)/shard_map/ppermute | solution.py:14
  54.5 30.2 %copy-start.21 = (bf16[4,4,128,128]{3,2,1,0:T(8,128)(2,1)}, bf16[4,4,128,128]{3,2,1,0:T(8,128)(2,1)S(1)}, u32[]{:S(2)}) copy-start(bf16[4,4,128,128]{3,2,1,0:T(8,128)(2,1)S(1)} %collective-permute-done.16.refs_36_) | copy-start | bytes 1572868
  54.5 15.6 %collective-permute-start.21 = (bf16[4,4,128,128]{3,2,1,0:T(8,128)(2,1)S(1)}, bf16[4,4,128,128]{3,2,1,0:T(8,128)(2,1)S(1)}, u32[]{:S(2)}, u32[]{:S(2)}) collective-permute-start(bf16[4,4,128,128]{3,2,1,0:T(8,128)(2,1)S(1)} %broadcast_select_fusion.6), channel_id=1, source_target_pairs={{0,4},{4,0},{1,5},{5,1},{2,6},{6,2},{3,7},{7,3},{8,12},{12,8},{9,1... | collective-permute-start | bytes 1572872 | tf_op jit(solution)/shard_map/ppermute | solution.py:14
  54.6 30.2 %copy-start.22 = (bf16[4,4,128,128]{3,2,1,0:T(8,128)(2,1)}, bf16[4,4,128,128]{3,2,1,0:T(8,128)(2,1)S(1)}, u32[]{:S(2)}) copy-start(bf16[4,4,128,128]{3,2,1,0:T(8,128)(2,1)S(1)} %collective-permute-done.15.refs_14_) | copy-start | bytes 1572868
  54.6 15.6 %collective-permute-start.20 = (bf16[4,4,128,128]{3,2,1,0:T(8,128)(2,1)}, bf16[4,4,128,128]{3,2,1,0:T(8,128)(2,1)S(1)}, u32[]{:S(2)}, u32[]{:S(2)}) collective-permute-start(bf16[4,4,128,128]{3,2,1,0:T(8,128)(2,1)} %collective-permute-done.1.refs_7_), channel_id=1, source_target_pairs={{0,4},{4,0},{1,5},{5,1},{2,6},{6,2},{3,7},{7,3},{8,12},{12,8},{9,1... | collective-permute-start | bytes 1572872 | tf_op jit(solution)/shard_map/ppermute | solution.py:14
  56.5 28.3 %copy-start.7 = (bf16[4,4,128,128]{3,2,1,0:T(8,128)(2,1)}, bf16[4,4,128,128]{3,2,1,0:T(8,128)(2,1)S(1)}, u32[]{:S(2)}) copy-start(bf16[4,4,128,128]{3,2,1,0:T(8,128)(2,1)S(1)} %collective-permute-done.13.refs_30_) | copy-start | bytes 1572868
  56.5 14.3 %collective-permute-start.18 = (bf16[4,4,128,128]{3,2,1,0:T(8,128)(2,1)S(1)}, bf16[4,4,128,128]{3,2,1,0:T(8,128)(2,1)S(1)}, u32[]{:S(2)}, u32[]{:S(2)}) collective-permute-start(bf16[4,4,128,128]{3,2,1,0:T(8,128)(2,1)S(1)} %collective-permute-done.9.refs_23_), channel_id=1, source_target_pairs={{0,16},{16,0},{8,24},{24,8},{1,17},{17,1},{9,25},{25,9},{2,18},{18... | collective-permute-start | bytes 1572872 | tf_op jit(solution)/shard_map/ppermute | solution.py:14
  68.6 16.2 %copy-start.23 = (bf16[4,4,128,128]{3,2,1,0:T(8,128)(2,1)}, bf16[4,4,128,128]{3,2,1,0:T(8,128)(2,1)S(1)}, u32[]{:S(2)}) copy-start(bf16[4,4,128,128]{3,2,1,0:T(8,128)(2,1)S(1)} %collective-permute-done.14.refs_10_) | copy-start | bytes 1572868
  68.6 14.8 %collective-permute-start.19 = (bf16[4,4,128,128]{3,2,1,0:T(8,128)(2,1)}, bf16[4,4,128,128]{3,2,1,0:T(8,128)(2,1)S(1)}, u32[]{:S(2)}, u32[]{:S(2)}) collective-permute-start(bf16[4,4,128,128]{3,2,1,0:T(8,128)(2,1)} %collective-permute-done.11.refs_9_), channel_id=1, source_target_pairs={{0,1},{1,2},{2,3},{3,0},{4,5},{5,6},{6,7},{7,4},{8,9},{9,10},{10,1... | collective-permute-start | bytes 1572872 | tf_op jit(solution)/shard_map/ppermute | solution.py:14
  68.6 30.4 %copy-start.8 = (bf16[4,4,128,128]{3,2,1,0:T(8,128)(2,1)}, bf16[4,4,128,128]{3,2,1,0:T(8,128)(2,1)S(1)}, u32[]{:S(2)}) copy-start(bf16[4,4,128,128]{3,2,1,0:T(8,128)(2,1)S(1)} %collective-permute-done.12.refs_24_) | copy-start | bytes 1572868
  68.6 14.8 %collective-permute-start.17 = (bf16[4,4,128,128]{3,2,1,0:T(8,128)(2,1)}, bf16[4,4,128,128]{3,2,1,0:T(8,128)(2,1)S(1)}, u32[]{:S(2)}, u32[]{:S(2)}) collective-permute-start(bf16[4,4,128,128]{3,2,1,0:T(8,128)(2,1)} %collective-permute-done.11.refs_9_), channel_id=1, source_target_pairs={{0,8},{8,0},{16,24},{24,16},{1,9},{9,1},{17,25},{25,17},{2,10},{10... | collective-permute-start | bytes 1572872 | tf_op jit(solution)/shard_map/ppermute | solution.py:14
  70.1 28.9 %copy-start.24 = (bf16[4,4,128,128]{3,2,1,0:T(8,128)(2,1)}, bf16[4,4,128,128]{3,2,1,0:T(8,128)(2,1)S(1)}, u32[]{:S(2)}) copy-start(bf16[4,4,128,128]{3,2,1,0:T(8,128)(2,1)S(1)} %collective-permute-done.21.refs_37_) | copy-start | bytes 1572868
  70.1 14.7 %collective-permute-start.26 = (bf16[4,4,128,128]{3,2,1,0:T(8,128)(2,1)S(1)}, bf16[4,4,128,128]{3,2,1,0:T(8,128)(2,1)S(1)}, u32[]{:S(2)}, u32[]{:S(2)}) collective-permute-start(bf16[4,4,128,128]{3,2,1,0:T(8,128)(2,1)S(1)} %broadcast_select_fusion.5), channel_id=1, source_target_pairs={{0,4},{4,0},{1,5},{5,1},{2,6},{6,2},{3,7},{7,3},{8,12},{12,8},{9,1... | collective-permute-start | bytes 1572872 | tf_op jit(solution)/shard_map/ppermute | solution.py:14
  70.2 28.8 %copy-start.25 = (bf16[4,4,128,128]{3,2,1,0:T(8,128)(2,1)}, bf16[4,4,128,128]{3,2,1,0:T(8,128)(2,1)S(1)}, u32[]{:S(2)}) copy-start(bf16[4,4,128,128]{3,2,1,0:T(8,128)(2,1)S(1)} %collective-permute-done.20.refs_15_) | copy-start | bytes 1572868
  70.2 14.8 %collective-permute-start.24 = (bf16[4,4,128,128]{3,2,1,0:T(8,128)(2,1)}, bf16[4,4,128,128]{3,2,1,0:T(8,128)(2,1)S(1)}, u32[]{:S(2)}, u32[]{:S(2)}) collective-permute-start(bf16[4,4,128,128]{3,2,1,0:T(8,128)(2,1)} %collective-permute-done.8.refs_8_), channel_id=1, source_target_pairs={{0,4},{4,0},{1,5},{5,1},{2,6},{6,2},{3,7},{7,3},{8,12},{12,8},{9,1... | collective-permute-start | bytes 1572872 | tf_op jit(solution)/shard_map/ppermute | solution.py:14
  70.7 28.3 %copy-start.9 = (bf16[4,4,128,128]{3,2,1,0:T(8,128)(2,1)}, bf16[4,4,128,128]{3,2,1,0:T(8,128)(2,1)S(1)}, u32[]{:S(2)}) copy-start(bf16[4,4,128,128]{3,2,1,0:T(8,128)(2,1)S(1)} %collective-permute-done.18.refs_31_) | copy-start | bytes 1572868
  70.7 14.7 %collective-permute-start.23 = (bf16[4,4,128,128]{3,2,1,0:T(8,128)(2,1)S(1)}, bf16[4,4,128,128]{3,2,1,0:T(8,128)(2,1)S(1)}, u32[]{:S(2)}, u32[]{:S(2)}) collective-permute-start(bf16[4,4,128,128]{3,2,1,0:T(8,128)(2,1)S(1)} %collective-permute-done.12.refs_24_), channel_id=1, source_target_pairs={{0,16},{16,0},{8,24},{24,8},{1,17},{17,1},{9,25},{25,9},{2,18},{18... | collective-permute-start | bytes 1572872 | tf_op jit(solution)/shard_map/ppermute | solution.py:14
  83.4 42.5 %copy-start.26 = (bf16[4,4,128,128]{3,2,1,0:T(8,128)(2,1)}, bf16[4,4,128,128]{3,2,1,0:T(8,128)(2,1)S(1)}, u32[]{:S(2)}) copy-start(bf16[4,4,128,128]{3,2,1,0:T(8,128)(2,1)S(1)} %collective-permute-done.19.refs_11_) | copy-start | bytes 1572868
  83.4 3.5 %collective-permute-start.25 = (bf16[4,4,128,128]{3,2,1,0:T(8,128)(2,1)S(1)}, bf16[4,4,128,128]{3,2,1,0:T(8,128)(2,1)S(1)}, u32[]{:S(2)}, u32[]{:S(2)}) collective-permute-start(bf16[4,4,128,128]{3,2,1,0:T(8,128)(2,1)S(1)} %collective-permute-done.14.refs_10_), channel_id=1, source_target_pairs={{0,4},{4,0},{1,5},{5,1},{2,6},{6,2},{3,7},{7,3},{8,12},{12,8},{9,1... | collective-permute-start | bytes 1572872 | tf_op jit(solution)/shard_map/ppermute | solution.py:14
  83.4 27.8 %copy-start.10 = (bf16[4,4,128,128]{3,2,1,0:T(8,128)(2,1)}, bf16[4,4,128,128]{3,2,1,0:T(8,128)(2,1)S(1)}, u32[]{:S(2)}) copy-start(bf16[4,4,128,128]{3,2,1,0:T(8,128)(2,1)S(1)} %collective-permute-done.17.refs_25_) | copy-start | bytes 1572868
  83.4 14.3 %collective-permute-start.22 = (bf16[4,4,128,128]{3,2,1,0:T(8,128)(2,1)S(1)}, bf16[4,4,128,128]{3,2,1,0:T(8,128)(2,1)S(1)}, u32[]{:S(2)}, u32[]{:S(2)}) collective-permute-start(bf16[4,4,128,128]{3,2,1,0:T(8,128)(2,1)S(1)} %collective-permute-done.14.refs_10_), channel_id=1, source_target_pairs={{0,8},{8,0},{16,24},{24,16},{1,9},{9,1},{17,25},{25,17},{2,10},{10... | collective-permute-start | bytes 1572872 | tf_op jit(solution)/shard_map/ppermute | solution.py:14
  84.8 26.5 %copy-start.27 = (bf16[4,4,128,128]{3,2,1,0:T(8,128)(2,1)}, bf16[4,4,128,128]{3,2,1,0:T(8,128)(2,1)S(1)}, u32[]{:S(2)}) copy-start(bf16[4,4,128,128]{3,2,1,0:T(8,128)(2,1)S(1)} %collective-permute-done.26.refs_38_) | copy-start | bytes 1572868
  84.8 14.2 %collective-permute-start.31 = (bf16[4,4,128,128]{3,2,1,0:T(8,128)(2,1)S(1)}, bf16[4,4,128,128]{3,2,1,0:T(8,128)(2,1)S(1)}, u32[]{:S(2)}, u32[]{:S(2)}) collective-permute-start(bf16[4,4,128,128]{3,2,1,0:T(8,128)(2,1)S(1)} %broadcast_select_fusion.4), channel_id=1, source_target_pairs={{0,4},{4,0},{1,5},{5,1},{2,6},{6,2},{3,7},{7,3},{8,12},{12,8},{9,1... | collective-permute-start | bytes 1572872 | tf_op jit(solution)/shard_map/ppermute | solution.py:14
  85.1 42.8 %copy-start.28 = (bf16[4,4,128,128]{3,2,1,0:T(8,128)(2,1)}, bf16[4,4,128,128]{3,2,1,0:T(8,128)(2,1)S(1)}, u32[]{:S(2)}) copy-start(bf16[4,4,128,128]{3,2,1,0:T(8,128)(2,1)S(1)} %collective-permute-done.24.refs_16_) | copy-start | bytes 1572868
  85.1 14.1 %collective-permute-start.29 = (bf16[4,4,128,128]{3,2,1,0:T(8,128)(2,1)}, bf16[4,4,128,128]{3,2,1,0:T(8,128)(2,1)S(1)}, u32[]{:S(2)}, u32[]{:S(2)}) collective-permute-start(bf16[4,4,128,128]{3,2,1,0:T(8,128)(2,1)} %collective-permute-done.11.refs_9_), channel_id=1, source_target_pairs={{0,4},{4,0},{1,5},{5,1},{2,6},{6,2},{3,7},{7,3},{8,12},{12,8},{9,1... | collective-permute-start | bytes 1572872 | tf_op jit(solution)/shard_map/ppermute | solution.py:14
  85.4 25.9 %copy-start.11 = (bf16[4,4,128,128]{3,2,1,0:T(8,128)(2,1)}, bf16[4,4,128,128]{3,2,1,0:T(8,128)(2,1)S(1)}, u32[]{:S(2)}) copy-start(bf16[4,4,128,128]{3,2,1,0:T(8,128)(2,1)S(1)} %collective-permute-done.23.refs_32_) | copy-start | bytes 1572868
  85.4 15.4 %collective-permute-start.28 = (bf16[4,4,128,128]{3,2,1,0:T(8,128)(2,1)S(1)}, bf16[4,4,128,128]{3,2,1,0:T(8,128)(2,1)S(1)}, u32[]{:S(2)}, u32[]{:S(2)}) collective-permute-start(bf16[4,4,128,128]{3,2,1,0:T(8,128)(2,1)S(1)} %collective-permute-done.17.refs_25_), channel_id=1, source_target_pairs={{0,16},{16,0},{8,24},{24,8},{1,17},{17,1},{9,25},{25,9},{2,18},{18... | collective-permute-start | bytes 1572872 | tf_op jit(solution)/shard_map/ppermute | solution.py:14
  86.9 13.8 %collective-permute-start.30 = (bf16[4,4,128,128]{3,2,1,0:T(8,128)(2,1)S(1)}, bf16[4,4,128,128]{3,2,1,0:T(8,128)(2,1)S(1)}, u32[]{:S(2)}, u32[]{:S(2)}) collective-permute-start(bf16[4,4,128,128]{3,2,1,0:T(8,128)(2,1)S(1)} %collective-permute-done.19.refs_11_), channel_id=1, source_target_pairs={{0,4},{4,0},{1,5},{5,1},{2,6},{6,2},{3,7},{7,3},{8,12},{12,8},{9,1... | collective-permute-start | bytes 1572872 | tf_op jit(solution)/shard_map/ppermute | solution.py:14
  97.8 15.7 %copy-start.12 = (bf16[4,4,128,128]{3,2,1,0:T(8,128)(2,1)}, bf16[4,4,128,128]{3,2,1,0:T(8,128)(2,1)S(1)}, u32[]{:S(2)}) copy-start(bf16[4,4,128,128]{3,2,1,0:T(8,128)(2,1)S(1)} %collective-permute-done.22.refs_26_) | copy-start | bytes 1572868
  97.8 13.5 %collective-permute-start.27 = (bf16[4,4,128,128]{3,2,1,0:T(8,128)(2,1)S(1)}, bf16[4,4,128,128]{3,2,1,0:T(8,128)(2,1)S(1)}, u32[]{:S(2)}, u32[]{:S(2)}) collective-permute-start(bf16[4,4,128,128]{3,2,1,0:T(8,128)(2,1)S(1)} %collective-permute-done.19.refs_11_), channel_id=1, source_target_pairs={{0,8},{8,0},{16,24},{24,16},{1,9},{9,1},{17,25},{25,17},{2,10},{10... | collective-permute-start | bytes 1572872 | tf_op jit(solution)/shard_map/ppermute | solution.py:14
  99.1 14.5 %copy-start.30 = (bf16[4,4,128,128]{3,2,1,0:T(8,128)(2,1)}, bf16[4,4,128,128]{3,2,1,0:T(8,128)(2,1)S(1)}, u32[]{:S(2)}) copy-start(bf16[4,4,128,128]{3,2,1,0:T(8,128)(2,1)S(1)} %collective-permute-done.31.refs_39_) | copy-start | bytes 1572868
  99.1 13.6 %collective-permute-start.33 = (bf16[4,4,128,128]{3,2,1,0:T(8,128)(2,1)S(1)}, bf16[4,4,128,128]{3,2,1,0:T(8,128)(2,1)S(1)}, u32[]{:S(2)}, u32[]{:S(2)}) collective-permute-start(bf16[4,4,128,128]{3,2,1,0:T(8,128)(2,1)S(1)} %broadcast_select_fusion.3), channel_id=1, source_target_pairs={{0,4},{4,0},{1,5},{5,1},{2,6},{6,2},{3,7},{7,3},{8,12},{12,8},{9,1... | collective-permute-start | bytes 1572872 | tf_op jit(solution)/shard_map/ppermute | solution.py:14
  99.2 28.7 %copy-start.31 = (bf16[4,4,128,128]{3,2,1,0:T(8,128)(2,1)}, bf16[4,4,128,128]{3,2,1,0:T(8,128)(2,1)S(1)}, u32[]{:S(2)}) copy-start(bf16[4,4,128,128]{3,2,1,0:T(8,128)(2,1)S(1)} %collective-permute-done.29.refs_17_) | copy-start | bytes 1572868
  99.2 14.3 %collective-permute-start.32 = (bf16[4,4,128,128]{3,2,1,0:T(8,128)(2,1)S(1)}, bf16[4,4,128,128]{3,2,1,0:T(8,128)(2,1)S(1)}, u32[]{:S(2)}, u32[]{:S(2)}) collective-permute-start(bf16[4,4,128,128]{3,2,1,0:T(8,128)(2,1)S(1)} %collective-permute-done.22.refs_26_), channel_id=1, source_target_pairs={{0,16},{16,0},{8,24},{24,8},{1,17},{17,1},{9,25},{25,9},{2,18},{18... | collective-permute-start | bytes 1572872 | tf_op jit(solution)/shard_map/ppermute | solution.py:14
  100.8 27.1 %copy-start.32 = (bf16[4,4,128,128]{3,2,1,0:T(8,128)(2,1)}, bf16[4,4,128,128]{3,2,1,0:T(8,128)(2,1)S(1)}, u32[]{:S(2)}) copy-start(bf16[4,4,128,128]{3,2,1,0:T(8,128)(2,1)S(1)} %collective-permute-done.30.refs_19_) | copy-start | bytes 1572868
  111.3 14.5 %copy-start.14 = (bf16[4,4,128,128]{3,2,1,0:T(8,128)(2,1)}, bf16[4,4,128,128]{3,2,1,0:T(8,128)(2,1)S(1)}, u32[]{:S(2)}) copy-start(bf16[4,4,128,128]{3,2,1,0:T(8,128)(2,1)S(1)} %collective-permute-done.27.refs_27_) | copy-start | bytes 1572868
  111.4 2.3 %collective-permute-start.35 = (bf16[4,4,128,128]{3,2,1,0:T(8,128)(2,1)S(1)}, bf16[4,4,128,128]{3,2,1,0:T(8,128)(2,1)S(1)}, u32[]{:S(2)}, u32[]{:S(2)}) collective-permute-start(bf16[4,4,128,128]{3,2,1,0:T(8,128)(2,1)S(1)} %broadcast_select_fusion.2), channel_id=1, source_target_pairs={{0,4},{4,0},{1,5},{5,1},{2,6},{6,2},{3,7},{7,3},{8,12},{12,8},{9,1... | collective-permute-start | bytes 1572872 | tf_op jit(solution)/shard_map/ppermute | solution.py:14
  111.4 14.3 %collective-permute-start.34 = (bf16[4,4,128,128]{3,2,1,0:T(8,128)(2,1)S(1)}, bf16[4,4,128,128]{3,2,1,0:T(8,128)(2,1)S(1)}, u32[]{:S(2)}, u32[]{:S(2)}) collective-permute-start(bf16[4,4,128,128]{3,2,1,0:T(8,128)(2,1)S(1)} %collective-permute-done.27.refs_27_), channel_id=1, source_target_pairs={{0,16},{16,0},{8,24},{24,8},{1,17},{17,1},{9,25},{25,9},{2,18},{18... | collective-permute-start | bytes 1572872 | tf_op jit(solution)/shard_map/ppermute | solution.py:14
  113.6 12.4 %collective-permute-start.36 = (bf16[4,4,128,128]{3,2,1,0:T(8,128)(2,1)S(1)}, bf16[4,4,128,128]{3,2,1,0:T(8,128)(2,1)S(1)}, u32[]{:S(2)}, u32[]{:S(2)}) collective-permute-start(bf16[4,4,128,128]{3,2,1,0:T(8,128)(2,1)S(1)} %broadcast_select_fusion.1), channel_id=1, source_target_pairs={{0,4},{4,0},{1,5},{5,1},{2,6},{6,2},{3,7},{7,3},{8,12},{12,8},{9,1... | collective-permute-start | bytes 1572872 | tf_op jit(solution)/shard_map/ppermute | solution.py:14
  125.9 2.0 %collective-permute-start.37 = (bf16[4,4,128,128]{3,2,1,0:T(8,128)(2,1)S(1)}, bf16[4,4,128,128]{3,2,1,0:T(8,128)(2,1)S(1)}, u32[]{:S(2)}, u32[]{:S(2)}) collective-permute-start(bf16[4,4,128,128]{3,2,1,0:T(8,128)(2,1)S(1)} %broadcast_select_fusion), channel_id=1, source_target_pairs={{0,4},{4,0},{1,5},{5,1},{2,6},{6,2},{3,7},{7,3},{8,12},{12,8},{9,1... | collective-permute-start | bytes 1572872 | tf_op jit(solution)/shard_map/ppermute | solution.py:14
  (12 other events, 90.6 us)

commit v5 on v4

--- a/solution.py
+++ b/solution.py
@@ -36,32 +36,36 @@
         return over_core(jnp.where(send_x, by_x, by_y))
 
     def round_one(own):
-        return together((own, along_x(own), along_z(own), over_core(own)))
-
-    def round_two(own, x0, p1, c0):
-        return own, c0, *together((x0, p1, along_x(p1), along_y(x0), along_z(p1)))
-
-    def round_three(own, c0, x0, p1, x1, y0, p2):
-        sent = along_x(p2), along_y(x1), along_z(p2), over_core(p1), shared(x0, y0)
-        return own, c0, x0, p1, y0, *together((x1, p2, *sent))
-
-    def round_four(own, c0, x0, p1, y0, x1, p2, x2, y1, p3, c1, s0):
-        sent = along_x(p3), along_y(x2), over_core(p2), over_core(p3), shared(x1, y1)
-        return own, c0, x0, p1, y0, x1, p2, y1, p3, c1, s0, *together((x2, *sent))
-
-    def round_five(own, c0, x0, p1, y0, x1, p2, y1, p3, c1, s0, x2, x3, y2, c2, c3, s1):
-        x3, y3, s2 = together((x3, along_y(x3), shared(x2, y2)))
-        s3 = shared(x3, y3)
-        pieces = own, p1, p2, p3
-        return pieces, (c0, c1, c2, c3), (x0, x1, x2, x3), (y0, y1, y2, y3), (s0, s1, s2, s3)
+        return together((own, along_x(own), along_z(own)))
+
+    def round_two(own, x0, p1):
+        return own, *together((x0, p1, along_x(p1), along_y(x0), along_z(p1)))
+
+    def round_three(own, x0, p1, x1, y0, p2):
+        sent = along_x(p2), along_y(x1), along_z(p2), shared(x0, y0)
+        return own, x0, p1, y0, *together((x1, p2, *sent))
+
+    def round_four(own, x0, p1, y0, x1, p2, x2, y1, p3, s0):
+        sent = along_x(p3), along_y(x2), shared(x1, y1), over_core(p1)
+        return own, x0, p1, y0, x1, y1, s0, *together((p2, p3, x2, *sent))
+
+    def round_five(own, x0, p1, y0, x1, y1, s0, p2, p3, x2, x3, y2, s1, c1):
+        sent = along_y(x3), shared(x2, y2), over_core(p2), over_core(p3)
+        x3, y3, s2, c2, c3 = together((x3, *sent))
+        x, y, s = (x0, x1, x2, x3), (y0, y1, y2, y3), (s0, s1, s2, shared(x3, y3))
+        return (own, p1, p2, p3), (c1, c2, c3), x, y, s
 
     half = own.shape[0] // 2
-    streams = [(own[:half],), (own[half:],)]
-    for one_round in (round_one, round_two, round_three, round_four, round_five):
+    streams = [round_one(own[:half]), round_one(own[half:])]
+    extra, streams[1] = together((extra, streams[1]))
+    for one_round in (round_two, round_three):
         streams = [one_round(*stream) for stream in streams]
-        if one_round is round_one:
-            extra, streams[1] = together((extra, streams[1]))
-    groups = [[(a, b) for a, b in zip(*both)] for both in zip(*streams)]
+    own, streams[0] = together((own, streams[0]))
+    c0 = over_core(own)
+    streams = [round_four(*stream) for stream in streams]
+    c0, streams[1] = together((c0, streams[1]))
+    groups = [list(zip(*parts)) for parts in zip(*[round_five(*one) for one in streams])]
+    groups[1].insert(0, (c0,))
     return groups, extra
 
 
@@ -84,14 +88,13 @@
     return line_window if sizes == (4, 2, 4) else ring_window
 
 
-def purify_kernel(piece_count, piece_rows, piece_slots, own_rows, out_slots, *refs):
+def purify_kernel(piece_count, own_rows, out_slots, *refs):
     place_ref, hole_ref, keep_ref, target_ref = refs[:4]
     piece_refs = refs[4 : 4 + piece_count]
     out_ref, panel, square, sem = refs[4 + piece_count :]
     window = own_rows + 2 * WIDE
     pairs = window // 2
     edge = out_ref.shape[-1]
-    per_piece = piece_rows * piece_slots
 
     zero = jnp.zeros((edge, edge), jnp.bfloat16)
 
@@ -114,11 +117,13 @@
             panel[spot] = zero
 
     started = jnp.int32(0)
-    for number, piece in enumerate(piece_refs):
-
-        def start(row, done, number=number, piece=piece):
+    first = 0
+    for piece in piece_refs:
+        piece_rows, piece_slots = piece.shape[:2]
+
+        def start(row, done, first=first, piece=piece, piece_slots=piece_slots):
             for slot in range(piece_slots):
-                spot = place_ref[number * per_piece + row * piece_slots + slot]
+                spot = place_ref[first + row * piece_slots + slot]
 
                 @pl.when(spot >= 0)
                 def _():
@@ -128,6 +133,7 @@
             return done
 
         started = lax.fori_loop(0, piece_rows, start, started)
+        first += piece_rows * piece_slots
 
     @pl.loop(0, square.shape[0])
     def _(spot):
@@ -240,9 +246,7 @@
 
     groups, tables = window_plan()(blocks, (spots, holes, keep, mine))
     flat = [part for group in groups for piece in group for part in piece]
-    kernel_body = lambda *refs: purify_kernel(
-        len(flat), flat[0].shape[0], slots, rows, out_slots, *refs
-    )
+    kernel_body = lambda *refs: purify_kernel(len(flat), rows, out_slots, *refs)
     smem = pl.BlockSpec(memory_space=pltpu.SMEM)
     hbm = pl.BlockSpec(memory_space=pl.ANY)
     return pl.pallas_call(

time: 161 us -> 160 us (level)
  waiting for transfers between devices: 83.9 us -> 80.9 us
  starting transfers between devices: 31.9 us -> 34.6 us
    ppermute x38 -> x37, waiting for transfers between devices: 83.9 us -> 80.9 us  [permuted(): return lax.ppermute(value, axes, pairs)]
    ppermute x38 -> x37, starting transfers between devices: 31.9 us -> 34.6 us  [permuted(): return lax.ppermute(value, axes, pairs)]
  transfers between devices with their start and end apart: 38 -> 37, of which waited for: 12 -> 17; matrix products, arithmetic and copies ran while one was open for 6% -> 6% of each run, Pallas kernels for 0% -> 0%
where the time goes in v5:
time: 160 us
  waiting for transfers between devices  80.9 us (51%)
  starting transfers between devices  34.6 us (22%)
  Pallas kernels  31.8 us (20%)
  local copies, waits for them, and re-layouts  9.5 us (6%)
  other arithmetic  2.14 us (1%)
    ppermute x37, waiting for transfers between devices, permuted(): return lax.ppermute(value, axes, pairs)  80.9 us
    ppermute x37, starting transfers between devices, permuted(): return lax.ppermute(value, axes, pairs)  34.6 us
    pallas_call x1, Pallas kernels, local(): pl.pallas_call(kernel_body, out_shape=jax.ShapeDtypeStruct((rows, out_slo...  31.8 us
    gather x1, local copies, waits for them, and re-layouts, local(): block_cols[row_ids[:, None, :, None] % order, slot_ids[None, :, None, :]]  4.57 us
  transfers between devices with their start and end apart: 37, of which 17 were waited for; matrix products, arithmetic and copies ran while one was open for 6% of the time, Pallas kernels for 0%

profile of v5, /device:TPU:0, one launch (start us, length us, event | category | flops | bytes accessed | tf_op | source)
XLA Modules:
  0.0 159.5 jit_solution(15747158501078054445)
XLA Ops:
  0.0 1.3 fusion.24
  1.4 3.1 %collective-permute-start.3 = (bf16[4,4,128,128]{3,2,1,0:T(8,128)(2,1)S(1)}, bf16[4,4,128,128]{3,2,1,0:T(8,128)(2,1)}, u32[]{:S(2)}, u32[]{:S(2)}) collective-permute-start(bf16[4,4,128,128]{3,2,1,0:T(8,128)(2,1)S(1)} %get-tuple-element.111.refs_4_), channel_id=1, source_target_pairs={{0,1},{1,2},{2,3},{3,0},{4,5},{5,6},{6,7},{7,4},{8,9},{9,10},{10,1... | collective-permute-start | bytes 1572872 | tf_op jit(solution)/shard_map/ppermute | solution.py:14
  4.4 1.5 collective-permute-start.2
  5.9 1.6 collective-permute-start.1
  7.5 0.5 collective-permute-start
  8.1 0.1 fusion
  8.2 0.1 constant_dynamic-slice_fusion
  8.2 0.7 reshape.222.refs_3_
  8.9 0.6 reshape.223.refs_2_
  9.6 0.1 copy.6
  9.7 0.1 broadcast_or_fusion
  9.8 0.1 reshape.224
  9.9 4.6 %gather_fusion = s32[640]{0:T(1024)S(1)} fusion(s32[64,16]{0,1:T(8,128)S(1)} %copy-done, s32[640]{0:T(1024)S(1)} %reshape.224), kind=kCustom, calls=%fused_computation | custom fusion | bytes 10240 | tf_op jit(solution)/shard_map/gather | solution.py:228
  14.5 0.1 add.343
  14.6 0.1 add.344
  14.7 0.6 gather_fusion.1
  15.3 4.0 %collective-permute-done.3.refs_6_ = bf16[4,4,128,128]{3,2,1,0:T(8,128)(2,1)} collective-permute-done((bf16[4,4,128,128]{3,2,1,0:T(8,128)(2,1)S(1)}, bf16[4,4,128,128]{3,2,1,0:T(8,128)(2,1)}, u32[]{:S(2)}, u32[]{:S(2)}) %collective-permute-start.3) | collective-permute-done | bytes 524320 | tf_op jit(solution)/shard_map/ppermute | solution.py:14
  19.3 1.5 collective-permute-start.6
  20.9 1.5 collective-permute-start.4
  22.4 1.5 collective-permute-start.5
  23.9 0.2 fusion.2
  24.1 0.6 compare_select_fusion.6.refs_1_
  24.7 0.6 fusion.11.refs_0_
  25.3 5.3 %collective-permute-done.1.refs_7_ = bf16[4,4,128,128]{3,2,1,0:T(8,128)(2,1)} collective-permute-done((bf16[4,4,128,128]{3,2,1,0:T(8,128)(2,1)S(1)}, bf16[4,4,128,128]{3,2,1,0:T(8,128)(2,1)}, u32[]{:S(2)}, u32[]{:S(2)}) %collective-permute-start.1) | collective-permute-done | bytes 524320 | tf_op jit(solution)/shard_map/ppermute | solution.py:14
  30.6 1.8 %collective-permute-start.13 = (bf16[4,4,128,128]{3,2,1,0:T(8,128)(2,1)S(1)}, bf16[4,4,128,128]{3,2,1,0:T(8,128)(2,1)S(1)}, u32[]{:S(2)}, u32[]{:S(2)}) collective-permute-start(bf16[4,4,128,128]{3,2,1,0:T(8,128)(2,1)S(1)} %collective-permute-done.refs_20_), channel_id=1, source_target_pairs={{0,16},{16,0},{8,24},{24,8},{1,17},{17,1},{9,25},{25,9},{2,18},{18... | collective-permute-start | bytes 1572872 | tf_op jit(solution)/shard_map/ppermute | solution.py:14
  32.3 1.3 collective-permute-start.14
  33.6 0.5 collective-permute-done.5.refs_27_
  34.1 1.0 collective-permute-start.12
  35.1 6.6 %collective-permute-done.6.refs_8_ = bf16[4,4,128,128]{3,2,1,0:T(8,128)(2,1)S(1)} collective-permute-done((bf16[4,4,128,128]{3,2,1,0:T(8,128)(2,1)}, bf16[4,4,128,128]{3,2,1,0:T(8,128)(2,1)S(1)}, u32[]{:S(2)}, u32[]{:S(2)}) %collective-permute-start.6) | collective-permute-done | bytes 524320 | tf_op jit(solution)/shard_map/ppermute | solution.py:14
  41.8 0.1 collective-permute-start.10
  41.9 1.8 %collective-permute-start.8 = (bf16[4,4,128,128]{3,2,1,0:T(8,128)(2,1)S(1)}, bf16[4,4,128,128]{3,2,1,0:T(8,128)(2,1)S(1)}, u32[]{:S(2)}, u32[]{:S(2)}) collective-permute-start(bf16[4,4,128,128]{3,2,1,0:T(8,128)(2,1)S(1)} %collective-permute-done.4.refs_21_), channel_id=1, source_target_pairs={{0,16},{16,0},{8,24},{24,8},{1,17},{17,1},{9,25},{25,9},{2,18},{18... | collective-permute-start | bytes 1572872 | tf_op jit(solution)/shard_map/ppermute | solution.py:14
  43.7 0.5 collective-permute-done.13.refs_28_
  44.1 1.6 collective-permute-start.9
  45.7 7.3 %collective-permute-done.14.refs_9_ = bf16[4,4,128,128]{3,2,1,0:T(8,128)(2,1)} collective-permute-done((bf16[4,4,128,128]{3,2,1,0:T(8,128)(2,1)}, bf16[4,4,128,128]{3,2,1,0:T(8,128)(2,1)}, u32[]{:S(2)}, u32[]{:S(2)}) %collective-permute-start.14) | collective-permute-done | bytes 524320 | tf_op jit(solution)/shard_map/ppermute | solution.py:14
  53.0 1.7 %collective-permute-start.7 = (bf16[4,4,128,128]{3,2,1,0:T(8,128)(2,1)S(1)}, bf16[4,4,128,128]{3,2,1,0:T(8,128)(2,1)S(1)}, u32[]{:S(2)}, u32[]{:S(2)}) collective-permute-start(bf16[4,4,128,128]{3,2,1,0:T(8,128)(2,1)S(1)} %collective-permute-done.6.refs_8_), channel_id=1, source_target_pairs={{0,8},{8,0},{16,24},{24,16},{1,9},{9,1},{17,25},{25,17},{2,10},{10... | collective-permute-start | bytes 1572872 | tf_op jit(solution)/shard_map/ppermute | solution.py:14
  55.0 1.6 collective-permute-start.16
  56.5 1.3 collective-permute-start.17
  57.8 6.3 %collective-permute-done.9.refs_10_ = bf16[4,4,128,128]{3,2,1,0:T(8,128)(2,1)S(1)} collective-permute-done((bf16[4,4,128,128]{3,2,1,0:T(8,128)(2,1)S(1)}, bf16[4,4,128,128]{3,2,1,0:T(8,128)(2,1)S(1)}, u32[]{:S(2)}, u32[]{:S(2)}) %collective-permute-start.9) | collective-permute-done | bytes 524320 | tf_op jit(solution)/shard_map/ppermute | solution.py:14
  64.2 1.7 %collective-permute-start.15 = (bf16[4,4,128,128]{3,2,1,0:T(8,128)(2,1)}, bf16[4,4,128,128]{3,2,1,0:T(8,128)(2,1)S(1)}, u32[]{:S(2)}, u32[]{:S(2)}) collective-permute-start(bf16[4,4,128,128]{3,2,1,0:T(8,128)(2,1)} %collective-permute-done.14.refs_9_), channel_id=1, source_target_pairs={{0,8},{8,0},{16,24},{24,16},{1,9},{9,1},{17,25},{25,17},{2,10},{10... | collective-permute-start | bytes 1572872 | tf_op jit(solution)/shard_map/ppermute | solution.py:14
  65.9 0.1 broadcast_select_fusion.4
  66.1 0.5 collective-permute-start.26
  66.6 0.3 copy-done.24
  66.9 2.4 %collective-permute-done.16.refs_30_ = bf16[4,4,128,128]{3,2,1,0:T(8,128)(2,1)S(1)} collective-permute-done((bf16[4,4,128,128]{3,2,1,0:T(8,128)(2,1)S(1)}, bf16[4,4,128,128]{3,2,1,0:T(8,128)(2,1)S(1)}, u32[]{:S(2)}, u32[]{:S(2)}) %collective-permute-start.16) | collective-permute-done | bytes 524320 | tf_op jit(solution)/shard_map/ppermute | solution.py:14
  69.3 0.3 collective-permute-start.23
  69.6 5.0 %collective-permute-done.17.refs_11_ = bf16[4,4,128,128]{3,2,1,0:T(8,128)(2,1)S(1)} collective-permute-done((bf16[4,4,128,128]{3,2,1,0:T(8,128)(2,1)}, bf16[4,4,128,128]{3,2,1,0:T(8,128)(2,1)S(1)}, u32[]{:S(2)}, u32[]{:S(2)}) %collective-permute-start.17) | collective-permute-done | bytes 524320 | tf_op jit(solution)/shard_map/ppermute | solution.py:14
  74.6 1.5 collective-permute-start.24
  76.1 3.1 %collective-permute-done.15.refs_24_ = bf16[4,4,128,128]{3,2,1,0:T(8,128)(2,1)S(1)} collective-permute-done((bf16[4,4,128,128]{3,2,1,0:T(8,128)(2,1)}, bf16[4,4,128,128]{3,2,1,0:T(8,128)(2,1)S(1)}, u32[]{:S(2)}, u32[]{:S(2)}) %collective-permute-start.15) | collective-permute-done | bytes 524320 | tf_op jit(solution)/shard_map/ppermute | solution.py:14
  79.4 0.6 collective-permute-start.22
  79.9 0.1 collective-permute-start.21
  80.0 7.9 %collective-permute-done.23.refs_25_ = bf16[4,4,128,128]{3,2,1,0:T(8,128)(2,1)S(1)} collective-permute-done((bf16[4,4,128,128]{3,2,1,0:T(8,128)(2,1)S(1)}, bf16[4,4,128,128]{3,2,1,0:T(8,128)(2,1)S(1)}, u32[]{:S(2)}, u32[]{:S(2)}) %collective-permute-start.23) | collective-permute-done | bytes 524320 | tf_op jit(solution)/shard_map/ppermute | solution.py:14
  87.9 1.5 collective-permute-start.19
  89.4 1.5 collective-permute-start.20
  91.2 0.5 collective-permute-start.29
  91.7 7.6 %collective-permute-done.19.refs_26_ = bf16[4,4,128,128]{3,2,1,0:T(8,128)(2,1)S(1)} collective-permute-done((bf16[4,4,128,128]{3,2,1,0:T(8,128)(2,1)S(1)}, bf16[4,4,128,128]{3,2,1,0:T(8,128)(2,1)S(1)}, u32[]{:S(2)}, u32[]{:S(2)}) %collective-permute-start.19) | collective-permute-done | bytes 524320 | tf_op jit(solution)/shard_map/ppermute | solution.py:14
  99.3 0.6 collective-permute-done.20.refs_32_
  99.9 1.4 collective-permute-start.27
  101.4 0.5 collective-permute-start.33
  101.9 0.2 collective-permute-start.34
  102.1 0.6 collective-permute-start.31
  102.7 11.9 %collective-permute-done.27.refs_33_ = bf16[4,4,128,128]{3,2,1,0:T(8,128)(2,1)S(1)} collective-permute-done((bf16[4,4,128,128]{3,2,1,0:T(8,128)(2,1)S(1)}, bf16[4,4,128,128]{3,2,1,0:T(8,128)(2,1)S(1)}, u32[]{:S(2)}, u32[]{:S(2)}) %collective-permute-start.27) | collective-permute-done | bytes 524320 | tf_op jit(solution)/shard_map/ppermute | solution.py:14
  114.9 9.9 %collective-permute-done.31.refs_34_ = bf16[4,4,128,128]{3,2,1,0:T(8,128)(2,1)S(1)} collective-permute-done((bf16[4,4,128,128]{3,2,1,0:T(8,128)(2,1)S(1)}, bf16[4,4,128,128]{3,2,1,0:T(8,128)(2,1)S(1)}, u32[]{:S(2)}, u32[]{:S(2)}) %collective-permute-start.31) | collective-permute-done | bytes 524320 | tf_op jit(solution)/shard_map/ppermute | solution.py:14
  125.0 1.8 %collective-permute-done.36.refs_42_ = bf16[4,4,128,128]{3,2,1,0:T(8,128)(2,1)S(1)} collective-permute-done((bf16[4,4,128,128]{3,2,1,0:T(8,128)(2,1)S(1)}, bf16[4,4,128,128]{3,2,1,0:T(8,128)(2,1)S(1)}, u32[]{:S(2)}, u32[]{:S(2)}) %collective-permute-start.36) | collective-permute-done | bytes 524320 | tf_op jit(solution)/shard_map/ppermute | solution.py:14
  127.0 0.8 copy-done.37
  127.7 31.8 %purify.1 = bf16[8,6,128,128]{3,2,1,0:T(8,128)(2,1)} custom-call(s32[640]{0:T(1024)} %fusion.11.refs_0_, s32[40]{0:T(128)} %compare_select_fusion.6.refs_1_, s32[320]{0:T(512)} %reshape.223.refs_2_, s32[48]{0:T(128)} %reshape.222.refs_3_, bf16[4,4,128,128]{3,2,1,0:T(8,128)(2,1)} %copy-done.17, bf16[4,4,128,128]{3,2,1,0:T(8,128)(2,1)} %copy-done.18, ...), custom_call_target="tpu_custom_call" | custom-call | tf_op jit(solution)/shard_map/purify/pallas_call | solution.py:252
  (125 shorter events, 1.2 us)
Async XLA Ops:
  1.3 13.2 %copy-start.17 = (bf16[4,4,128,128]{3,2,1,0:T(8,128)(2,1)}, bf16[4,4,128,128]{3,2,1,0:T(8,128)(2,1)S(1)}, u32[]{:S(2)}) copy-start(bf16[4,4,128,128]{3,2,1,0:T(8,128)(2,1)S(1)} %get-tuple-element.111.refs_4_) | copy-start | bytes 1572868
  1.4 18.0 %collective-permute-start.3 = (bf16[4,4,128,128]{3,2,1,0:T(8,128)(2,1)S(1)}, bf16[4,4,128,128]{3,2,1,0:T(8,128)(2,1)}, u32[]{:S(2)}, u32[]{:S(2)}) collective-permute-start(bf16[4,4,128,128]{3,2,1,0:T(8,128)(2,1)S(1)} %get-tuple-element.111.refs_4_), channel_id=1, source_target_pairs={{0,1},{1,2},{2,3},{3,0},{4,5},{5,6},{6,7},{7,4},{8,9},{9,10},{10,1... | collective-permute-start | bytes 1572872 | tf_op jit(solution)/shard_map/ppermute | solution.py:14
  4.4 14.9 %collective-permute-start.2 = (bf16[4,4,128,128]{3,2,1,0:T(8,128)(2,1)S(1)}, bf16[4,4,128,128]{3,2,1,0:T(8,128)(2,1)S(1)}, u32[]{:S(2)}, u32[]{:S(2)}) collective-permute-start(bf16[4,4,128,128]{3,2,1,0:T(8,128)(2,1)S(1)} %get-tuple-element.111.refs_4_), channel_id=1, source_target_pairs={{0,8},{8,0},{16,24},{24,16},{1,9},{9,1},{17,25},{25,17},{2,10},{10... | collective-permute-start | bytes 1572872 | tf_op jit(solution)/shard_map/ppermute | solution.py:14
  5.9 24.6 %collective-permute-start.1 = (bf16[4,4,128,128]{3,2,1,0:T(8,128)(2,1)S(1)}, bf16[4,4,128,128]{3,2,1,0:T(8,128)(2,1)}, u32[]{:S(2)}, u32[]{:S(2)}) collective-permute-start(bf16[4,4,128,128]{3,2,1,0:T(8,128)(2,1)S(1)} %get-tuple-element.134.refs_5_), channel_id=1, source_target_pairs={{0,1},{1,2},{2,3},{3,0},{4,5},{5,6},{6,7},{7,4},{8,9},{9,10},{10,1... | collective-permute-start | bytes 1572872 | tf_op jit(solution)/shard_map/ppermute | solution.py:14
  7.5 23.1 %collective-permute-start = (bf16[4,4,128,128]{3,2,1,0:T(8,128)(2,1)S(1)}, bf16[4,4,128,128]{3,2,1,0:T(8,128)(2,1)S(1)}, u32[]{:S(2)}, u32[]{:S(2)}) collective-permute-start(bf16[4,4,128,128]{3,2,1,0:T(8,128)(2,1)S(1)} %get-tuple-element.134.refs_5_), channel_id=1, source_target_pairs={{0,8},{8,0},{16,24},{24,16},{1,9},{9,1},{17,25},{25,17},{2,10},{10... | collective-permute-start | bytes 1572872 | tf_op jit(solution)/shard_map/ppermute | solution.py:14
  19.3 35.5 %copy-start.1 = (bf16[4,4,128,128]{3,2,1,0:T(8,128)(2,1)}, bf16[4,4,128,128]{3,2,1,0:T(8,128)(2,1)S(1)}, u32[]{:S(2)}) copy-start(bf16[4,4,128,128]{3,2,1,0:T(8,128)(2,1)S(1)} %collective-permute-done.2.refs_19_) | copy-start | bytes 1572868
  19.3 22.4 %collective-permute-start.6 = (bf16[4,4,128,128]{3,2,1,0:T(8,128)(2,1)}, bf16[4,4,128,128]{3,2,1,0:T(8,128)(2,1)S(1)}, u32[]{:S(2)}, u32[]{:S(2)}) collective-permute-start(bf16[4,4,128,128]{3,2,1,0:T(8,128)(2,1)} %collective-permute-done.3.refs_6_), channel_id=1, source_target_pairs={{0,1},{1,2},{2,3},{3,0},{4,5},{5,6},{6,7},{7,4},{8,9},{9,10},{10,1... | collective-permute-start | bytes 1572872 | tf_op jit(solution)/shard_map/ppermute | solution.py:14
  20.9 20.9 %collective-permute-start.4 = (bf16[4,4,128,128]{3,2,1,0:T(8,128)(2,1)}, bf16[4,4,128,128]{3,2,1,0:T(8,128)(2,1)S(1)}, u32[]{:S(2)}, u32[]{:S(2)}) collective-permute-start(bf16[4,4,128,128]{3,2,1,0:T(8,128)(2,1)} %collective-permute-done.3.refs_6_), channel_id=1, source_target_pairs={{0,8},{8,0},{16,24},{24,16},{1,9},{9,1},{17,25},{25,17},{2,10},{10... | collective-permute-start | bytes 1572872 | tf_op jit(solution)/shard_map/ppermute | solution.py:14
  22.4 11.8 %collective-permute-start.5 = (bf16[4,4,128,128]{3,2,1,0:T(8,128)(2,1)S(1)}, bf16[4,4,128,128]{3,2,1,0:T(8,128)(2,1)S(1)}, u32[]{:S(2)}, u32[]{:S(2)}) collective-permute-start(bf16[4,4,128,128]{3,2,1,0:T(8,128)(2,1)S(1)} %collective-permute-done.2.refs_19_), channel_id=1, source_target_pairs={{0,16},{16,0},{8,24},{24,8},{1,17},{17,1},{9,25},{25,9},{2,18},{18... | collective-permute-start | bytes 1572872 | tf_op jit(solution)/shard_map/ppermute | solution.py:14
  30.6 24.3 %copy-start.2 = (bf16[4,4,128,128]{3,2,1,0:T(8,128)(2,1)}, bf16[4,4,128,128]{3,2,1,0:T(8,128)(2,1)S(1)}, u32[]{:S(2)}) copy-start(bf16[4,4,128,128]{3,2,1,0:T(8,128)(2,1)S(1)} %collective-permute-done.refs_20_) | copy-start | bytes 1572868
  30.6 13.6 %collective-permute-start.13 = (bf16[4,4,128,128]{3,2,1,0:T(8,128)(2,1)S(1)}, bf16[4,4,128,128]{3,2,1,0:T(8,128)(2,1)S(1)}, u32[]{:S(2)}, u32[]{:S(2)}) collective-permute-start(bf16[4,4,128,128]{3,2,1,0:T(8,128)(2,1)S(1)} %collective-permute-done.refs_20_), channel_id=1, source_target_pairs={{0,16},{16,0},{8,24},{24,8},{1,17},{17,1},{9,25},{25,9},{2,18},{18... | collective-permute-start | bytes 1572872 | tf_op jit(solution)/shard_map/ppermute | solution.py:14
  32.3 20.7 %collective-permute-start.14 = (bf16[4,4,128,128]{3,2,1,0:T(8,128)(2,1)}, bf16[4,4,128,128]{3,2,1,0:T(8,128)(2,1)}, u32[]{:S(2)}, u32[]{:S(2)}) collective-permute-start(bf16[4,4,128,128]{3,2,1,0:T(8,128)(2,1)} %collective-permute-done.1.refs_7_), channel_id=1, source_target_pairs={{0,1},{1,2},{2,3},{3,0},{4,5},{5,6},{6,7},{7,4},{8,9},{9,10},{10,1... | collective-permute-start | bytes 1572872 | tf_op jit(solution)/shard_map/ppermute | solution.py:14
  34.1 20.7 %copy-start.4 = (bf16[4,4,128,128]{3,2,1,0:T(8,128)(2,1)}, bf16[4,4,128,128]{3,2,1,0:T(8,128)(2,1)S(1)}, u32[]{:S(2)}) copy-start(bf16[4,4,128,128]{3,2,1,0:T(8,128)(2,1)S(1)} %collective-permute-done.5.refs_27_) | copy-start | bytes 1572868
  34.1 20.6 %collective-permute-start.12 = (bf16[4,4,128,128]{3,2,1,0:T(8,128)(2,1)}, bf16[4,4,128,128]{3,2,1,0:T(8,128)(2,1)S(1)}, u32[]{:S(2)}, u32[]{:S(2)}) collective-permute-start(bf16[4,4,128,128]{3,2,1,0:T(8,128)(2,1)} %collective-permute-done.1.refs_7_), channel_id=1, source_target_pairs={{0,8},{8,0},{16,24},{24,16},{1,9},{9,1},{17,25},{25,17},{2,10},{10... | collective-permute-start | bytes 1572872 | tf_op jit(solution)/shard_map/ppermute | solution.py:14
  41.7 49.5 %copy-start.21 = (bf16[4,4,128,128]{3,2,1,0:T(8,128)(2,1)}, bf16[4,4,128,128]{3,2,1,0:T(8,128)(2,1)S(1)}, u32[]{:S(2)}) copy-start(bf16[4,4,128,128]{3,2,1,0:T(8,128)(2,1)S(1)} %collective-permute-done.6.refs_8_) | copy-start | bytes 1572868
  41.8 24.1 %copy-start.3 = (bf16[4,4,128,128]{3,2,1,0:T(8,128)(2,1)}, bf16[4,4,128,128]{3,2,1,0:T(8,128)(2,1)S(1)}, u32[]{:S(2)}) copy-start(bf16[4,4,128,128]{3,2,1,0:T(8,128)(2,1)S(1)} %collective-permute-done.4.refs_21_) | copy-start | bytes 1572868
  41.8 37.4 %copy-start.20 = (bf16[8,4,128,128]{3,2,1,0:T(8,128)(2,1)S(1)}, bf16[8,4,128,128]{3,2,1,0:T(8,128)(2,1)}, u32[]{:S(2)}) copy-start(bf16[8,4,128,128]{3,2,1,0:T(8,128)(2,1)} %param.3) | copy-start | bytes 3145732
  41.8 13.1 %collective-permute-start.10 = (bf16[4,4,128,128]{3,2,1,0:T(8,128)(2,1)S(1)}, bf16[4,4,128,128]{3,2,1,0:T(8,128)(2,1)S(1)}, u32[]{:S(2)}, u32[]{:S(2)}) collective-permute-start(bf16[4,4,128,128]{3,2,1,0:T(8,128)(2,1)S(1)} %broadcast_select_fusion.7), channel_id=1, source_target_pairs={{0,4},{4,0},{1,5},{5,1},{2,6},{6,2},{3,7},{7,3},{8,12},{12,8},{9,1... | collective-permute-start | bytes 1572872 | tf_op jit(solution)/shard_map/ppermute | solution.py:14
  41.9 14.6 %collective-permute-start.8 = (bf16[4,4,128,128]{3,2,1,0:T(8,128)(2,1)S(1)}, bf16[4,4,128,128]{3,2,1,0:T(8,128)(2,1)S(1)}, u32[]{:S(2)}, u32[]{:S(2)}) collective-permute-start(bf16[4,4,128,128]{3,2,1,0:T(8,128)(2,1)S(1)} %collective-permute-done.4.refs_21_), channel_id=1, source_target_pairs={{0,16},{16,0},{8,24},{24,8},{1,17},{17,1},{9,25},{25,9},{2,18},{18... | collective-permute-start | bytes 1572872 | tf_op jit(solution)/shard_map/ppermute | solution.py:14
  44.1 21.8 %copy-start.5 = (bf16[4,4,128,128]{3,2,1,0:T(8,128)(2,1)}, bf16[4,4,128,128]{3,2,1,0:T(8,128)(2,1)S(1)}, u32[]{:S(2)}) copy-start(bf16[4,4,128,128]{3,2,1,0:T(8,128)(2,1)S(1)} %collective-permute-done.13.refs_28_) | copy-start | bytes 1572868
  44.1 20.0 %collective-permute-start.9 = (bf16[4,4,128,128]{3,2,1,0:T(8,128)(2,1)S(1)}, bf16[4,4,128,128]{3,2,1,0:T(8,128)(2,1)S(1)}, u32[]{:S(2)}, u32[]{:S(2)}) collective-permute-start(bf16[4,4,128,128]{3,2,1,0:T(8,128)(2,1)S(1)} %collective-permute-done.6.refs_8_), channel_id=1, source_target_pairs={{0,1},{1,2},{2,3},{3,0},{4,5},{5,6},{6,7},{7,4},{8,9},{9,10},{10,1... | collective-permute-start | bytes 1572872 | tf_op jit(solution)/shard_map/ppermute | solution.py:14
  53.0 12.9 %collective-permute-start.7 = (bf16[4,4,128,128]{3,2,1,0:T(8,128)(2,1)S(1)}, bf16[4,4,128,128]{3,2,1,0:T(8,128)(2,1)S(1)}, u32[]{:S(2)}, u32[]{:S(2)}) collective-permute-start(bf16[4,4,128,128]{3,2,1,0:T(8,128)(2,1)S(1)} %collective-permute-done.6.refs_8_), channel_id=1, source_target_pairs={{0,8},{8,0},{16,24},{24,16},{1,9},{9,1},{17,25},{25,17},{2,10},{10... | collective-permute-start | bytes 1572872 | tf_op jit(solution)/shard_map/ppermute | solution.py:14
  54.8 24.5 %copy-start.6 = (bf16[4,4,128,128]{3,2,1,0:T(8,128)(2,1)}, bf16[4,4,128,128]{3,2,1,0:T(8,128)(2,1)S(1)}, u32[]{:S(2)}) copy-start(bf16[4,4,128,128]{3,2,1,0:T(8,128)(2,1)S(1)} %collective-permute-done.12.refs_22_) | copy-start | bytes 1572868
  54.9 11.2 %collective-permute-start.18 = (bf16[4,4,128,128]{3,2,1,0:T(8,128)(2,1)S(1)}, bf16[4,4,128,128]{3,2,1,0:T(8,128)(2,1)S(1)}, u32[]{:S(2)}, u32[]{:S(2)}) collective-permute-start(bf16[4,4,128,128]{3,2,1,0:T(8,128)(2,1)S(1)} %broadcast_select_fusion.6), channel_id=1, source_target_pairs={{0,4},{4,0},{1,5},{5,1},{2,6},{6,2},{3,7},{7,3},{8,12},{12,8},{9,1... | collective-permute-start | bytes 1572872 | tf_op jit(solution)/shard_map/ppermute | solution.py:14
  54.9 24.4 %copy-start.22 = (bf16[4,4,128,128]{3,2,1,0:T(8,128)(2,1)}, bf16[4,4,128,128]{3,2,1,0:T(8,128)(2,1)S(1)}, u32[]{:S(2)}) copy-start(bf16[4,4,128,128]{3,2,1,0:T(8,128)(2,1)S(1)} %collective-permute-done.10.refs_35_) | copy-start | bytes 1572868
  55.0 14.3 %collective-permute-start.16 = (bf16[4,4,128,128]{3,2,1,0:T(8,128)(2,1)S(1)}, bf16[4,4,128,128]{3,2,1,0:T(8,128)(2,1)S(1)}, u32[]{:S(2)}, u32[]{:S(2)}) collective-permute-start(bf16[4,4,128,128]{3,2,1,0:T(8,128)(2,1)S(1)} %collective-permute-done.12.refs_22_), channel_id=1, source_target_pairs={{0,16},{16,0},{8,24},{24,8},{1,17},{17,1},{9,25},{25,9},{2,18},{18... | collective-permute-start | bytes 1572872 | tf_op jit(solution)/shard_map/ppermute | solution.py:14
  56.5 22.8 %copy-start.7 = (bf16[4,4,128,128]{3,2,1,0:T(8,128)(2,1)}, bf16[4,4,128,128]{3,2,1,0:T(8,128)(2,1)S(1)}, u32[]{:S(2)}) copy-start(bf16[4,4,128,128]{3,2,1,0:T(8,128)(2,1)S(1)} %collective-permute-done.8.refs_29_) | copy-start | bytes 1572868
  56.5 18.0 %collective-permute-start.17 = (bf16[4,4,128,128]{3,2,1,0:T(8,128)(2,1)}, bf16[4,4,128,128]{3,2,1,0:T(8,128)(2,1)S(1)}, u32[]{:S(2)}, u32[]{:S(2)}) collective-permute-start(bf16[4,4,128,128]{3,2,1,0:T(8,128)(2,1)} %collective-permute-done.14.refs_9_), channel_id=1, source_target_pairs={{0,1},{1,2},{2,3},{3,0},{4,5},{5,6},{6,7},{7,4},{8,9},{9,10},{10,1... | collective-permute-start | bytes 1572872 | tf_op jit(solution)/shard_map/ppermute | solution.py:14
  64.2 35.1 %copy-start.23 = (bf16[4,4,128,128]{3,2,1,0:T(8,128)(2,1)}, bf16[4,4,128,128]{3,2,1,0:T(8,128)(2,1)S(1)}, u32[]{:S(2)}) copy-start(bf16[4,4,128,128]{3,2,1,0:T(8,128)(2,1)S(1)} %collective-permute-done.9.refs_10_) | copy-start | bytes 1572868
  64.2 15.1 %collective-permute-start.15 = (bf16[4,4,128,128]{3,2,1,0:T(8,128)(2,1)}, bf16[4,4,128,128]{3,2,1,0:T(8,128)(2,1)S(1)}, u32[]{:S(2)}, u32[]{:S(2)}) collective-permute-start(bf16[4,4,128,128]{3,2,1,0:T(8,128)(2,1)} %collective-permute-done.14.refs_9_), channel_id=1, source_target_pairs={{0,8},{8,0},{16,24},{24,16},{1,9},{9,1},{17,25},{25,17},{2,10},{10... | collective-permute-start | bytes 1572872 | tf_op jit(solution)/shard_map/ppermute | solution.py:14
  65.9 25.1 %copy-start.8 = (bf16[4,4,128,128]{3,2,1,0:T(8,128)(2,1)}, bf16[4,4,128,128]{3,2,1,0:T(8,128)(2,1)S(1)}, u32[]{:S(2)}) copy-start(bf16[4,4,128,128]{3,2,1,0:T(8,128)(2,1)S(1)} %collective-permute-done.7.refs_23_) | copy-start | bytes 1572868
  66.0 13.3 %collective-permute-start.25 = (bf16[4,4,128,128]{3,2,1,0:T(8,128)(2,1)S(1)}, bf16[4,4,128,128]{3,2,1,0:T(8,128)(2,1)S(1)}, u32[]{:S(2)}, u32[]{:S(2)}) collective-permute-start(bf16[4,4,128,128]{3,2,1,0:T(8,128)(2,1)S(1)} %broadcast_select_fusion.4), channel_id=1, source_target_pairs={{0,4},{4,0},{1,5},{5,1},{2,6},{6,2},{3,7},{7,3},{8,12},{12,8},{9,1... | collective-permute-start | bytes 1572872 | tf_op jit(solution)/shard_map/ppermute | solution.py:14
  66.1 13.8 %collective-permute-start.26 = (bf16[4,4,128,128]{3,2,1,0:T(8,128)(2,1)}, bf16[4,4,128,128]{3,2,1,0:T(8,128)(2,1)S(1)}, u32[]{:S(2)}, u32[]{:S(2)}) collective-permute-start(bf16[4,4,128,128]{3,2,1,0:T(8,128)(2,1)} %collective-permute-done.3.refs_6_), channel_id=1, source_target_pairs={{0,4},{4,0},{1,5},{5,1},{2,6},{6,2},{3,7},{7,3},{8,12},{12,8},{9,1... | collective-permute-start | bytes 1572872 | tf_op jit(solution)/shard_map/ppermute | solution.py:14
  69.3 21.7 %copy-start.9 = (bf16[4,4,128,128]{3,2,1,0:T(8,128)(2,1)}, bf16[4,4,128,128]{3,2,1,0:T(8,128)(2,1)S(1)}, u32[]{:S(2)}) copy-start(bf16[4,4,128,128]{3,2,1,0:T(8,128)(2,1)S(1)} %collective-permute-done.16.refs_30_) | copy-start | bytes 1572868
  69.3 18.6 %collective-permute-start.23 = (bf16[4,4,128,128]{3,2,1,0:T(8,128)(2,1)S(1)}, bf16[4,4,128,128]{3,2,1,0:T(8,128)(2,1)S(1)}, u32[]{:S(2)}, u32[]{:S(2)}) collective-permute-start(bf16[4,4,128,128]{3,2,1,0:T(8,128)(2,1)S(1)} %collective-permute-done.9.refs_10_), channel_id=1, source_target_pairs={{0,8},{8,0},{16,24},{24,16},{1,9},{9,1},{17,25},{25,17},{2,10},{10... | collective-permute-start | bytes 1572872 | tf_op jit(solution)/shard_map/ppermute | solution.py:14
  74.6 27.4 %copy-start.25 = (bf16[4,4,128,128]{3,2,1,0:T(8,128)(2,1)}, bf16[4,4,128,128]{3,2,1,0:T(8,128)(2,1)S(1)}, u32[]{:S(2)}) copy-start(bf16[4,4,128,128]{3,2,1,0:T(8,128)(2,1)S(1)} %collective-permute-done.17.refs_11_) | copy-start | bytes 1572868
  74.6 14.9 %collective-permute-start.24 = (bf16[4,4,128,128]{3,2,1,0:T(8,128)(2,1)S(1)}, bf16[4,4,128,128]{3,2,1,0:T(8,128)(2,1)S(1)}, u32[]{:S(2)}, u32[]{:S(2)}) collective-permute-start(bf16[4,4,128,128]{3,2,1,0:T(8,128)(2,1)S(1)} %collective-permute-done.7.refs_23_), channel_id=1, source_target_pairs={{0,16},{16,0},{8,24},{24,8},{1,17},{17,1},{9,25},{25,9},{2,18},{18... | collective-permute-start | bytes 1572872 | tf_op jit(solution)/shard_map/ppermute | solution.py:14
  79.2 22.0 %copy-start.10 = (bf16[4,4,128,128]{3,2,1,0:T(8,128)(2,1)}, bf16[4,4,128,128]{3,2,1,0:T(8,128)(2,1)S(1)}, u32[]{:S(2)}) copy-start(bf16[4,4,128,128]{3,2,1,0:T(8,128)(2,1)S(1)} %collective-permute-done.15.refs_24_) | copy-start | bytes 1572868
  79.2 22.0 %collective-permute-start.11 = (bf16[8,4,128,128]{3,2,1,0:T(8,128)(2,1)S(1)}, bf16[8,4,128,128]{3,2,1,0:T(8,128)(2,1)S(1)}, u32[]{:S(2)}, u32[]{:S(2)}) collective-permute-start(bf16[8,4,128,128]{3,2,1,0:T(8,128)(2,1)S(1)} %copy-done.20), channel_id=1, source_target_pairs={{0,4},{4,0},{1,5},{5,1},{2,6},{6,2},{3,7},{7,3},{8,12},{12,8},{9,1... | collective-permute-start | bytes 3145736 | tf_op jit(solution)/shard_map/ppermute | solution.py:14
  79.3 22.0 %copy-start.26 = (bf16[4,4,128,128]{3,2,1,0:T(8,128)(2,1)}, bf16[4,4,128,128]{3,2,1,0:T(8,128)(2,1)S(1)}, u32[]{:S(2)}) copy-start(bf16[4,4,128,128]{3,2,1,0:T(8,128)(2,1)S(1)} %collective-permute-done.25.refs_37_) | copy-start | bytes 1572868
  79.4 11.7 %collective-permute-start.22 = (bf16[4,4,128,128]{3,2,1,0:T(8,128)(2,1)}, bf16[4,4,128,128]{3,2,1,0:T(8,128)(2,1)S(1)}, u32[]{:S(2)}, u32[]{:S(2)}) collective-permute-start(bf16[4,4,128,128]{3,2,1,0:T(8,128)(2,1)} %collective-permute-done.1.refs_7_), channel_id=1, source_target_pairs={{0,4},{4,0},{1,5},{5,1},{2,6},{6,2},{3,7},{7,3},{8,12},{12,8},{9,1... | collective-permute-start | bytes 1572872 | tf_op jit(solution)/shard_map/ppermute | solution.py:14
  79.9 47.0 %copy-start.27 = (bf16[4,4,128,128]{3,2,1,0:T(8,128)(2,1)}, bf16[4,4,128,128]{3,2,1,0:T(8,128)(2,1)S(1)}, u32[]{:S(2)}) copy-start(bf16[4,4,128,128]{3,2,1,0:T(8,128)(2,1)S(1)} %collective-permute-done.26.refs_13_) | copy-start | bytes 1572868
  79.9 11.2 %collective-permute-start.21 = (bf16[4,4,128,128]{3,2,1,0:T(8,128)(2,1)S(1)}, bf16[4,4,128,128]{3,2,1,0:T(8,128)(2,1)S(1)}, u32[]{:S(2)}, u32[]{:S(2)}) collective-permute-start(bf16[4,4,128,128]{3,2,1,0:T(8,128)(2,1)S(1)} %broadcast_select_fusion.5), channel_id=1, source_target_pairs={{0,4},{4,0},{1,5},{5,1},{2,6},{6,2},{3,7},{7,3},{8,12},{12,8},{9,1... | collective-permute-start | bytes 1572872 | tf_op jit(solution)/shard_map/ppermute | solution.py:14
  87.9 26.8 %copy-start.11 = (bf16[4,4,128,128]{3,2,1,0:T(8,128)(2,1)}, bf16[4,4,128,128]{3,2,1,0:T(8,128)(2,1)S(1)}, u32[]{:S(2)}) copy-start(bf16[4,4,128,128]{3,2,1,0:T(8,128)(2,1)S(1)} %collective-permute-done.23.refs_25_) | copy-start | bytes 1572868
  87.9 11.4 %collective-permute-start.19 = (bf16[4,4,128,128]{3,2,1,0:T(8,128)(2,1)S(1)}, bf16[4,4,128,128]{3,2,1,0:T(8,128)(2,1)S(1)}, u32[]{:S(2)}, u32[]{:S(2)}) collective-permute-start(bf16[4,4,128,128]{3,2,1,0:T(8,128)(2,1)S(1)} %collective-permute-done.17.refs_11_), channel_id=1, source_target_pairs={{0,8},{8,0},{16,24},{24,16},{1,9},{9,1},{17,25},{25,17},{2,10},{10... | collective-permute-start | bytes 1572872 | tf_op jit(solution)/shard_map/ppermute | solution.py:14
  89.4 10.4 %collective-permute-start.20 = (bf16[4,4,128,128]{3,2,1,0:T(8,128)(2,1)S(1)}, bf16[4,4,128,128]{3,2,1,0:T(8,128)(2,1)S(1)}, u32[]{:S(2)}, u32[]{:S(2)}) collective-permute-start(bf16[4,4,128,128]{3,2,1,0:T(8,128)(2,1)S(1)} %collective-permute-done.15.refs_24_), channel_id=1, source_target_pairs={{0,16},{16,0},{8,24},{24,8},{1,17},{17,1},{9,25},{25,9},{2,18},{18... | collective-permute-start | bytes 1572872 | tf_op jit(solution)/shard_map/ppermute | solution.py:14
  91.0 35.9 %copy-start.28 = (bf16[4,4,128,128]{3,2,1,0:T(8,128)(2,1)}, bf16[4,4,128,128]{3,2,1,0:T(8,128)(2,1)S(1)}, u32[]{:S(2)}) copy-start(bf16[4,4,128,128]{3,2,1,0:T(8,128)(2,1)S(1)} %collective-permute-done.22.refs_14_) | copy-start | bytes 1572868
  91.0 10.4 %collective-permute-start.28 = (bf16[4,4,128,128]{3,2,1,0:T(8,128)(2,1)S(1)}, bf16[4,4,128,128]{3,2,1,0:T(8,128)(2,1)S(1)}, u32[]{:S(2)}, u32[]{:S(2)}) collective-permute-start(bf16[4,4,128,128]{3,2,1,0:T(8,128)(2,1)S(1)} %broadcast_select_fusion.3), channel_id=1, source_target_pairs={{0,4},{4,0},{1,5},{5,1},{2,6},{6,2},{3,7},{7,3},{8,12},{12,8},{9,1... | collective-permute-start | bytes 1572872 | tf_op jit(solution)/shard_map/ppermute | solution.py:14
  91.1 35.8 %copy-start.29 = (bf16[4,4,128,128]{3,2,1,0:T(8,128)(2,1)}, bf16[4,4,128,128]{3,2,1,0:T(8,128)(2,1)S(1)}, u32[]{:S(2)}) copy-start(bf16[4,4,128,128]{3,2,1,0:T(8,128)(2,1)S(1)} %collective-permute-done.21.refs_38_) | copy-start | bytes 1572868
  91.2 10.8 %collective-permute-start.29 = (bf16[4,4,128,128]{3,2,1,0:T(8,128)(2,1)S(1)}, bf16[4,4,128,128]{3,2,1,0:T(8,128)(2,1)S(1)}, u32[]{:S(2)}, u32[]{:S(2)}) collective-permute-start(bf16[4,4,128,128]{3,2,1,0:T(8,128)(2,1)S(1)} %collective-permute-done.6.refs_8_), channel_id=1, source_target_pairs={{0,4},{4,0},{1,5},{5,1},{2,6},{6,2},{3,7},{7,3},{8,12},{12,8},{9,1... | collective-permute-start | bytes 1572872 | tf_op jit(solution)/shard_map/ppermute | solution.py:14
  99.2 25.6 %copy-start.13 = (bf16[4,4,128,128]{3,2,1,0:T(8,128)(2,1)}, bf16[4,4,128,128]{3,2,1,0:T(8,128)(2,1)S(1)}, u32[]{:S(2)}) copy-start(bf16[4,4,128,128]{3,2,1,0:T(8,128)(2,1)S(1)} %collective-permute-done.19.refs_26_) | copy-start | bytes 1572868
  99.3 2.8 %collective-permute-start.30 = (bf16[4,4,128,128]{3,2,1,0:T(8,128)(2,1)S(1)}, bf16[4,4,128,128]{3,2,1,0:T(8,128)(2,1)S(1)}, u32[]{:S(2)}, u32[]{:S(2)}) collective-permute-start(bf16[4,4,128,128]{3,2,1,0:T(8,128)(2,1)S(1)} %collective-permute-done.9.refs_10_), channel_id=1, source_target_pairs={{0,4},{4,0},{1,5},{5,1},{2,6},{6,2},{3,7},{7,3},{8,12},{12,8},{9,1... | collective-permute-start | bytes 1572872 | tf_op jit(solution)/shard_map/ppermute | solution.py:14
  99.9 14.9 %copy-start.14 = (bf16[4,4,128,128]{3,2,1,0:T(8,128)(2,1)}, bf16[4,4,128,128]{3,2,1,0:T(8,128)(2,1)S(1)}, u32[]{:S(2)}) copy-start(bf16[4,4,128,128]{3,2,1,0:T(8,128)(2,1)S(1)} %collective-permute-done.20.refs_32_) | copy-start | bytes 1572868
  99.9 14.8 %collective-permute-start.27 = (bf16[4,4,128,128]{3,2,1,0:T(8,128)(2,1)S(1)}, bf16[4,4,128,128]{3,2,1,0:T(8,128)(2,1)S(1)}, u32[]{:S(2)}, u32[]{:S(2)}) collective-permute-start(bf16[4,4,128,128]{3,2,1,0:T(8,128)(2,1)S(1)} %collective-permute-done.23.refs_25_), channel_id=1, source_target_pairs={{0,16},{16,0},{8,24},{24,8},{1,17},{17,1},{9,25},{25,9},{2,18},{18... | collective-permute-start | bytes 1572872 | tf_op jit(solution)/shard_map/ppermute | solution.py:14
  101.3 13.5 %copy-start.19 = (bf16[8,4,128,128]{3,2,1,0:T(8,128)(2,1)}, bf16[8,4,128,128]{3,2,1,0:T(8,128)(2,1)S(1)}, u32[]{:S(2)}) copy-start(bf16[8,4,128,128]{3,2,1,0:T(8,128)(2,1)S(1)} %collective-permute-done.11.refs_12_) | copy-start | bytes 3145732
  101.3 13.5 %collective-permute-start.32 = (bf16[4,4,128,128]{3,2,1,0:T(8,128)(2,1)S(1)}, bf16[4,4,128,128]{3,2,1,0:T(8,128)(2,1)S(1)}, u32[]{:S(2)}, u32[]{:S(2)}) collective-permute-start(bf16[4,4,128,128]{3,2,1,0:T(8,128)(2,1)S(1)} %broadcast_select_fusion.2), channel_id=1, source_target_pairs={{0,4},{4,0},{1,5},{5,1},{2,6},{6,2},{3,7},{7,3},{8,12},{12,8},{9,1... | collective-permute-start | bytes 1572872 | tf_op jit(solution)/shard_map/ppermute | solution.py:14
  101.4 23.5 %copy-start.30 = (bf16[4,4,128,128]{3,2,1,0:T(8,128)(2,1)}, bf16[4,4,128,128]{3,2,1,0:T(8,128)(2,1)S(1)}, u32[]{:S(2)}) copy-start(bf16[4,4,128,128]{3,2,1,0:T(8,128)(2,1)S(1)} %collective-permute-done.28.refs_39_) | copy-start | bytes 1572868
  101.4 13.4 %collective-permute-start.33 = (bf16[4,4,128,128]{3,2,1,0:T(8,128)(2,1)}, bf16[4,4,128,128]{3,2,1,0:T(8,128)(2,1)S(1)}, u32[]{:S(2)}, u32[]{:S(2)}) collective-permute-start(bf16[4,4,128,128]{3,2,1,0:T(8,128)(2,1)} %collective-permute-done.14.refs_9_), channel_id=1, source_target_pairs={{0,4},{4,0},{1,5},{5,1},{2,6},{6,2},{3,7},{7,3},{8,12},{12,8},{9,1... | collective-permute-start | bytes 1572872 | tf_op jit(solution)/shard_map/ppermute | solution.py:14
  101.9 23.1 %copy-start.31 = (bf16[4,4,128,128]{3,2,1,0:T(8,128)(2,1)}, bf16[4,4,128,128]{3,2,1,0:T(8,128)(2,1)S(1)}, u32[]{:S(2)}) copy-start(bf16[4,4,128,128]{3,2,1,0:T(8,128)(2,1)S(1)} %collective-permute-done.29.refs_15_) | copy-start | bytes 1572868
  101.9 13.0 %collective-permute-start.34 = (bf16[4,4,128,128]{3,2,1,0:T(8,128)(2,1)S(1)}, bf16[4,4,128,128]{3,2,1,0:T(8,128)(2,1)S(1)}, u32[]{:S(2)}, u32[]{:S(2)}) collective-permute-start(bf16[4,4,128,128]{3,2,1,0:T(8,128)(2,1)S(1)} %collective-permute-done.17.refs_11_), channel_id=1, source_target_pairs={{0,4},{4,0},{1,5},{5,1},{2,6},{6,2},{3,7},{7,3},{8,12},{12,8},{9,1... | collective-permute-start | bytes 1572872 | tf_op jit(solution)/shard_map/ppermute | solution.py:14
  102.1 22.9 %copy-start.32 = (bf16[4,4,128,128]{3,2,1,0:T(8,128)(2,1)}, bf16[4,4,128,128]{3,2,1,0:T(8,128)(2,1)S(1)}, u32[]{:S(2)}) copy-start(bf16[4,4,128,128]{3,2,1,0:T(8,128)(2,1)S(1)} %collective-permute-done.30.refs_17_) | copy-start | bytes 1572868
  102.1 22.7 %collective-permute-start.31 = (bf16[4,4,128,128]{3,2,1,0:T(8,128)(2,1)S(1)}, bf16[4,4,128,128]{3,2,1,0:T(8,128)(2,1)S(1)}, u32[]{:S(2)}, u32[]{:S(2)}) collective-permute-start(bf16[4,4,128,128]{3,2,1,0:T(8,128)(2,1)S(1)} %collective-permute-done.19.refs_26_), channel_id=1, source_target_pairs={{0,16},{16,0},{8,24},{24,8},{1,17},{17,1},{9,25},{25,9},{2,18},{18... | collective-permute-start | bytes 1572872 | tf_op jit(solution)/shard_map/ppermute | solution.py:14
  114.8 10.3 %collective-permute-start.35 = (bf16[4,4,128,128]{3,2,1,0:T(8,128)(2,1)S(1)}, bf16[4,4,128,128]{3,2,1,0:T(8,128)(2,1)S(1)}, u32[]{:S(2)}, u32[]{:S(2)}) collective-permute-start(bf16[4,4,128,128]{3,2,1,0:T(8,128)(2,1)S(1)} %broadcast_select_fusion.1), channel_id=1, source_target_pairs={{0,4},{4,0},{1,5},{5,1},{2,6},{6,2},{3,7},{7,3},{8,12},{12,8},{9,1... | collective-permute-start | bytes 1572872 | tf_op jit(solution)/shard_map/ppermute | solution.py:14
  124.9 2.0 %collective-permute-start.36 = (bf16[4,4,128,128]{3,2,1,0:T(8,128)(2,1)S(1)}, bf16[4,4,128,128]{3,2,1,0:T(8,128)(2,1)S(1)}, u32[]{:S(2)}, u32[]{:S(2)}) collective-permute-start(bf16[4,4,128,128]{3,2,1,0:T(8,128)(2,1)S(1)} %broadcast_select_fusion), channel_id=1, source_target_pairs={{0,4},{4,0},{1,5},{5,1},{2,6},{6,2},{3,7},{7,3},{8,12},{12,8},{9,1... | collective-permute-start | bytes 1572872 | tf_op jit(solution)/shard_map/ppermute | solution.py:14
  (12 other events, 92.8 us)

commit v6 on v5

--- a/solution.py
+++ b/solution.py
@@ -48,12 +48,6 @@
     def round_four(own, x0, p1, y0, x1, p2, x2, y1, p3, s0):
         sent = along_x(p3), along_y(x2), shared(x1, y1), over_core(p1)
         return own, x0, p1, y0, x1, y1, s0, *together((p2, p3, x2, *sent))
-
-    def round_five(own, x0, p1, y0, x1, y1, s0, p2, p3, x2, x3, y2, s1, c1):
-        sent = along_y(x3), shared(x2, y2), over_core(p2), over_core(p3)
-        x3, y3, s2, c2, c3 = together((x3, *sent))
-        x, y, s = (x0, x1, x2, x3), (y0, y1, y2, y3), (s0, s1, s2, shared(x3, y3))
-        return (own, p1, p2, p3), (c1, c2, c3), x, y, s
 
     half = own.shape[0] // 2
     streams = [round_one(own[:half]), round_one(own[half:])]
@@ -64,8 +58,29 @@
     c0 = over_core(own)
     streams = [round_four(*stream) for stream in streams]
     c0, streams[1] = together((c0, streams[1]))
-    groups = [list(zip(*parts)) for parts in zip(*[round_five(*one) for one in streams])]
-    groups[1].insert(0, (c0,))
+    p0, x0, p1, y0, x1, y1, s0, p2, p3, x2, x3, y2, s1, c1 = map(list, zip(*streams))
+
+    def to_other(h):
+        return shared(x2[h], y2[h]), over_core(p2[h]), over_core(p3[h])
+
+    first = along_y(x3[0])
+    x3[1], x2[0], y2[0], p2[0], p3[0] = together((x3[1], x2[0], y2[0], p2[0], p3[0]))
+    second = along_y(x3[1])
+    crossed = to_other(0)
+    first, crossed, x2[1], y2[1], p2[1], p3[1] = together(
+        (first, crossed, x2[1], y2[1], p2[1], p3[1])
+    )
+    s3 = shared(x3[0], first)
+    second, s3, after = together((second, s3, to_other(1)))
+    s3 = s3, shared(x3[1], second)
+    s2, c2, c3 = zip(crossed, after)
+    groups = [
+        [p0, p1, p2, p3],
+        [(c0,), c1, c2, c3],
+        [x0, x1, x2, x3],
+        [y0, y1, y2, (first, second)],
+        [s0, s1, s2, s3],
+    ]
     return groups, extra
 
 

time: 160 us -> 157 us (0.981)
  waiting for transfers between devices: 80.9 us -> 77.6 us
    ppermute x37, waiting for transfers between devices: 80.9 us -> 77.6 us  [permuted(): return lax.ppermute(value, axes, pairs)]
  transfers between devices with their start and end apart: 37 -> 37, of which waited for: 17 -> 15; matrix products, arithmetic and copies ran while one was open for 6% -> 6% of each run, Pallas kernels for 0% -> 0%
where the time goes in v6:
time: 157 us
  waiting for transfers between devices  77.6 us (49%)
  starting transfers between devices  34.8 us (22%)
  Pallas kernels  31.8 us (20%)
  local copies, waits for them, and re-layouts  10.2 us (6%)
  other arithmetic  2.15 us (1%)
    ppermute x37, waiting for transfers between devices, permuted(): return lax.ppermute(value, axes, pairs)  77.6 us
    ppermute x37, starting transfers between devices, permuted(): return lax.ppermute(value, axes, pairs)  34.8 us
    pallas_call x1, Pallas kernels, local(): pl.pallas_call(kernel_body, out_shape=jax.ShapeDtypeStruct((rows, out_slo...  31.8 us
    gather x1, local copies, waits for them, and re-layouts, local(): block_cols[row_ids[:, None, :, None] % order, slot_ids[None, :, None, :]]  4.57 us
  transfers between devices with their start and end apart: 37, of which 15 were waited for; matrix products, arithmetic and copies ran while one was open for 6% of the time, Pallas kernels for 0%

profile of v6, /device:TPU:0, one launch (start us, length us, event | category | flops | bytes accessed | tf_op | source)
XLA Modules:
  0.0 157.2 jit_solution(8203082547108802222)
XLA Ops:
  0.0 1.3 fusion.24
  1.4 3.1 %collective-permute-start.3 = (bf16[4,4,128,128]{3,2,1,0:T(8,128)(2,1)S(1)}, bf16[4,4,128,128]{3,2,1,0:T(8,128)(2,1)}, u32[]{:S(2)}, u32[]{:S(2)}) collective-permute-start(bf16[4,4,128,128]{3,2,1,0:T(8,128)(2,1)S(1)} %get-tuple-element.119.refs_4_), channel_id=1, source_target_pairs={{0,1},{1,2},{2,3},{3,0},{4,5},{5,6},{6,7},{7,4},{8,9},{9,10},{10,1... | collective-permute-start | bytes 1572872 | tf_op jit(solution)/shard_map/ppermute | solution.py:14
  4.4 1.5 collective-permute-start.2
  5.9 1.6 %collective-permute-start.1 = (bf16[4,4,128,128]{3,2,1,0:T(8,128)(2,1)S(1)}, bf16[4,4,128,128]{3,2,1,0:T(8,128)(2,1)}, u32[]{:S(2)}, u32[]{:S(2)}) collective-permute-start(bf16[4,4,128,128]{3,2,1,0:T(8,128)(2,1)S(1)} %get-tuple-element.142.refs_5_), channel_id=1, source_target_pairs={{0,1},{1,2},{2,3},{3,0},{4,5},{5,6},{6,7},{7,4},{8,9},{9,10},{10,1... | collective-permute-start | bytes 1572872 | tf_op jit(solution)/shard_map/ppermute | solution.py:14
  7.5 0.5 collective-permute-start
  8.1 0.1 fusion
  8.3 0.1 copy.6
  8.4 0.6 gather_fusion.1
  9.0 0.2 fusion.2
  9.2 0.1 broadcast_or_fusion
  9.3 0.6 compare_select_fusion.6.refs_1_
  9.9 9.4 %collective-permute-done.3.refs_6_ = bf16[4,4,128,128]{3,2,1,0:T(8,128)(2,1)} collective-permute-done((bf16[4,4,128,128]{3,2,1,0:T(8,128)(2,1)S(1)}, bf16[4,4,128,128]{3,2,1,0:T(8,128)(2,1)}, u32[]{:S(2)}, u32[]{:S(2)}) %collective-permute-start.3) | collective-permute-done | bytes 524320 | tf_op jit(solution)/shard_map/ppermute | solution.py:14
  19.3 1.5 collective-permute-start.6
  20.9 1.5 collective-permute-start.4
  22.4 1.5 collective-permute-start.5
  23.9 0.6 reshape.222.refs_3_
  24.6 0.6 reshape.223.refs_2_
  25.2 0.1 reshape.224
  25.3 4.6 %gather_fusion = s32[640]{0:T(1024)S(1)} fusion(s32[64,16]{0,1:T(8,128)S(1)} %copy-done, s32[640]{0:T(1024)S(1)} %reshape.224), kind=kCustom, calls=%fused_computation | custom fusion | bytes 10240 | tf_op jit(solution)/shard_map/gather | solution.py:243
  30.0 0.1 add.344
  30.1 0.6 fusion.11.refs_0_
  30.7 1.6 %collective-permute-start.13 = (bf16[4,4,128,128]{3,2,1,0:T(8,128)(2,1)S(1)}, bf16[4,4,128,128]{3,2,1,0:T(8,128)(2,1)S(1)}, u32[]{:S(2)}, u32[]{:S(2)}) collective-permute-start(bf16[4,4,128,128]{3,2,1,0:T(8,128)(2,1)S(1)} %collective-permute-done.refs_20_), channel_id=1, source_target_pairs={{0,16},{16,0},{8,24},{24,8},{1,17},{17,1},{9,25},{25,9},{2,18},{18... | collective-permute-start | bytes 1572872 | tf_op jit(solution)/shard_map/ppermute | solution.py:14
  32.3 1.3 collective-permute-start.14
  33.6 0.5 collective-permute-done.5.refs_27_
  34.1 1.0 collective-permute-start.12
  35.1 6.7 %collective-permute-done.6.refs_8_ = bf16[4,4,128,128]{3,2,1,0:T(8,128)(2,1)} collective-permute-done((bf16[4,4,128,128]{3,2,1,0:T(8,128)(2,1)}, bf16[4,4,128,128]{3,2,1,0:T(8,128)(2,1)}, u32[]{:S(2)}, u32[]{:S(2)}) %collective-permute-start.6) | collective-permute-done | bytes 524320 | tf_op jit(solution)/shard_map/ppermute | solution.py:14
  42.0 1.8 %collective-permute-start.8 = (bf16[4,4,128,128]{3,2,1,0:T(8,128)(2,1)S(1)}, bf16[4,4,128,128]{3,2,1,0:T(8,128)(2,1)S(1)}, u32[]{:S(2)}, u32[]{:S(2)}) collective-permute-start(bf16[4,4,128,128]{3,2,1,0:T(8,128)(2,1)S(1)} %collective-permute-done.4.refs_21_), channel_id=1, source_target_pairs={{0,16},{16,0},{8,24},{24,8},{1,17},{17,1},{9,25},{25,9},{2,18},{18... | collective-permute-start | bytes 1572872 | tf_op jit(solution)/shard_map/ppermute | solution.py:14
  43.8 0.4 collective-permute-done.13.refs_28_
  44.1 1.6 %collective-permute-start.9 = (bf16[4,4,128,128]{3,2,1,0:T(8,128)(2,1)}, bf16[4,4,128,128]{3,2,1,0:T(8,128)(2,1)S(1)}, u32[]{:S(2)}, u32[]{:S(2)}) collective-permute-start(bf16[4,4,128,128]{3,2,1,0:T(8,128)(2,1)} %collective-permute-done.6.refs_8_), channel_id=1, source_target_pairs={{0,1},{1,2},{2,3},{3,0},{4,5},{5,6},{6,7},{7,4},{8,9},{9,10},{10,1... | collective-permute-start | bytes 1572872 | tf_op jit(solution)/shard_map/ppermute | solution.py:14
  45.7 7.2 %collective-permute-done.14.refs_9_ = bf16[4,4,128,128]{3,2,1,0:T(8,128)(2,1)S(1)} collective-permute-done((bf16[4,4,128,128]{3,2,1,0:T(8,128)(2,1)}, bf16[4,4,128,128]{3,2,1,0:T(8,128)(2,1)S(1)}, u32[]{:S(2)}, u32[]{:S(2)}) %collective-permute-start.14) | collective-permute-done | bytes 524320 | tf_op jit(solution)/shard_map/ppermute | solution.py:14
  52.9 1.7 %collective-permute-start.7 = (bf16[4,4,128,128]{3,2,1,0:T(8,128)(2,1)}, bf16[4,4,128,128]{3,2,1,0:T(8,128)(2,1)S(1)}, u32[]{:S(2)}, u32[]{:S(2)}) collective-permute-start(bf16[4,4,128,128]{3,2,1,0:T(8,128)(2,1)} %collective-permute-done.6.refs_8_), channel_id=1, source_target_pairs={{0,8},{8,0},{16,24},{24,16},{1,9},{9,1},{17,25},{25,17},{2,10},{10... | collective-permute-start | bytes 1572872 | tf_op jit(solution)/shard_map/ppermute | solution.py:14
  54.8 1.6 %collective-permute-start.16 = (bf16[4,4,128,128]{3,2,1,0:T(8,128)(2,1)S(1)}, bf16[4,4,128,128]{3,2,1,0:T(8,128)(2,1)S(1)}, u32[]{:S(2)}, u32[]{:S(2)}) collective-permute-start(bf16[4,4,128,128]{3,2,1,0:T(8,128)(2,1)S(1)} %collective-permute-done.12.refs_22_), channel_id=1, source_target_pairs={{0,16},{16,0},{8,24},{24,8},{1,17},{17,1},{9,25},{25,9},{2,18},{18... | collective-permute-start | bytes 1572872 | tf_op jit(solution)/shard_map/ppermute | solution.py:14
  56.4 1.4 collective-permute-start.17
  57.9 6.3 %collective-permute-done.9.refs_10_ = bf16[4,4,128,128]{3,2,1,0:T(8,128)(2,1)S(1)} collective-permute-done((bf16[4,4,128,128]{3,2,1,0:T(8,128)(2,1)}, bf16[4,4,128,128]{3,2,1,0:T(8,128)(2,1)S(1)}, u32[]{:S(2)}, u32[]{:S(2)}) %collective-permute-start.9) | collective-permute-done | bytes 524320 | tf_op jit(solution)/shard_map/ppermute | solution.py:14
  64.2 1.7 %collective-permute-start.15 = (bf16[4,4,128,128]{3,2,1,0:T(8,128)(2,1)S(1)}, bf16[4,4,128,128]{3,2,1,0:T(8,128)(2,1)S(1)}, u32[]{:S(2)}, u32[]{:S(2)}) collective-permute-start(bf16[4,4,128,128]{3,2,1,0:T(8,128)(2,1)S(1)} %collective-permute-done.14.refs_9_), channel_id=1, source_target_pairs={{0,8},{8,0},{16,24},{24,16},{1,9},{9,1},{17,25},{25,17},{2,10},{10... | collective-permute-start | bytes 1572872 | tf_op jit(solution)/shard_map/ppermute | solution.py:14
  65.9 0.1 broadcast_select_fusion.4
  66.1 0.5 collective-permute-start.26
  66.6 0.3 copy-done.24
  66.9 2.3 %collective-permute-done.16.refs_30_ = bf16[4,4,128,128]{3,2,1,0:T(8,128)(2,1)S(1)} collective-permute-done((bf16[4,4,128,128]{3,2,1,0:T(8,128)(2,1)S(1)}, bf16[4,4,128,128]{3,2,1,0:T(8,128)(2,1)S(1)}, u32[]{:S(2)}, u32[]{:S(2)}) %collective-permute-start.16) | collective-permute-done | bytes 524320 | tf_op jit(solution)/shard_map/ppermute | solution.py:14
  69.2 0.3 collective-permute-start.23
  69.5 5.1 %collective-permute-done.17.refs_11_ = bf16[4,4,128,128]{3,2,1,0:T(8,128)(2,1)S(1)} collective-permute-done((bf16[4,4,128,128]{3,2,1,0:T(8,128)(2,1)S(1)}, bf16[4,4,128,128]{3,2,1,0:T(8,128)(2,1)S(1)}, u32[]{:S(2)}, u32[]{:S(2)}) %collective-permute-start.17) | collective-permute-done | bytes 524320 | tf_op jit(solution)/shard_map/ppermute | solution.py:14
  74.6 1.5 collective-permute-start.24
  76.1 2.9 %collective-permute-done.15.refs_24_ = bf16[4,4,128,128]{3,2,1,0:T(8,128)(2,1)S(1)} collective-permute-done((bf16[4,4,128,128]{3,2,1,0:T(8,128)(2,1)S(1)}, bf16[4,4,128,128]{3,2,1,0:T(8,128)(2,1)S(1)}, u32[]{:S(2)}, u32[]{:S(2)}) %collective-permute-start.15) | collective-permute-done | bytes 524320 | tf_op jit(solution)/shard_map/ppermute | solution.py:14
  79.1 0.6 collective-permute-start.22
  79.7 0.1 collective-permute-start.21
  79.8 8.1 %collective-permute-done.23.refs_25_ = bf16[4,4,128,128]{3,2,1,0:T(8,128)(2,1)S(1)} collective-permute-done((bf16[4,4,128,128]{3,2,1,0:T(8,128)(2,1)S(1)}, bf16[4,4,128,128]{3,2,1,0:T(8,128)(2,1)S(1)}, u32[]{:S(2)}, u32[]{:S(2)}) %collective-permute-start.23) | collective-permute-done | bytes 524320 | tf_op jit(solution)/shard_map/ppermute | solution.py:14
  87.9 1.3 collective-permute-start.19
  89.2 1.5 collective-permute-start.20
  90.7 0.5 collective-permute-start.27
  91.3 8.2 %collective-permute-done.19.refs_26_ = bf16[4,4,128,128]{3,2,1,0:T(8,128)(2,1)S(1)} collective-permute-done((bf16[4,4,128,128]{3,2,1,0:T(8,128)(2,1)S(1)}, bf16[4,4,128,128]{3,2,1,0:T(8,128)(2,1)S(1)}, u32[]{:S(2)}, u32[]{:S(2)}) %collective-permute-start.19) | collective-permute-done | bytes 524320 | tf_op jit(solution)/shard_map/ppermute | solution.py:14
  99.5 4.6 %collective-permute-done.20.refs_32_ = bf16[4,4,128,128]{3,2,1,0:T(8,128)(2,1)S(1)} collective-permute-done((bf16[4,4,128,128]{3,2,1,0:T(8,128)(2,1)S(1)}, bf16[4,4,128,128]{3,2,1,0:T(8,128)(2,1)S(1)}, u32[]{:S(2)}, u32[]{:S(2)}) %collective-permute-start.20) | collective-permute-done | bytes 524320 | tf_op jit(solution)/shard_map/ppermute | solution.py:14
  104.2 0.1 collective-permute-start.28
  104.3 0.5 collective-permute-start.29
  104.8 0.1 collective-permute-start.30
  104.8 1.5 collective-permute-start.31
  106.4 8.0 %collective-permute-done.27.refs_33_ = bf16[4,4,128,128]{3,2,1,0:T(8,128)(2,1)S(1)} collective-permute-done((bf16[4,4,128,128]{3,2,1,0:T(8,128)(2,1)S(1)}, bf16[4,4,128,128]{3,2,1,0:T(8,128)(2,1)S(1)}, u32[]{:S(2)}, u32[]{:S(2)}) %collective-permute-start.27) | collective-permute-done | bytes 524320 | tf_op jit(solution)/shard_map/ppermute | solution.py:14
  114.6 0.6 copy-done.15
  115.2 0.2 copy-done.30
  115.4 0.5 collective-permute-start.32
  115.9 0.5 collective-permute-start.35
  116.4 6.0 %collective-permute-done.31.refs_34_ = bf16[4,4,128,128]{3,2,1,0:T(8,128)(2,1)S(1)} collective-permute-done((bf16[4,4,128,128]{3,2,1,0:T(8,128)(2,1)S(1)}, bf16[4,4,128,128]{3,2,1,0:T(8,128)(2,1)S(1)}, u32[]{:S(2)}, u32[]{:S(2)}) %collective-permute-start.31) | collective-permute-done | bytes 524320 | tf_op jit(solution)/shard_map/ppermute | solution.py:14
  122.6 1.9 %collective-permute-done.36.refs_42_ = bf16[4,4,128,128]{3,2,1,0:T(8,128)(2,1)S(1)} collective-permute-done((bf16[4,4,128,128]{3,2,1,0:T(8,128)(2,1)S(1)}, bf16[4,4,128,128]{3,2,1,0:T(8,128)(2,1)S(1)}, u32[]{:S(2)}, u32[]{:S(2)}) %collective-permute-start.36) | collective-permute-done | bytes 524320 | tf_op jit(solution)/shard_map/ppermute | solution.py:14
  124.6 0.8 copy-done.35
  125.4 31.8 %purify.1 = bf16[8,6,128,128]{3,2,1,0:T(8,128)(2,1)} custom-call(s32[640]{0:T(1024)} %fusion.11.refs_0_, s32[40]{0:T(128)} %compare_select_fusion.6.refs_1_, s32[320]{0:T(512)} %reshape.223.refs_2_, s32[48]{0:T(128)} %reshape.222.refs_3_, bf16[4,4,128,128]{3,2,1,0:T(8,128)(2,1)} %copy-done.17, bf16[4,4,128,128]{3,2,1,0:T(8,128)(2,1)} %copy-done.18, ...), custom_call_target="tpu_custom_call" | custom-call | tf_op jit(solution)/shard_map/purify/pallas_call | solution.py:267
  (121 shorter events, 1.1 us)
Async XLA Ops:
  0.0 8.3 %copy-start = (s32[64,16]{0,1:T(8,128)S(1)}, s32[64,16]{0,1:T(8,128)}, u32[]{:S(2)}) copy-start(s32[64,16]{0,1:T(8,128)} %param.4) | copy-start | bytes 12292
  1.3 28.6 %copy-start.17 = (bf16[4,4,128,128]{3,2,1,0:T(8,128)(2,1)}, bf16[4,4,128,128]{3,2,1,0:T(8,128)(2,1)S(1)}, u32[]{:S(2)}) copy-start(bf16[4,4,128,128]{3,2,1,0:T(8,128)(2,1)S(1)} %get-tuple-element.119.refs_4_) | copy-start | bytes 1572868
  1.3 28.6 %copy-start.18 = (bf16[4,4,128,128]{3,2,1,0:T(8,128)(2,1)}, bf16[4,4,128,128]{3,2,1,0:T(8,128)(2,1)S(1)}, u32[]{:S(2)}) copy-start(bf16[4,4,128,128]{3,2,1,0:T(8,128)(2,1)S(1)} %get-tuple-element.142.refs_5_) | copy-start | bytes 1572868
  1.4 18.0 %collective-permute-start.3 = (bf16[4,4,128,128]{3,2,1,0:T(8,128)(2,1)S(1)}, bf16[4,4,128,128]{3,2,1,0:T(8,128)(2,1)}, u32[]{:S(2)}, u32[]{:S(2)}) collective-permute-start(bf16[4,4,128,128]{3,2,1,0:T(8,128)(2,1)S(1)} %get-tuple-element.119.refs_4_), channel_id=1, source_target_pairs={{0,1},{1,2},{2,3},{3,0},{4,5},{5,6},{6,7},{7,4},{8,9},{9,10},{10,1... | collective-permute-start | bytes 1572872 | tf_op jit(solution)/shard_map/ppermute | solution.py:14
  4.4 14.9 %collective-permute-start.2 = (bf16[4,4,128,128]{3,2,1,0:T(8,128)(2,1)S(1)}, bf16[4,4,128,128]{3,2,1,0:T(8,128)(2,1)S(1)}, u32[]{:S(2)}, u32[]{:S(2)}) collective-permute-start(bf16[4,4,128,128]{3,2,1,0:T(8,128)(2,1)S(1)} %get-tuple-element.119.refs_4_), channel_id=1, source_target_pairs={{0,8},{8,0},{16,24},{24,16},{1,9},{9,1},{17,25},{25,17},{2,10},{10... | collective-permute-start | bytes 1572872 | tf_op jit(solution)/shard_map/ppermute | solution.py:14
  5.9 24.8 %collective-permute-start.1 = (bf16[4,4,128,128]{3,2,1,0:T(8,128)(2,1)S(1)}, bf16[4,4,128,128]{3,2,1,0:T(8,128)(2,1)}, u32[]{:S(2)}, u32[]{:S(2)}) collective-permute-start(bf16[4,4,128,128]{3,2,1,0:T(8,128)(2,1)S(1)} %get-tuple-element.142.refs_5_), channel_id=1, source_target_pairs={{0,1},{1,2},{2,3},{3,0},{4,5},{5,6},{6,7},{7,4},{8,9},{9,10},{10,1... | collective-permute-start | bytes 1572872 | tf_op jit(solution)/shard_map/ppermute | solution.py:14
  7.5 23.2 %collective-permute-start = (bf16[4,4,128,128]{3,2,1,0:T(8,128)(2,1)S(1)}, bf16[4,4,128,128]{3,2,1,0:T(8,128)(2,1)S(1)}, u32[]{:S(2)}, u32[]{:S(2)}) collective-permute-start(bf16[4,4,128,128]{3,2,1,0:T(8,128)(2,1)S(1)} %get-tuple-element.142.refs_5_), channel_id=1, source_target_pairs={{0,8},{8,0},{16,24},{24,16},{1,9},{9,1},{17,25},{25,17},{2,10},{10... | collective-permute-start | bytes 1572872 | tf_op jit(solution)/shard_map/ppermute | solution.py:14
  19.3 22.5 %copy-start.1 = (bf16[4,4,128,128]{3,2,1,0:T(8,128)(2,1)}, bf16[4,4,128,128]{3,2,1,0:T(8,128)(2,1)S(1)}, u32[]{:S(2)}) copy-start(bf16[4,4,128,128]{3,2,1,0:T(8,128)(2,1)S(1)} %collective-permute-done.2.refs_19_) | copy-start | bytes 1572868
  19.3 22.5 %collective-permute-start.6 = (bf16[4,4,128,128]{3,2,1,0:T(8,128)(2,1)}, bf16[4,4,128,128]{3,2,1,0:T(8,128)(2,1)}, u32[]{:S(2)}, u32[]{:S(2)}) collective-permute-start(bf16[4,4,128,128]{3,2,1,0:T(8,128)(2,1)} %collective-permute-done.3.refs_6_), channel_id=1, source_target_pairs={{0,1},{1,2},{2,3},{3,0},{4,5},{5,6},{6,7},{7,4},{8,9},{9,10},{10,1... | collective-permute-start | bytes 1572872 | tf_op jit(solution)/shard_map/ppermute | solution.py:14
  20.9 20.9 %collective-permute-start.4 = (bf16[4,4,128,128]{3,2,1,0:T(8,128)(2,1)}, bf16[4,4,128,128]{3,2,1,0:T(8,128)(2,1)S(1)}, u32[]{:S(2)}, u32[]{:S(2)}) collective-permute-start(bf16[4,4,128,128]{3,2,1,0:T(8,128)(2,1)} %collective-permute-done.3.refs_6_), channel_id=1, source_target_pairs={{0,8},{8,0},{16,24},{24,16},{1,9},{9,1},{17,25},{25,17},{2,10},{10... | collective-permute-start | bytes 1572872 | tf_op jit(solution)/shard_map/ppermute | solution.py:14
  22.4 11.8 %collective-permute-start.5 = (bf16[4,4,128,128]{3,2,1,0:T(8,128)(2,1)S(1)}, bf16[4,4,128,128]{3,2,1,0:T(8,128)(2,1)S(1)}, u32[]{:S(2)}, u32[]{:S(2)}) collective-permute-start(bf16[4,4,128,128]{3,2,1,0:T(8,128)(2,1)S(1)} %collective-permute-done.2.refs_19_), channel_id=1, source_target_pairs={{0,16},{16,0},{8,24},{24,8},{1,17},{17,1},{9,25},{25,9},{2,18},{18... | collective-permute-start | bytes 1572872 | tf_op jit(solution)/shard_map/ppermute | solution.py:14
  30.7 24.0 %copy-start.2 = (bf16[4,4,128,128]{3,2,1,0:T(8,128)(2,1)}, bf16[4,4,128,128]{3,2,1,0:T(8,128)(2,1)S(1)}, u32[]{:S(2)}) copy-start(bf16[4,4,128,128]{3,2,1,0:T(8,128)(2,1)S(1)} %collective-permute-done.refs_20_) | copy-start | bytes 1572868
  30.7 13.4 %collective-permute-start.13 = (bf16[4,4,128,128]{3,2,1,0:T(8,128)(2,1)S(1)}, bf16[4,4,128,128]{3,2,1,0:T(8,128)(2,1)S(1)}, u32[]{:S(2)}, u32[]{:S(2)}) collective-permute-start(bf16[4,4,128,128]{3,2,1,0:T(8,128)(2,1)S(1)} %collective-permute-done.refs_20_), channel_id=1, source_target_pairs={{0,16},{16,0},{8,24},{24,8},{1,17},{17,1},{9,25},{25,9},{2,18},{18... | collective-permute-start | bytes 1572872 | tf_op jit(solution)/shard_map/ppermute | solution.py:14
  32.3 20.6 %collective-permute-start.14 = (bf16[4,4,128,128]{3,2,1,0:T(8,128)(2,1)}, bf16[4,4,128,128]{3,2,1,0:T(8,128)(2,1)S(1)}, u32[]{:S(2)}, u32[]{:S(2)}) collective-permute-start(bf16[4,4,128,128]{3,2,1,0:T(8,128)(2,1)} %collective-permute-done.1.refs_7_), channel_id=1, source_target_pairs={{0,1},{1,2},{2,3},{3,0},{4,5},{5,6},{6,7},{7,4},{8,9},{9,10},{10,1... | collective-permute-start | bytes 1572872 | tf_op jit(solution)/shard_map/ppermute | solution.py:14
  34.1 20.6 %copy-start.4 = (bf16[4,4,128,128]{3,2,1,0:T(8,128)(2,1)}, bf16[4,4,128,128]{3,2,1,0:T(8,128)(2,1)S(1)}, u32[]{:S(2)}) copy-start(bf16[4,4,128,128]{3,2,1,0:T(8,128)(2,1)S(1)} %collective-permute-done.5.refs_27_) | copy-start | bytes 1572868
  34.1 20.5 %collective-permute-start.12 = (bf16[4,4,128,128]{3,2,1,0:T(8,128)(2,1)}, bf16[4,4,128,128]{3,2,1,0:T(8,128)(2,1)S(1)}, u32[]{:S(2)}, u32[]{:S(2)}) collective-permute-start(bf16[4,4,128,128]{3,2,1,0:T(8,128)(2,1)} %collective-permute-done.1.refs_7_), channel_id=1, source_target_pairs={{0,8},{8,0},{16,24},{24,16},{1,9},{9,1},{17,25},{25,17},{2,10},{10... | collective-permute-start | bytes 1572872 | tf_op jit(solution)/shard_map/ppermute | solution.py:14
  41.8 24.1 %copy-start.3 = (bf16[4,4,128,128]{3,2,1,0:T(8,128)(2,1)}, bf16[4,4,128,128]{3,2,1,0:T(8,128)(2,1)S(1)}, u32[]{:S(2)}) copy-start(bf16[4,4,128,128]{3,2,1,0:T(8,128)(2,1)S(1)} %collective-permute-done.4.refs_21_) | copy-start | bytes 1572868
  41.9 37.2 %copy-start.20 = (bf16[8,4,128,128]{3,2,1,0:T(8,128)(2,1)S(1)}, bf16[8,4,128,128]{3,2,1,0:T(8,128)(2,1)}, u32[]{:S(2)}) copy-start(bf16[8,4,128,128]{3,2,1,0:T(8,128)(2,1)} %param.3) | copy-start | bytes 3145732
  41.9 12.9 %collective-permute-start.10 = (bf16[4,4,128,128]{3,2,1,0:T(8,128)(2,1)S(1)}, bf16[4,4,128,128]{3,2,1,0:T(8,128)(2,1)S(1)}, u32[]{:S(2)}, u32[]{:S(2)}) collective-permute-start(bf16[4,4,128,128]{3,2,1,0:T(8,128)(2,1)S(1)} %broadcast_select_fusion.7), channel_id=1, source_target_pairs={{0,4},{4,0},{1,5},{5,1},{2,6},{6,2},{3,7},{7,3},{8,12},{12,8},{9,1... | collective-permute-start | bytes 1572872 | tf_op jit(solution)/shard_map/ppermute | solution.py:14
  42.0 14.5 %collective-permute-start.8 = (bf16[4,4,128,128]{3,2,1,0:T(8,128)(2,1)S(1)}, bf16[4,4,128,128]{3,2,1,0:T(8,128)(2,1)S(1)}, u32[]{:S(2)}, u32[]{:S(2)}) collective-permute-start(bf16[4,4,128,128]{3,2,1,0:T(8,128)(2,1)S(1)} %collective-permute-done.4.refs_21_), channel_id=1, source_target_pairs={{0,16},{16,0},{8,24},{24,8},{1,17},{17,1},{9,25},{25,9},{2,18},{18... | collective-permute-start | bytes 1572872 | tf_op jit(solution)/shard_map/ppermute | solution.py:14
  44.1 21.8 %copy-start.5 = (bf16[4,4,128,128]{3,2,1,0:T(8,128)(2,1)}, bf16[4,4,128,128]{3,2,1,0:T(8,128)(2,1)S(1)}, u32[]{:S(2)}) copy-start(bf16[4,4,128,128]{3,2,1,0:T(8,128)(2,1)S(1)} %collective-permute-done.13.refs_28_) | copy-start | bytes 1572868
  44.1 20.0 %collective-permute-start.9 = (bf16[4,4,128,128]{3,2,1,0:T(8,128)(2,1)}, bf16[4,4,128,128]{3,2,1,0:T(8,128)(2,1)S(1)}, u32[]{:S(2)}, u32[]{:S(2)}) collective-permute-start(bf16[4,4,128,128]{3,2,1,0:T(8,128)(2,1)} %collective-permute-done.6.refs_8_), channel_id=1, source_target_pairs={{0,1},{1,2},{2,3},{3,0},{4,5},{5,6},{6,7},{7,4},{8,9},{9,10},{10,1... | collective-permute-start | bytes 1572872 | tf_op jit(solution)/shard_map/ppermute | solution.py:14
  52.9 62.9 %copy-start.21 = (bf16[4,4,128,128]{3,2,1,0:T(8,128)(2,1)}, bf16[4,4,128,128]{3,2,1,0:T(8,128)(2,1)S(1)}, u32[]{:S(2)}) copy-start(bf16[4,4,128,128]{3,2,1,0:T(8,128)(2,1)S(1)} %collective-permute-done.14.refs_9_) | copy-start | bytes 1572868
  52.9 13.0 %collective-permute-start.7 = (bf16[4,4,128,128]{3,2,1,0:T(8,128)(2,1)}, bf16[4,4,128,128]{3,2,1,0:T(8,128)(2,1)S(1)}, u32[]{:S(2)}, u32[]{:S(2)}) collective-permute-start(bf16[4,4,128,128]{3,2,1,0:T(8,128)(2,1)} %collective-permute-done.6.refs_8_), channel_id=1, source_target_pairs={{0,8},{8,0},{16,24},{24,16},{1,9},{9,1},{17,25},{25,17},{2,10},{10... | collective-permute-start | bytes 1572872 | tf_op jit(solution)/shard_map/ppermute | solution.py:14
  54.7 24.4 %copy-start.6 = (bf16[4,4,128,128]{3,2,1,0:T(8,128)(2,1)}, bf16[4,4,128,128]{3,2,1,0:T(8,128)(2,1)S(1)}, u32[]{:S(2)}) copy-start(bf16[4,4,128,128]{3,2,1,0:T(8,128)(2,1)S(1)} %collective-permute-done.12.refs_22_) | copy-start | bytes 1572868
  54.7 11.3 %collective-permute-start.18 = (bf16[4,4,128,128]{3,2,1,0:T(8,128)(2,1)S(1)}, bf16[4,4,128,128]{3,2,1,0:T(8,128)(2,1)S(1)}, u32[]{:S(2)}, u32[]{:S(2)}) collective-permute-start(bf16[4,4,128,128]{3,2,1,0:T(8,128)(2,1)S(1)} %broadcast_select_fusion.6), channel_id=1, source_target_pairs={{0,4},{4,0},{1,5},{5,1},{2,6},{6,2},{3,7},{7,3},{8,12},{12,8},{9,1... | collective-permute-start | bytes 1572872 | tf_op jit(solution)/shard_map/ppermute | solution.py:14
  54.8 24.3 %copy-start.22 = (bf16[4,4,128,128]{3,2,1,0:T(8,128)(2,1)}, bf16[4,4,128,128]{3,2,1,0:T(8,128)(2,1)S(1)}, u32[]{:S(2)}) copy-start(bf16[4,4,128,128]{3,2,1,0:T(8,128)(2,1)S(1)} %collective-permute-done.10.refs_35_) | copy-start | bytes 1572868
  54.8 14.3 %collective-permute-start.16 = (bf16[4,4,128,128]{3,2,1,0:T(8,128)(2,1)S(1)}, bf16[4,4,128,128]{3,2,1,0:T(8,128)(2,1)S(1)}, u32[]{:S(2)}, u32[]{:S(2)}) collective-permute-start(bf16[4,4,128,128]{3,2,1,0:T(8,128)(2,1)S(1)} %collective-permute-done.12.refs_22_), channel_id=1, source_target_pairs={{0,16},{16,0},{8,24},{24,8},{1,17},{17,1},{9,25},{25,9},{2,18},{18... | collective-permute-start | bytes 1572872 | tf_op jit(solution)/shard_map/ppermute | solution.py:14
  56.4 22.7 %copy-start.7 = (bf16[4,4,128,128]{3,2,1,0:T(8,128)(2,1)}, bf16[4,4,128,128]{3,2,1,0:T(8,128)(2,1)S(1)}, u32[]{:S(2)}) copy-start(bf16[4,4,128,128]{3,2,1,0:T(8,128)(2,1)S(1)} %collective-permute-done.8.refs_29_) | copy-start | bytes 1572868
  56.4 18.1 %collective-permute-start.17 = (bf16[4,4,128,128]{3,2,1,0:T(8,128)(2,1)S(1)}, bf16[4,4,128,128]{3,2,1,0:T(8,128)(2,1)S(1)}, u32[]{:S(2)}, u32[]{:S(2)}) collective-permute-start(bf16[4,4,128,128]{3,2,1,0:T(8,128)(2,1)S(1)} %collective-permute-done.14.refs_9_), channel_id=1, source_target_pairs={{0,1},{1,2},{2,3},{3,0},{4,5},{5,6},{6,7},{7,4},{8,9},{9,10},{10,1... | collective-permute-start | bytes 1572872 | tf_op jit(solution)/shard_map/ppermute | solution.py:14
  64.2 40.6 %copy-start.23 = (bf16[4,4,128,128]{3,2,1,0:T(8,128)(2,1)}, bf16[4,4,128,128]{3,2,1,0:T(8,128)(2,1)S(1)}, u32[]{:S(2)}) copy-start(bf16[4,4,128,128]{3,2,1,0:T(8,128)(2,1)S(1)} %collective-permute-done.9.refs_10_) | copy-start | bytes 1572868
  64.2 14.9 %collective-permute-start.15 = (bf16[4,4,128,128]{3,2,1,0:T(8,128)(2,1)S(1)}, bf16[4,4,128,128]{3,2,1,0:T(8,128)(2,1)S(1)}, u32[]{:S(2)}, u32[]{:S(2)}) collective-permute-start(bf16[4,4,128,128]{3,2,1,0:T(8,128)(2,1)S(1)} %collective-permute-done.14.refs_9_), channel_id=1, source_target_pairs={{0,8},{8,0},{16,24},{24,16},{1,9},{9,1},{17,25},{25,17},{2,10},{10... | collective-permute-start | bytes 1572872 | tf_op jit(solution)/shard_map/ppermute | solution.py:14
  65.9 38.2 %copy-start.8 = (bf16[4,4,128,128]{3,2,1,0:T(8,128)(2,1)}, bf16[4,4,128,128]{3,2,1,0:T(8,128)(2,1)S(1)}, u32[]{:S(2)}) copy-start(bf16[4,4,128,128]{3,2,1,0:T(8,128)(2,1)S(1)} %collective-permute-done.7.refs_23_) | copy-start | bytes 1572868
  66.0 13.1 %collective-permute-start.25 = (bf16[4,4,128,128]{3,2,1,0:T(8,128)(2,1)S(1)}, bf16[4,4,128,128]{3,2,1,0:T(8,128)(2,1)S(1)}, u32[]{:S(2)}, u32[]{:S(2)}) collective-permute-start(bf16[4,4,128,128]{3,2,1,0:T(8,128)(2,1)S(1)} %broadcast_select_fusion.4), channel_id=1, source_target_pairs={{0,4},{4,0},{1,5},{5,1},{2,6},{6,2},{3,7},{7,3},{8,12},{12,8},{9,1... | collective-permute-start | bytes 1572872 | tf_op jit(solution)/shard_map/ppermute | solution.py:14
  66.1 13.6 %collective-permute-start.26 = (bf16[4,4,128,128]{3,2,1,0:T(8,128)(2,1)}, bf16[4,4,128,128]{3,2,1,0:T(8,128)(2,1)S(1)}, u32[]{:S(2)}, u32[]{:S(2)}) collective-permute-start(bf16[4,4,128,128]{3,2,1,0:T(8,128)(2,1)} %collective-permute-done.3.refs_6_), channel_id=1, source_target_pairs={{0,4},{4,0},{1,5},{5,1},{2,6},{6,2},{3,7},{7,3},{8,12},{12,8},{9,1... | collective-permute-start | bytes 1572872 | tf_op jit(solution)/shard_map/ppermute | solution.py:14
  69.2 35.0 %copy-start.9 = (bf16[4,4,128,128]{3,2,1,0:T(8,128)(2,1)}, bf16[4,4,128,128]{3,2,1,0:T(8,128)(2,1)S(1)}, u32[]{:S(2)}) copy-start(bf16[4,4,128,128]{3,2,1,0:T(8,128)(2,1)S(1)} %collective-permute-done.16.refs_30_) | copy-start | bytes 1572868
  69.2 18.7 %collective-permute-start.23 = (bf16[4,4,128,128]{3,2,1,0:T(8,128)(2,1)S(1)}, bf16[4,4,128,128]{3,2,1,0:T(8,128)(2,1)S(1)}, u32[]{:S(2)}, u32[]{:S(2)}) collective-permute-start(bf16[4,4,128,128]{3,2,1,0:T(8,128)(2,1)S(1)} %collective-permute-done.9.refs_10_), channel_id=1, source_target_pairs={{0,8},{8,0},{16,24},{24,16},{1,9},{9,1},{17,25},{25,17},{2,10},{10... | collective-permute-start | bytes 1572872 | tf_op jit(solution)/shard_map/ppermute | solution.py:14
  74.6 50.0 %copy-start.25 = (bf16[4,4,128,128]{3,2,1,0:T(8,128)(2,1)}, bf16[4,4,128,128]{3,2,1,0:T(8,128)(2,1)S(1)}, u32[]{:S(2)}) copy-start(bf16[4,4,128,128]{3,2,1,0:T(8,128)(2,1)S(1)} %collective-permute-done.17.refs_11_) | copy-start | bytes 1572868
  74.6 14.7 %collective-permute-start.24 = (bf16[4,4,128,128]{3,2,1,0:T(8,128)(2,1)S(1)}, bf16[4,4,128,128]{3,2,1,0:T(8,128)(2,1)S(1)}, u32[]{:S(2)}, u32[]{:S(2)}) collective-permute-start(bf16[4,4,128,128]{3,2,1,0:T(8,128)(2,1)S(1)} %collective-permute-done.7.refs_23_), channel_id=1, source_target_pairs={{0,16},{16,0},{8,24},{24,8},{1,17},{17,1},{9,25},{25,9},{2,18},{18... | collective-permute-start | bytes 1572872 | tf_op jit(solution)/shard_map/ppermute | solution.py:14
  79.0 35.5 %copy-start.10 = (bf16[4,4,128,128]{3,2,1,0:T(8,128)(2,1)}, bf16[4,4,128,128]{3,2,1,0:T(8,128)(2,1)S(1)}, u32[]{:S(2)}) copy-start(bf16[4,4,128,128]{3,2,1,0:T(8,128)(2,1)S(1)} %collective-permute-done.15.refs_24_) | copy-start | bytes 1572868
  79.0 25.1 %collective-permute-start.11 = (bf16[8,4,128,128]{3,2,1,0:T(8,128)(2,1)S(1)}, bf16[8,4,128,128]{3,2,1,0:T(8,128)(2,1)S(1)}, u32[]{:S(2)}, u32[]{:S(2)}) collective-permute-start(bf16[8,4,128,128]{3,2,1,0:T(8,128)(2,1)S(1)} %copy-done.20), channel_id=1, source_target_pairs={{0,4},{4,0},{1,5},{5,1},{2,6},{6,2},{3,7},{7,3},{8,12},{12,8},{9,1... | collective-permute-start | bytes 3145736 | tf_op jit(solution)/shard_map/ppermute | solution.py:14
  79.1 45.4 %copy-start.26 = (bf16[4,4,128,128]{3,2,1,0:T(8,128)(2,1)}, bf16[4,4,128,128]{3,2,1,0:T(8,128)(2,1)S(1)}, u32[]{:S(2)}) copy-start(bf16[4,4,128,128]{3,2,1,0:T(8,128)(2,1)S(1)} %collective-permute-done.25.refs_37_) | copy-start | bytes 1572868
  79.1 11.6 %collective-permute-start.22 = (bf16[4,4,128,128]{3,2,1,0:T(8,128)(2,1)}, bf16[4,4,128,128]{3,2,1,0:T(8,128)(2,1)S(1)}, u32[]{:S(2)}, u32[]{:S(2)}) collective-permute-start(bf16[4,4,128,128]{3,2,1,0:T(8,128)(2,1)} %collective-permute-done.1.refs_7_), channel_id=1, source_target_pairs={{0,4},{4,0},{1,5},{5,1},{2,6},{6,2},{3,7},{7,3},{8,12},{12,8},{9,1... | collective-permute-start | bytes 1572872 | tf_op jit(solution)/shard_map/ppermute | solution.py:14
  79.7 44.8 %copy-start.27 = (bf16[4,4,128,128]{3,2,1,0:T(8,128)(2,1)}, bf16[4,4,128,128]{3,2,1,0:T(8,128)(2,1)S(1)}, u32[]{:S(2)}) copy-start(bf16[4,4,128,128]{3,2,1,0:T(8,128)(2,1)S(1)} %collective-permute-done.26.refs_13_) | copy-start | bytes 1572868
  79.7 11.6 %collective-permute-start.21 = (bf16[4,4,128,128]{3,2,1,0:T(8,128)(2,1)S(1)}, bf16[4,4,128,128]{3,2,1,0:T(8,128)(2,1)S(1)}, u32[]{:S(2)}, u32[]{:S(2)}) collective-permute-start(bf16[4,4,128,128]{3,2,1,0:T(8,128)(2,1)S(1)} %broadcast_select_fusion.5), channel_id=1, source_target_pairs={{0,4},{4,0},{1,5},{5,1},{2,6},{6,2},{3,7},{7,3},{8,12},{12,8},{9,1... | collective-permute-start | bytes 1572872 | tf_op jit(solution)/shard_map/ppermute | solution.py:14
  87.9 26.6 %copy-start.11 = (bf16[4,4,128,128]{3,2,1,0:T(8,128)(2,1)}, bf16[4,4,128,128]{3,2,1,0:T(8,128)(2,1)S(1)}, u32[]{:S(2)}) copy-start(bf16[4,4,128,128]{3,2,1,0:T(8,128)(2,1)S(1)} %collective-permute-done.23.refs_25_) | copy-start | bytes 1572868
  87.9 11.6 %collective-permute-start.19 = (bf16[4,4,128,128]{3,2,1,0:T(8,128)(2,1)S(1)}, bf16[4,4,128,128]{3,2,1,0:T(8,128)(2,1)S(1)}, u32[]{:S(2)}, u32[]{:S(2)}) collective-permute-start(bf16[4,4,128,128]{3,2,1,0:T(8,128)(2,1)S(1)} %collective-permute-done.17.refs_11_), channel_id=1, source_target_pairs={{0,8},{8,0},{16,24},{24,16},{1,9},{9,1},{17,25},{25,17},{2,10},{10... | collective-permute-start | bytes 1572872 | tf_op jit(solution)/shard_map/ppermute | solution.py:14
  89.2 25.3 %copy-start.12 = (bf16[4,4,128,128]{3,2,1,0:T(8,128)(2,1)}, bf16[4,4,128,128]{3,2,1,0:T(8,128)(2,1)S(1)}, u32[]{:S(2)}) copy-start(bf16[4,4,128,128]{3,2,1,0:T(8,128)(2,1)S(1)} %collective-permute-done.24.refs_31_) | copy-start | bytes 1572868
  89.2 14.9 %collective-permute-start.20 = (bf16[4,4,128,128]{3,2,1,0:T(8,128)(2,1)S(1)}, bf16[4,4,128,128]{3,2,1,0:T(8,128)(2,1)S(1)}, u32[]{:S(2)}, u32[]{:S(2)}) collective-permute-start(bf16[4,4,128,128]{3,2,1,0:T(8,128)(2,1)S(1)} %collective-permute-done.15.refs_24_), channel_id=1, source_target_pairs={{0,16},{16,0},{8,24},{24,8},{1,17},{17,1},{9,25},{25,9},{2,18},{18... | collective-permute-start | bytes 1572872 | tf_op jit(solution)/shard_map/ppermute | solution.py:14
  90.7 33.8 %copy-start.28 = (bf16[4,4,128,128]{3,2,1,0:T(8,128)(2,1)}, bf16[4,4,128,128]{3,2,1,0:T(8,128)(2,1)S(1)}, u32[]{:S(2)}) copy-start(bf16[4,4,128,128]{3,2,1,0:T(8,128)(2,1)S(1)} %collective-permute-done.22.refs_14_) | copy-start | bytes 1572868
  90.7 23.6 %collective-permute-start.27 = (bf16[4,4,128,128]{3,2,1,0:T(8,128)(2,1)S(1)}, bf16[4,4,128,128]{3,2,1,0:T(8,128)(2,1)S(1)}, u32[]{:S(2)}, u32[]{:S(2)}) collective-permute-start(bf16[4,4,128,128]{3,2,1,0:T(8,128)(2,1)S(1)} %collective-permute-done.23.refs_25_), channel_id=1, source_target_pairs={{0,16},{16,0},{8,24},{24,8},{1,17},{17,1},{9,25},{25,9},{2,18},{18... | collective-permute-start | bytes 1572872 | tf_op jit(solution)/shard_map/ppermute | solution.py:14
  91.3 12.8 %copy-start.29 = (bf16[4,4,128,128]{3,2,1,0:T(8,128)(2,1)}, bf16[4,4,128,128]{3,2,1,0:T(8,128)(2,1)S(1)}, u32[]{:S(2)}) copy-start(bf16[4,4,128,128]{3,2,1,0:T(8,128)(2,1)S(1)} %collective-permute-done.21.refs_38_) | copy-start | bytes 1572868
  99.5 23.0 %copy-start.13 = (bf16[4,4,128,128]{3,2,1,0:T(8,128)(2,1)}, bf16[4,4,128,128]{3,2,1,0:T(8,128)(2,1)S(1)}, u32[]{:S(2)}) copy-start(bf16[4,4,128,128]{3,2,1,0:T(8,128)(2,1)S(1)} %collective-permute-done.19.refs_26_) | copy-start | bytes 1572868
  104.1 10.4 %copy-start.14 = (bf16[4,4,128,128]{3,2,1,0:T(8,128)(2,1)}, bf16[4,4,128,128]{3,2,1,0:T(8,128)(2,1)S(1)}, u32[]{:S(2)}) copy-start(bf16[4,4,128,128]{3,2,1,0:T(8,128)(2,1)S(1)} %collective-permute-done.20.refs_32_) | copy-start | bytes 1572868
  104.1 10.4 %copy-start.19 = (bf16[8,4,128,128]{3,2,1,0:T(8,128)(2,1)}, bf16[8,4,128,128]{3,2,1,0:T(8,128)(2,1)S(1)}, u32[]{:S(2)}) copy-start(bf16[8,4,128,128]{3,2,1,0:T(8,128)(2,1)S(1)} %collective-permute-done.11.refs_12_) | copy-start | bytes 3145732
  104.2 10.2 %collective-permute-start.28 = (bf16[4,4,128,128]{3,2,1,0:T(8,128)(2,1)S(1)}, bf16[4,4,128,128]{3,2,1,0:T(8,128)(2,1)}, u32[]{:S(2)}, u32[]{:S(2)}) collective-permute-start(bf16[4,4,128,128]{3,2,1,0:T(8,128)(2,1)S(1)} %broadcast_select_fusion.3), channel_id=1, source_target_pairs={{0,4},{4,0},{1,5},{5,1},{2,6},{6,2},{3,7},{7,3},{8,12},{12,8},{9,1... | collective-permute-start | bytes 1572872 | tf_op jit(solution)/shard_map/ppermute | solution.py:14
  104.3 10.1 %collective-permute-start.29 = (bf16[4,4,128,128]{3,2,1,0:T(8,128)(2,1)}, bf16[4,4,128,128]{3,2,1,0:T(8,128)(2,1)S(1)}, u32[]{:S(2)}, u32[]{:S(2)}) collective-permute-start(bf16[4,4,128,128]{3,2,1,0:T(8,128)(2,1)} %collective-permute-done.6.refs_8_), channel_id=1, source_target_pairs={{0,4},{4,0},{1,5},{5,1},{2,6},{6,2},{3,7},{7,3},{8,12},{12,8},{9,1... | collective-permute-start | bytes 1572872 | tf_op jit(solution)/shard_map/ppermute | solution.py:14
  104.8 9.6 %collective-permute-start.30 = (bf16[4,4,128,128]{3,2,1,0:T(8,128)(2,1)S(1)}, bf16[4,4,128,128]{3,2,1,0:T(8,128)(2,1)}, u32[]{:S(2)}, u32[]{:S(2)}) collective-permute-start(bf16[4,4,128,128]{3,2,1,0:T(8,128)(2,1)S(1)} %collective-permute-done.9.refs_10_), channel_id=1, source_target_pairs={{0,4},{4,0},{1,5},{5,1},{2,6},{6,2},{3,7},{7,3},{8,12},{12,8},{9,1... | collective-permute-start | bytes 1572872 | tf_op jit(solution)/shard_map/ppermute | solution.py:14
  104.8 17.6 %collective-permute-start.31 = (bf16[4,4,128,128]{3,2,1,0:T(8,128)(2,1)S(1)}, bf16[4,4,128,128]{3,2,1,0:T(8,128)(2,1)S(1)}, u32[]{:S(2)}, u32[]{:S(2)}) collective-permute-start(bf16[4,4,128,128]{3,2,1,0:T(8,128)(2,1)S(1)} %collective-permute-done.19.refs_26_), channel_id=1, source_target_pairs={{0,16},{16,0},{8,24},{24,8},{1,17},{17,1},{9,25},{25,9},{2,18},{18... | collective-permute-start | bytes 1572872 | tf_op jit(solution)/shard_map/ppermute | solution.py:14
  115.4 7.1 %collective-permute-start.33 = (bf16[4,4,128,128]{3,2,1,0:T(8,128)(2,1)S(1)}, bf16[4,4,128,128]{3,2,1,0:T(8,128)(2,1)S(1)}, u32[]{:S(2)}, u32[]{:S(2)}) collective-permute-start(bf16[4,4,128,128]{3,2,1,0:T(8,128)(2,1)S(1)} %broadcast_select_fusion.1), channel_id=1, source_target_pairs={{0,4},{4,0},{1,5},{5,1},{2,6},{6,2},{3,7},{7,3},{8,12},{12,8},{9,1... | collective-permute-start | bytes 1572872 | tf_op jit(solution)/shard_map/ppermute | solution.py:14
  115.4 7.1 %collective-permute-start.32 = (bf16[4,4,128,128]{3,2,1,0:T(8,128)(2,1)S(1)}, bf16[4,4,128,128]{3,2,1,0:T(8,128)(2,1)S(1)}, u32[]{:S(2)}, u32[]{:S(2)}) collective-permute-start(bf16[4,4,128,128]{3,2,1,0:T(8,128)(2,1)S(1)} %broadcast_select_fusion.2), channel_id=1, source_target_pairs={{0,4},{4,0},{1,5},{5,1},{2,6},{6,2},{3,7},{7,3},{8,12},{12,8},{9,1... | collective-permute-start | bytes 1572872 | tf_op jit(solution)/shard_map/ppermute | solution.py:14
  115.9 6.6 %collective-permute-start.34 = (bf16[4,4,128,128]{3,2,1,0:T(8,128)(2,1)S(1)}, bf16[4,4,128,128]{3,2,1,0:T(8,128)(2,1)S(1)}, u32[]{:S(2)}, u32[]{:S(2)}) collective-permute-start(bf16[4,4,128,128]{3,2,1,0:T(8,128)(2,1)S(1)} %collective-permute-done.14.refs_9_), channel_id=1, source_target_pairs={{0,4},{4,0},{1,5},{5,1},{2,6},{6,2},{3,7},{7,3},{8,12},{12,8},{9,1... | collective-permute-start | bytes 1572872 | tf_op jit(solution)/shard_map/ppermute | solution.py:14
  115.9 6.6 %collective-permute-start.35 = (bf16[4,4,128,128]{3,2,1,0:T(8,128)(2,1)S(1)}, bf16[4,4,128,128]{3,2,1,0:T(8,128)(2,1)S(1)}, u32[]{:S(2)}, u32[]{:S(2)}) collective-permute-start(bf16[4,4,128,128]{3,2,1,0:T(8,128)(2,1)S(1)} %collective-permute-done.17.refs_11_), channel_id=1, source_target_pairs={{0,4},{4,0},{1,5},{5,1},{2,6},{6,2},{3,7},{7,3},{8,12},{12,8},{9,1... | collective-permute-start | bytes 1572872 | tf_op jit(solution)/shard_map/ppermute | solution.py:14
  122.5 2.0 %collective-permute-start.36 = (bf16[4,4,128,128]{3,2,1,0:T(8,128)(2,1)S(1)}, bf16[4,4,128,128]{3,2,1,0:T(8,128)(2,1)S(1)}, u32[]{:S(2)}, u32[]{:S(2)}) collective-permute-start(bf16[4,4,128,128]{3,2,1,0:T(8,128)(2,1)S(1)} %broadcast_select_fusion), channel_id=1, source_target_pairs={{0,4},{4,0},{1,5},{5,1},{2,6},{6,2},{3,7},{7,3},{8,12},{12,8},{9,1... | collective-permute-start | bytes 1572872 | tf_op jit(solution)/shard_map/ppermute | solution.py:14
  (10 other events, 22.2 us)
